TPU v7x, 256 devices: a whole 4x4x8 slice. The times are simulated.
256 devices in a mesh: patch: 64 (over x, z_lo, y, core), tp: 4 (over z_hi).
Axes of the slice: x: 4, y: 4, z: 8 (z_hi: 4, z_lo: 2; z = z_hi * 2 + z_lo), core: 2. Of those that a mesh axis runs over, the one named last changes fastest.
Arguments:
- activations: bfloat16 [2, 4096, 4096], P(None, 'patch', 'tp'), may hold values from -3000 to 3000
- mod_shift: bfloat16 [2, 4096], P(None, 'tp'), may hold values from -3 to 3
- mod_scale: bfloat16 [2, 4096], P(None, 'tp'), may hold values from -3 to 3
- w_query: bfloat16 [4096, 2048], P(None, 'tp'), may hold values from -0.09375 to 0.09375
- w_key: bfloat16 [4096, 2048], P(None, 'tp'), may hold values from -0.09375 to 0.09375
- w_value: bfloat16 [4096, 2048], P(None, 'tp'), may hold values from -0.09375 to 0.09375
- query_gain: float32 [128], replicated, may hold values from 1 to 2.5
- key_gain: float32 [128], replicated, may hold values from 1 to 2.5
- stale_keys: bfloat16 [2, 4096, 2048], P(None, 'patch', 'tp'), may hold values from -200 to 200
- stale_values: bfloat16 [2, 4096, 2048], P(None, 'patch', 'tp'), may hold values from -6 to 6
Outputs:
- attended: bfloat16 [2, 4096, 2048], P(None, 'patch', 'tp')
- fresh_keys: bfloat16 [2, 4096, 2048], P(None, 'patch', 'tp')
- fresh_values: bfloat16 [2, 4096, 2048], P(None, 'patch', 'tp')
All inputs are finite; a program needn't handle non-finite values.
Results may differ from a plain program's by a relative error of at most 0.022.
Values may be sent and summed in bfloat16 or wider, within the bound.
No kernel may reach another device: no remote copies, remote signals or barrier semaphores. Data moves between devices by JAX's collectives and lax.ppermute only.
A program may use at most 128 MiB of HBM per device.

v0:
```python
import math

import jax
import jax.numpy as jnp
from jax import lax
from jax.sharding import PartitionSpec as P


def head_norm(projected, gain_vector):
    shaped = projected.reshape(projected.shape[:-1] + (-1, gain_vector.shape[0]))
    scaled = (
        shaped * lax.rsqrt(jnp.mean(shaped * shaped, axis=-1, keepdims=True) + 1e-06) * gain_vector
    )
    return scaled.reshape(projected.shape).astype(jnp.bfloat16)


def make_fold(query_block, tok_rows, own_index, score_scale):
    heads_here = query_block.shape[2]
    head_dim = query_block.shape[3]

    def fold_rows(running, pieces, offset):
        run_max, run_total, run_numer = running
        piece_keys, piece_values = pieces
        count = piece_keys.shape[0]
        piece_rows = piece_keys.shape[1]
        split_keys = piece_keys.reshape(count, piece_rows, heads_here, head_dim)
        split_values = piece_values.reshape(count, piece_rows, heads_here, head_dim)
        scores = (
            jnp.einsum(
                "bqhd,bkhd->bqhk", query_block, split_keys, preferred_element_type=jnp.float32
            )
            * score_scale
        )
        columns = jnp.arange(piece_rows, dtype=jnp.int32)
        is_own = columns // tok_rows == own_index
        scores = jnp.where(is_own[None, None, None, :], -1e30, scores)
        new_max = jnp.maximum(run_max, jnp.max(scores, axis=-1))
        factor = jnp.exp(run_max - new_max)
        weights = jnp.exp(scores - new_max[..., None])
        new_total = run_total * factor + jnp.sum(weights, axis=-1)
        new_numer = run_numer * factor[..., None] + jnp.einsum(
            "bqhk,bkhd->bqhd",
            weights.astype(jnp.bfloat16),
            split_values,
            preferred_element_type=jnp.float32,
        )
        return (new_max, new_total, new_numer)

    return fold_rows


def on_device(
    activations,
    mod_shift,
    mod_scale,
    w_query,
    w_key,
    w_value,
    query_gain,
    key_gain,
    stale_keys,
    stale_values,
):
    images, tok_rows, _ = activations.shape
    head_dim = query_gain.shape[0]
    features = w_query.shape[1]
    heads_here = features // head_dim
    score_scale = 1.0 / math.sqrt(head_dim)
    values = activations.astype(jnp.float32)
    width = values.shape[2] * lax.axis_size("tp")
    row_sums = jnp.sum(values, axis=-1)
    row_squares = jnp.sum(values * values, axis=-1)
    row_sums, row_squares = lax.psum((row_sums, row_squares), "tp")
    row_mean = (row_sums / width)[..., None]
    row_var = (row_squares / width)[..., None] - row_mean * row_mean
    normed = (values - row_mean) * lax.rsqrt(row_var + 1e-06)
    shifted = (
        normed * (1.0 + mod_scale.astype(jnp.float32)[:, None, :])
        + mod_shift.astype(jnp.float32)[:, None, :]
    )
    modulated = lax.all_gather(shifted.astype(jnp.bfloat16), "tp", axis=2, tiled=True)
    flat_rows = modulated.reshape(images * tok_rows, -1)
    queries = head_norm(jnp.dot(flat_rows, w_query, preferred_element_type=jnp.float32), query_gain)
    queries = queries.reshape(images, tok_rows, heads_here, head_dim)
    fresh_keys = head_norm(jnp.dot(flat_rows, w_key, preferred_element_type=jnp.float32), key_gain)
    fresh_keys = fresh_keys.reshape(images, tok_rows, features)
    fresh_values = jnp.dot(flat_rows, w_value, preferred_element_type=jnp.float32).astype(
        jnp.bfloat16
    )
    fresh_values = fresh_values.reshape(images, tok_rows, features)
    own_keys = fresh_keys.reshape(images, tok_rows, heads_here, head_dim)
    own_values = fresh_values.reshape(images, tok_rows, heads_here, head_dim)
    near_scores = (
        jnp.einsum("bqhd,bkhd->bqhk", queries, own_keys, preferred_element_type=jnp.float32)
        * score_scale
    )
    near_max = jnp.max(near_scores, axis=-1)
    near_exp = jnp.exp(near_scores - near_max[..., None])
    near_total = jnp.sum(near_exp, axis=-1)
    near_numer = jnp.einsum(
        "bqhk,bkhd->bqhd",
        near_exp.astype(jnp.bfloat16),
        own_values,
        preferred_element_type=jnp.float32,
    )
    own_index = lax.axis_index("patch")
    fold_rows = make_fold(queries, tok_rows, own_index, score_scale)
    top_max, weight_total, numerator = fold_rows(
        (near_max, near_total, near_numer),
        (
            lax.all_gather(stale_keys, "patch", axis=1, tiled=True),
            lax.all_gather(stale_values, "patch", axis=1, tiled=True),
        ),
        jnp.int32(0),
    )
    ratio = numerator / weight_total[..., None]
    attended = ratio.reshape(images, tok_rows, features).astype(jnp.bfloat16)
    return (attended, fresh_keys, fresh_values)


def solution(mesh):
    in_specs = (
        P(None, "patch", "tp"),
        P(None, "tp"),
        P(None, "tp"),
        P(None, "tp"),
        P(None, "tp"),
        P(None, "tp"),
        P(),
        P(),
        P(None, "patch", "tp"),
        P(None, "patch", "tp"),
    )
    out_specs = (P(None, "patch", "tp"), P(None, "patch", "tp"), P(None, "patch", "tp"))
    return jax.shard_map(
        on_device, mesh=mesh, in_specs=in_specs, out_specs=out_specs, check_vma=False
    )
```

profile of v0, /device:TPU:1, one launch (start us, length us, event | category | flops | bytes accessed | tf_op | source)
XLA Modules:
  0.0 327.5 jit_solution(2122418577723598183)
XLA Ops:
  7.2 0.0 all-gather.4.cloned.1.call-start
  7.2 0.7 convert_element_type.47
  7.9 0.7 convert_add_fusion
  8.6 1.1 convert_reduce_fusion
  9.7 13.7 %all-reduce = (f32[2,64]{1,0:T(2,128)S(1)}, f32[2,64]{1,0:T(2,128)S(1)}) all-reduce(f32[2,64]{1,0:T(2,128)S(1)} %get-tuple-element.4, f32[2,64]{1,0:T(2,128)S(1)} %get-tuple-element.3), channel_id=1, replica_groups=mesh['patch'=64,'tp'=4] {'tp'}, use_global_device_ids=true, to_apply=%region_3.0 | all-reduce | flops 256 | bytes 2048 | tf_op jit(solution)/shard_map/psum | solution.py:73
  23.4 1.9 fusion.21
  25.4 0.0 all-gather.4.cloned.1.call-update
  25.4 0.0 all-gather.6.cloned.1.call-start
  25.4 1.7 copy.39
  27.1 0.0 all-gather.6.cloned.1.call-update
  27.1 0.0 all-gather.8.cloned.1.call-start
  27.2 1.7 copy.43
  28.9 0.0 all-gather.8.cloned.1.call-update
  28.9 6.4 %copy.52 = bf16[512,4096]{1,0:T(8,128)(2,1)} copy(bf16[512,4096]{0,1:T(8,128)(2,1)} %bitcast.66) | data formatting | bytes 8388608 | tf_op jit(solution)/shard_map/dot_general | solution.py:83
  35.3 0.0 copy-start.3
  35.3 6.4 %copy.51 = bf16[512,4096]{1,0:T(8,128)(2,1)} copy(bf16[512,4096]{0,1:T(8,128)(2,1)} %bitcast.67) | data formatting | bytes 8388608 | tf_op jit(solution)/shard_map/dot_general | solution.py:85
  41.7 19.2 %all-gather.4.cloned.1.call-done = bf16[2,64,4096]{2,1,0:T(8,128)(2,1)} async-done(((bf16[2,64,1024]{2,1,0:T(8,128)(2,1)}), bf16[2,64,4096]{2,1,0:T(8,128)(2,1)}) %all-gather.4.cloned.1.call-update) | async-done | bytes 1048592 | tf_op jit(solution)/shard_map/all_gather | solution.py:81
  60.9 0.0 copy-start.1
  60.9 0.0 copy-start.4
  60.9 3.3 %convolution_convert_fusion = bf16[128,512]{1,0:T(8,128)(2,1)S(1)} fusion(bf16[128,4096]{1,0:T(8,128)(2,1)} %bitcast.62, bf16[4096,512]{1,0:T(8,128)(2,1)} %param.15), kind=kOutput, calls=%fused_computation.19 | convolution fusion | flops 536936448 | bytes 5373952 | tf_op jit(solution)/shard_map/dot_general | solution.py:87
  64.3 0.0 copy-start.2
  64.3 4.2 %multiply_reduce_fusion.1 = (f32[128,4]{0,1:T(4,128)S(1)}, f32[128,4,128]{2,0,1:T(8,128)S(1)}) fusion(bf16[128,4096,1]{1,0,2:T(8,128)(2,1)} %bitcast.63, bf16[4,128,4096]{2,1,0:T(8,128)(2,1)} %bitcast.61), kind=kOutput, calls=%fused_computation.33 | convolution fusion | flops 537001472 | bytes 5507072 | tf_op jit(solution)/shard_map/dot_general | solution.py:85
  68.5 0.0 copy-done.3
  68.5 0.1 multiply_convert_fusion.1
  68.6 0.1 copy.47
  68.7 0.7 convert_element_type.58
  69.5 0.0 copy-done.1
  69.5 3.8 %multiply_reduce_fusion = (f32[128,4]{0,1:T(4,128)S(1)}, f32[128,4,128]{2,0,1:T(8,128)S(1)}) fusion(bf16[128,4096,1]{1,0,2:T(8,128)(2,1)S(1)} %bitcast.64, bf16[4,128,4096]{2,1,0:T(8,128)(2,1)} %bitcast.60), kind=kOutput, calls=%fused_computation.31 | convolution fusion | flops 537001472 | bytes 5507072 | tf_op jit(solution)/shard_map/dot_general | solution.py:83
  73.3 0.0 copy-done.4
  73.3 0.1 multiply_convert_fusion
  73.5 0.2 fusion.38
  73.7 0.1 fusion.23
  73.7 100.7 %all-gather.6.cloned.1.call-done = bf16[2,4096,512]{2,0,1:T(2,128)(2,1)} async-done(((bf16[2,64,512]{2,0,1:T(2,128)(2,1)}), bf16[2,4096,512]{2,0,1:T(2,128)(2,1)}) %all-gather.6.cloned.1.call-update) | async-done | bytes 8388624 | tf_op jit(solution)/shard_map/all_gather | solution.py:111
  174.5 21.4 %copy.40 = bf16[2,4096,512]{1,2,0:T(8,128)(2,1)} copy(bf16[2,4096,512]{2,0,1:T(2,128)(2,1)} %all-gather.6.cloned.1.call-done) | data formatting | bytes 16777216 | tf_op jit(solution)/shard_map/all_gather | solution.py:111
  195.8 0.0 copy-done.2
  195.8 6.0 %bitcast_reduce_fusion = (f32[2,64,4]{1,2,0:T(4,128)S(1)}, f32[2,4,64,4096]{3,2,1,0:T(8,128)S(1)}) fusion(pred[4096]{0:T(1024)(128)(4,1)S(1)} %fusion.32, bf16[2,4096,4,128]{1,3,2,0:T(8,128)(2,1)} %bitcast.59, bf16[2,64,4,128]{3,1,0,2:T(8,128)(2,1)S(1)} %bitcast.69), kind=kOutput, calls=%fused_computation.1 | convolution fusion | flops 543161856 | bytes 16914432 | tf_op jit(solution)/shard_map/bqhd,bkhd->bqhk/dot_general | solution.py:29
  201.8 0.0 copy-start
  201.9 3.2 copy-done
  205.1 2.0 fusion.1
  207.1 82.9 %all-gather.8.cloned.1.call-done = bf16[2,4096,512]{2,0,1:T(2,128)(2,1)} async-done(((bf16[2,64,512]{2,0,1:T(2,128)(2,1)}), bf16[2,4096,512]{2,0,1:T(2,128)(2,1)}) %all-gather.8.cloned.1.call-update) | async-done | bytes 8388624 | tf_op jit(solution)/shard_map/all_gather | solution.py:112
  290.0 21.1 %copy.44 = bf16[2,4096,512]{1,2,0:T(8,128)(2,1)} copy(bf16[2,4096,512]{2,0,1:T(2,128)(2,1)} %all-gather.8.cloned.1.call-done) | data formatting | bytes 16777216 | tf_op jit(solution)/shard_map/all_gather | solution.py:112
  311.1 8.9 %fusion.13 = f32[2,64,4,128]{3,1,2,0:T(8,128)S(1)} fusion(bf16[2,4096,4,128]{1,3,2,0:T(8,128)(2,1)} %bitcast.65, f32[2,4,64,4096]{3,2,1,0:T(8,128)} %copy-done, f32[2,64,4]{1,2,0:T(4,128)S(1)} %max.13, pred[4096]{0:T(1024)(128)(4,1)S(1)} %fusion.32), kind=kOutput, calls=%fused_computation.17 | convolution fusion | flops 545259520 | bytes 17045504 | tf_op jit(solution)/shard_map/bqhk,bkhd->bqhd/dot_general | solution.py:41
  320.0 0.3 fusion.17
  320.3 0.7 copy.69
  (7 shorter events, 0.1 us)
Async XLA Ops:
  7.2 53.8 %all-gather.4.cloned.1.call-start = ((), (), s32[]{:S(2)}) async-start(), calls=%async_computation | async-start | bytes 1310720 | tf_op jit(solution)/shard_map/all_gather | solution.py:81
  25.4 149.1 %all-gather.6.cloned.1.call-start = ((), (), s32[]{:S(2)}) async-start(), calls=%async_computation.1 | async-start | bytes 8519680 | tf_op jit(solution)/shard_map/all_gather | solution.py:111
  27.1 262.8 %all-gather.8.cloned.1.call-start = ((), (), s32[]{:S(2)}) async-start(), calls=%async_computation.2 | async-start | bytes 8519680 | tf_op jit(solution)/shard_map/all_gather | solution.py:112
  35.3 33.2 %copy-start.3 = (f32[128]{0:T(128)S(1)}, f32[128]{0:T(128)}, u32[]{:S(2)}) copy-start(f32[128]{0:T(128)} %param.17) | copy-start | bytes 1540
  60.9 8.5 %copy-start.1 = (bf16[2,64,4096]{2,1,0:T(8,128)(2,1)S(1)}, bf16[2,64,4096]{2,1,0:T(8,128)(2,1)}, u32[]{:S(2)}) copy-start(bf16[2,64,4096]{2,1,0:T(8,128)(2,1)} %all-gather.4.cloned.1.call-done) | copy-start | bytes 3145732
  60.9 12.4 %copy-start.4 = (f32[128]{0:T(128)S(1)}, f32[128]{0:T(128)}, u32[]{:S(2)}) copy-start(f32[128]{0:T(128)} %param.16) | copy-start | bytes 1540
  64.3 131.6 %copy-start.2 = (bf16[128,512]{1,0:T(8,128)(2,1)}, bf16[128,512]{1,0:T(8,128)(2,1)S(1)}, u32[]{:S(2)}) copy-start(bf16[128,512]{1,0:T(8,128)(2,1)S(1)} %convolution_convert_fusion) | copy-start | bytes 393220
  201.8 3.2 copy-start
Sparse Core Ops, SparseCore 0:
  25.5 35.3 all-gather.3
  62.8 111.6 all-gather.5
  176.9 113.0 all-gather.7
where the time goes:
time: 329 us; the launch traced here: 327 us
  waiting for transfers between devices  203 us (62%)
  local copies, waits for them, and re-layouts  63.5 us (19%)
  matrix products  26.7 us (8%)
  between operations  13.9 us (4%)
  blocking collectives  13.7 us (4%)
  other arithmetic  6.77 us (2%)
    all_gather x1, waiting for transfers between devices, on_device(): lax.all_gather(stale_keys, 'patch', axis=1, tiled=True)  101 us
    all_gather x1, waiting for transfers between devices, on_device(): lax.all_gather(stale_values, 'patch', axis=1, tiled=True)  82.9 us
    all_gather x1, local copies, waits for them, and re-layouts, on_device(): lax.all_gather(stale_keys, 'patch', axis=1, tiled=True)  21.4 us
    all_gather x1, local copies, waits for them, and re-layouts, on_device(): lax.all_gather(stale_values, 'patch', axis=1, tiled=True)  21.1 us
    all_gather x1, waiting for transfers between devices, on_device(): lax.all_gather(shifted.astype(jnp.bfloat16), 'tp', axis=2, tiled=True)  19.2 us
    psum x1, blocking collectives, on_device(): row_sums, row_squares = lax.psum((row_sums, row_squares), 'tp')  13.7 us
    dot_general x1, matrix products, fold_rows(): jnp.einsum('bqhk,bkhd->bqhd', weights.astype(jnp.bfloat16), split_values,...  8.88 us
    unnamed x12, local copies, waits for them, and re-layouts  6.6 us
  transfers between devices with their start and end apart: 3, of which 3 were waited for; matrix products, arithmetic and copies ran while one was open for 18% of the time, Pallas kernels for 0%

commit v1 on v0

v1 whole, which is shorter than its diff:
```python
import math

import jax
import jax.numpy as jnp
from jax import lax
from jax.experimental import pallas as pl
from jax.experimental.pallas import tpu as pltpu
from jax.sharding import Mesh, PartitionSpec as P

HEAD = 128
TOK = 64
IMG = 2
WIDTH = 4096
PART = 1024
COLS = 512
ROWS = IMG * TOK
SCORE = math.log2(math.e) / math.sqrt(HEAD)
F32 = jnp.float32
BF16 = jnp.bfloat16
GROUP = ("zl", "core")


def params(limit):
    return pltpu.CompilerParams(vmem_limit_bytes=limit * 1024 * 1024)


def vmem(count):
    return [pl.BlockSpec(memory_space=pltpu.VMEM)] * count


def smem():
    return pl.BlockSpec(memory_space=pltpu.SMEM)


def dot_t(a, b):
    return lax.dot_general(a, b, (((1,), (1,)), ((), ())), preferred_element_type=F32)


def head_slice(me, d):
    return pl.ds(pl.multiple_of((me ^ d) * HEAD, HEAD), HEAD)


def pack_kernel(me_ref, keys, values, *outs):
    me = me_ref[0]
    for d in range(4):
        cut = head_slice(me, d)
        for i in range(IMG):
            outs[d][i, 0] = keys[i, :, cut]
            outs[d][i, 1] = values[i, :, cut]


def pack(me, keys, values):
    return pl.pallas_call(
        pack_kernel,
        out_shape=[jax.ShapeDtypeStruct((IMG, 2, TOK, HEAD), BF16)] * 4,
        in_specs=[smem()] + vmem(2),
        out_specs=vmem(4),
        compiler_params=params(8),
        name="pack_stale",
    )(me, keys, values)


def project_kernel(idx, x0, x1, x2, x3, m0, m1, m2, m3, wq, wk, wv, qg, kg,
                   q0, q1, q2, q3, qa, fk, fv, xs, acc):
    g = pl.program_id(0)

    @pl.when(g == 0)
    def _():
        blocks = [x[...].astype(F32) for x in (x0, x1, x2, x3)]
        total = sum(jnp.sum(b, axis=-1, keepdims=True) for b in blocks)
        mean = total / WIDTH
        square = sum(jnp.sum((b - mean) * (b - mean), axis=-1, keepdims=True) for b in blocks)
        rstd = lax.rsqrt(square / WIDTH + 1e-06)
        for j, (b, m) in enumerate(zip(blocks, (m0, m1, m2, m3))):
            for i in range(IMG):
                rows = slice(i * TOK, (i + 1) * TOK)
                normed = (b[rows] - mean[rows]) * rstd[rows]
                out = normed * (1.0 + m[IMG + i : IMG + i + 1, :]) + m[i : i + 1, :]
                out = out.astype(BF16)
                xs[2 * j, rows, :] = out[:, : PART // 2]
                xs[2 * j + 1, rows, :] = out[:, PART // 2 :]
        acc[...] = jnp.zeros_like(acc)

    part = xs[g]
    for j, w in enumerate((wq, wk, wv)):
        acc[j] += jnp.dot(part, w[...], preferred_element_type=F32)

    @pl.when(g == pl.num_programs(0) - 1)
    def _():
        for j, (gain, out) in enumerate(((qg, qa), (kg, fk))):
            for h in range(4):
                cut = slice(h * HEAD, (h + 1) * HEAD)
                v = acc[j, :, cut]
                v = v * lax.rsqrt(jnp.mean(v * v, axis=-1, keepdims=True) + 1e-06) * gain[...]
                out[:, cut] = v.astype(BF16)
        fv[...] = acc[2].astype(BF16)
        for d, q in enumerate((q0, q1, q2, q3)):
            q[...] = qa[:, head_slice(idx[4], d)]


def project(idx, xs, ms, weights, gains):
    def whole(shape):
        return pl.BlockSpec(shape, lambda g, idx: (0,) * len(shape))

    def weight_map(g, idx):
        return (idx[g // 2] * 2 + g % 2, 0)

    return pl.pallas_call(
        project_kernel,
        grid_spec=pltpu.PrefetchScalarGridSpec(
            num_scalar_prefetch=1,
            grid=(8,),
            in_specs=[whole((ROWS, PART))] * 4
            + [whole((2 * IMG, PART))] * 4
            + [pl.BlockSpec((PART // 2, COLS), weight_map)] * 3
            + [whole((1, HEAD))] * 2,
            out_specs=[whole((ROWS, HEAD))] * 4 + [whole((ROWS, COLS))] * 3,
            scratch_shapes=[
                pltpu.VMEM((8, ROWS, PART // 2), BF16),
                pltpu.VMEM((3, ROWS, COLS), F32),
            ],
        ),
        out_shape=[jax.ShapeDtypeStruct((ROWS, HEAD), BF16)] * 4
        + [jax.ShapeDtypeStruct((ROWS, COLS), BF16)] * 3,
        compiler_params=params(24),
        name="project",
    )(idx, *xs, *ms, *weights, *gains)


def near_kernel(qa, fk, fv, out, lse):
    lanes = lax.broadcasted_iota(jnp.int32, (TOK, HEAD), 1)
    for i in range(IMG):
        rows = slice(i * TOK, (i + 1) * TOK)
        levels = jnp.zeros((TOK, HEAD), F32)
        for h in range(4):
            cut = slice(h * HEAD, (h + 1) * HEAD)
            s = dot_t(qa[rows, cut], fk[rows, cut]) * SCORE
            top = jnp.max(s, axis=-1, keepdims=True)
            p = jnp.exp2(s - top)
            total = jnp.sum(p, axis=-1, keepdims=True)
            numer = jnp.dot(p.astype(BF16), fv[rows, cut], preferred_element_type=F32)
            out[rows, cut] = numer / total
            levels = jnp.where(lanes == h, top + jnp.log2(total), levels)
        lse[rows, :] = levels


def near(qa, fk, fv):
    return pl.pallas_call(
        near_kernel,
        out_shape=[
            jax.ShapeDtypeStruct((ROWS, COLS), F32),
            jax.ShapeDtypeStruct((ROWS, HEAD), F32),
        ],
        in_specs=vmem(3),
        out_specs=vmem(2),
        compiler_params=params(8),
        name="near",
    )(qa, fk, fv)


def attend_kernel(q0, q1, q2, q3, a0, b0, a1, b1, *outs):
    qs = (q0, q1, q2, q3)
    entries = 16
    count = entries * TOK
    row_patch = lax.broadcasted_iota(jnp.int32, (4 * TOK, 4 * TOK), 0) // TOK
    col_patch = lax.broadcasted_iota(jnp.int32, (4 * TOK, 4 * TOK), 1) // TOK
    own = row_patch == col_patch
    lse_rows = [jnp.zeros((1, HEAD), F32) for _ in range(4)]
    row = lax.broadcasted_iota(jnp.int32, (TOK, HEAD), 0)
    lane = lax.broadcasted_iota(jnp.int32, (TOK, HEAD), 1)
    for i, streams in enumerate(((a0, b0), (a1, b1))):
        q = jnp.concatenate([r[i * TOK : (i + 1) * TOK] for r in qs], axis=0)
        top = total = numer = None
        for stream in streams:
            for c in range(stream.shape[0] // entries):
                span = slice(c * entries, (c + 1) * entries)
                k = stream[span, 0].reshape(count, HEAD)
                v = stream[span, 1].reshape(count, HEAD)
                s = dot_t(q, k) * SCORE
                if top is None:
                    s = jnp.concatenate(
                        [jnp.where(own, -1e30, s[:, : 4 * TOK]), s[:, 4 * TOK :]], axis=1
                    )
                    top = jnp.max(s, axis=-1, keepdims=True)
                    p = jnp.exp2(s - top)
                    total = jnp.sum(p, axis=-1, keepdims=True)
                    numer = jnp.dot(p.astype(BF16), v, preferred_element_type=F32)
                else:
                    new = jnp.maximum(top, jnp.max(s, axis=-1, keepdims=True))
                    factor = jnp.exp2(top - new)
                    p = jnp.exp2(s - new)
                    total = total * factor + jnp.sum(p, axis=-1, keepdims=True)
                    numer = numer * factor + jnp.dot(
                        p.astype(BF16), v, preferred_element_type=F32
                    )
                    top = new
        out = (numer / total).astype(BF16)
        level = top + jnp.log2(total)
        for d in range(4):
            span = slice(d * TOK, (d + 1) * TOK)
            outs[d][i * TOK : (i + 1) * TOK, :] = out[span]
            lse_rows[d] += jnp.sum(
                jnp.where(lane == row + i * TOK, level[span], 0.0), axis=0, keepdims=True
            )
    sub = lax.broadcasted_iota(jnp.int32, (16, HEAD), 0)
    for d in range(4):
        high = lse_rows[d].astype(BF16).astype(F32)
        rest = lse_rows[d] - high
        middle = rest.astype(BF16).astype(F32)
        low = rest - middle
        tail = jnp.where(sub == 0, high, jnp.where(sub == 1, middle, jnp.where(sub == 2, low, 0.0)))
        outs[d][ROWS : ROWS + 16, :] = tail.astype(BF16)


def attend(qs, streams):
    return pl.pallas_call(
        attend_kernel,
        out_shape=[jax.ShapeDtypeStruct((ROWS + 16, HEAD), BF16)] * 4,
        in_specs=vmem(8),
        out_specs=vmem(4),
        compiler_params=params(32),
        name="attend",
    )(*qs, *streams)


def combine_kernel(me_ref, r0, r1, r2, r3, near_out, near_lse, att):
    me = me_ref[0]
    row = lax.broadcasted_iota(jnp.int32, (ROWS, HEAD), 0)
    lane = lax.broadcasted_iota(jnp.int32, (ROWS, HEAD), 1)
    for d, r in enumerate((r0, r1, r2, r3)):
        cut = head_slice(me, d)
        tail = r[ROWS : ROWS + 16, :].astype(F32)
        level = tail[0:1] + tail[1:2] + tail[2:3]
        far_lse = jnp.sum(jnp.where(lane == row, level, 0.0), axis=1, keepdims=True)
        own_lse = jnp.sum(
            jnp.where(lane == (me ^ d), near_lse[...], 0.0), axis=1, keepdims=True
        )
        top = jnp.maximum(far_lse, own_lse)
        far_weight = jnp.exp2(far_lse - top)
        own_weight = jnp.exp2(own_lse - top)
        out = r[:ROWS, :].astype(F32) * far_weight + near_out[:, cut] * own_weight
        att[:, cut] = (out / (far_weight + own_weight)).astype(BF16)


def combine(me, rs, near_out, near_lse):
    return pl.pallas_call(
        combine_kernel,
        out_shape=jax.ShapeDtypeStruct((ROWS, COLS), BF16),
        in_specs=[smem()] + vmem(6),
        out_specs=pl.BlockSpec(memory_space=pltpu.VMEM),
        compiler_params=params(8),
        name="combine",
    )(me, *rs, near_out, near_lse)


def group_swap(parts):
    return [parts[0]] + [
        lax.ppermute(parts[d], GROUP, [(i, i ^ d) for i in range(4)]) for d in (1, 2, 3)
    ]


def swap(value, axis, step):
    flips = ((1, 3), (3, 1))[step]
    if axis == "zh":
        names, far, near_ = ("core", axis), 1, 4
    else:
        names, far, near_ = (axis, "core"), 2, 1
    perm = [
        (a * far + c * near_, (a ^ flips[c]) * far + c * near_)
        for a in range(4)
        for c in range(2)
    ]
    return lax.ppermute(value, names, perm)


def spread(stream, first, second):
    for axis in (first, second):
        for step in range(2):
            other = swap(stream, axis, step)
            if axis == second and step == 1:
                return stream, other
            stream = jnp.concatenate([stream, other], axis=0)


def on_device(activations, mod_shift, mod_scale, w_query, w_key, w_value,
              query_gain, key_gain, stale_keys, stale_values):
    me = lax.axis_index("zl") * 2 + lax.axis_index("core")
    rank = lax.axis_index("zh")
    core = lax.axis_index("core")
    me1 = me.reshape(1).astype(jnp.int32)

    x0 = activations.reshape(ROWS, PART)
    m0 = jnp.concatenate([mod_shift, mod_scale], axis=0).astype(F32)
    x1, x2 = swap(x0, "zh", 0), swap(x0, "zh", 1)
    m1, m2 = swap(m0, "zh", 0), swap(m0, "zh", 1)

    packed = group_swap(pack(me1, stale_keys, stale_values))
    streams = [jnp.stack([p[i] for p in packed], axis=0) for i in range(IMG)]

    x3 = swap(x1, "zh", 1)
    m3 = swap(m1, "zh", 1)
    first = jnp.where(core == 0, 1, 3)
    idx = jnp.stack([rank, rank ^ first, rank ^ (first ^ 2), rank ^ 2, me]).astype(jnp.int32)

    a0, b0 = spread(streams[0], "x", "y")
    a1, b1 = spread(streams[1], "y", "x")

    q0, q1, q2, q3, qa, fk, fv = project(
        idx, (x0, x1, x2, x3), (m0, m1, m2, m3), (w_query, w_key, w_value),
        (query_gain.reshape(1, HEAD), key_gain.reshape(1, HEAD)),
    )
    qs = group_swap([q0, q1, q2, q3])
    near_out, near_lse = near(qa, fk, fv)
    outs = group_swap(attend(qs, (a0, b0, a1, b1)))
    att = combine(me1, outs, near_out, near_lse)
    shape = (IMG, TOK, COLS)
    return att.reshape(shape), fk.reshape(shape), fv.reshape(shape)


def solution(mesh):
    split = Mesh(mesh.devices.reshape(4, 2, 4, 2, 4), ("x", "zl", "y", "core", "zh"))
    patch = ("x", "zl", "y", "core")
    rows = P(None, patch, "zh")
    cols = P(None, "zh")
    return jax.shard_map(
        on_device,
        mesh=split,
        in_specs=(rows, cols, cols, cols, cols, cols, P(), P(), rows, rows),
        out_specs=(rows, rows, rows),
        check_vma=False,
    )
```

time: 329 us -> 103 us (0.31)
  waiting for transfers between devices: 203 us -> 36.8 us
  local copies, waits for them, and re-layouts: 63.5 us -> 9.51 us
  starting transfers between devices: 0.12 us -> 40.8 us
  matrix products: 26.7 us -> 0 us
  Pallas kernels: 0 us -> 14.9 us
  blocking collectives: 13.7 us -> 0 us
  between operations: 13.9 us -> 0.87 us
  other arithmetic: 6.77 us -> 0.05 us
    all_gather x3 -> x0, waiting for transfers between devices: 203 us -> none  [the longest x1 101 us: on_device(): lax.all_gather(stale_keys, 'patch', axis=1, tiled=True)]
    all_gather x2 -> x0, local copies, waits for them, and re-layouts: 42.5 us -> none  [the longest x1 21.4 us: on_device(): lax.all_gather(stale_keys, 'patch', axis=1, tiled=True)]
    ppermute x0 -> x23, starting transfers between devices: none -> 40.8 us  [the longest x14 20.9 us: swap(): return lax.ppermute(value, names, perm)]
    ppermute x0 -> x23, waiting for transfers between devices: none -> 36.8 us  [the longest x14 30.5 us: swap(): return lax.ppermute(value, names, perm)]
    dot_general x7 -> x0, matrix products: 26.7 us -> none  [the longest x1 8.88 us: fold_rows(): jnp.einsum('bqhk,bkhd->bqhd', weights.astype(jnp.bfloat16), split_values,...]
    pallas_call x0 -> x5, Pallas kernels: none -> 14.9 us  [the longest x1 6.89 us: project(): pl.pallas_call(project_kernel, grid_spec=pltpu.PrefetchScalarGridSpec(num...]
    psum x1 -> x0, blocking collectives: 13.7 us -> none  [on_device(): row_sums, row_squares = lax.psum((row_sums, row_squares), 'tp')]
    dot_general x2 -> x0, local copies, waits for them, and re-layouts: 12.8 us -> none  [the longest x1 6.41 us: on_device(): jnp.dot(flat_rows, w_key, preferred_element_type=jnp.float32)]
  transfers between devices with their start and end apart: 3 -> 23, of which waited for: 3 -> 14; matrix products, arithmetic and copies ran while one was open for 18% -> 1% of each run, Pallas kernels for 0% -> 9%
where the time goes in v1:
time: 103 us
  starting transfers between devices  40.8 us (40%)
  waiting for transfers between devices  36.8 us (36%)
  Pallas kernels  14.9 us (14%)
  local copies, waits for them, and re-layouts  9.51 us (9%)
    ppermute x14, waiting for transfers between devices, swap(): return lax.ppermute(value, names, perm)  30.5 us
    ppermute x14, starting transfers between devices, swap(): return lax.ppermute(value, names, perm)  20.9 us
    ppermute x9, starting transfers between devices, group_swap(): lax.ppermute(parts[d], GROUP, [(i, i ^ d) for i in range(4)])  19.9 us
    unnamed x30, local copies, waits for them, and re-layouts  8.92 us
    pallas_call x1, Pallas kernels, project(): pl.pallas_call(project_kernel, grid_spec=pltpu.PrefetchScalarGridSpec(num...  6.89 us
    ppermute x9, waiting for transfers between devices, group_swap(): lax.ppermute(parts[d], GROUP, [(i, i ^ d) for i in range(4)])  6.32 us
    pallas_call x1, Pallas kernels, attend(): pl.pallas_call(attend_kernel, out_shape=[jax.ShapeDtypeStruct((ROWS + 16,...  5.19 us
  transfers between devices with their start and end apart: 23, of which 14 were waited for; matrix products, arithmetic and copies ran while one was open for 1% of the time, Pallas kernels for 9%

profile of v1, /device:TPU:1, one launch (start us, length us, event | category | flops | bytes accessed | tf_op | source)
XLA Modules:
  0.0 102.9 jit_solution(7792040321352998342)
XLA Ops:
  0.7 0.9 copy-done.6
  1.6 0.9 copy-done.7
  2.5 0.1 pack_stale.1
  2.6 3.3 %collective-permute-start.9 = (bf16[2,2,64,128]{3,2,1,0:T(8,128)(2,1)S(1)}, bf16[2,2,64,128]{3,2,1,0:T(8,128)(2,1)S(1)}, u32[]{:S(2)}, u32[]{:S(2)}) collective-permute-start(bf16[2,2,64,128]{3,2,1,0:T(8,128)(2,1)S(1)} %get-tuple-element.25), channel_id=1, source_target_pairs={{0,4},{4,0},{32,36},{36,32},{1,5},{5,1},{33,37},{37,33},{2,6},{6,2... | collective-permute-start | bytes 196616 | tf_op jit(solution)/shard_map/ppermute | solution.py:258
  5.9 0.0 collective-permute-start.10
  5.9 1.7 %collective-permute-start.11 = (bf16[2,2,64,128]{3,2,1,0:T(8,128)(2,1)S(1)}, bf16[2,2,64,128]{3,2,1,0:T(8,128)(2,1)S(1)}, u32[]{:S(2)}, u32[]{:S(2)}) collective-permute-start(bf16[2,2,64,128]{3,2,1,0:T(8,128)(2,1)S(1)} %get-tuple-element.27), channel_id=1, source_target_pairs={{0,36},{4,32},{32,4},{36,0},{1,37},{5,33},{33,5},{37,1},{2,38},{6,... | collective-permute-start | bytes 196616 | tf_op jit(solution)/shard_map/ppermute | solution.py:258
  7.7 0.0 collective-permute-done.9
  7.7 0.1 constant_dynamic-update-slice_fusion.27
  7.8 1.8 %collective-permute-done.10 = bf16[2,2,64,128]{3,2,1,0:T(8,128)(2,1)S(1)} collective-permute-done((bf16[2,2,64,128]{3,2,1,0:T(8,128)(2,1)S(1)}, bf16[2,2,64,128]{3,2,1,0:T(8,128)(2,1)S(1)}, u32[]{:S(2)}, u32[]{:S(2)}) %collective-permute-start.10) | collective-permute-done | bytes 65568 | tf_op jit(solution)/shard_map/ppermute | solution.py:258
  9.6 0.1 constant_dynamic-update-slice_fusion.26
  9.6 1.5 %collective-permute-done.11 = bf16[2,2,64,128]{3,2,1,0:T(8,128)(2,1)S(1)} collective-permute-done((bf16[2,2,64,128]{3,2,1,0:T(8,128)(2,1)S(1)}, bf16[2,2,64,128]{3,2,1,0:T(8,128)(2,1)S(1)}, u32[]{:S(2)}, u32[]{:S(2)}) %collective-permute-start.11) | collective-permute-done | bytes 65568 | tf_op jit(solution)/shard_map/ppermute | solution.py:258
  11.1 0.1 constant_dynamic-update-slice_fusion.25
  11.3 1.6 %collective-permute-start.16 = (bf16[4,2,64,128]{3,2,1,0:T(8,128)(2,1)S(1)}, bf16[4,2,64,128]{3,2,1,0:T(8,128)(2,1)S(1)}, u32[]{:S(2)}, u32[]{:S(2)}) collective-permute-start(bf16[4,2,64,128]{3,2,1,0:T(8,128)(2,1)S(1)} %pad_maximum_fusion.1), channel_id=1, source_target_pairs={{0,8},{4,28},{8,0},{12,20},{16,24},{20,12},{24,16},{28,4},{1,9},{5... | collective-permute-start | bytes 393224 | tf_op jit(solution)/shard_map/ppermute | solution.py:273
  12.8 2.6 %collective-permute-start.12 = (bf16[4,2,64,128]{3,2,1,0:T(8,128)(2,1)S(1)}, bf16[4,2,64,128]{3,2,1,0:T(8,128)(2,1)S(1)}, u32[]{:S(2)}, u32[]{:S(2)}) collective-permute-start(bf16[4,2,64,128]{3,2,1,0:T(8,128)(2,1)S(1)} %pad_maximum_fusion), channel_id=1, source_target_pairs={{0,64},{4,196},{64,0},{68,132},{128,192},{132,68},{192,128},{196,4... | collective-permute-start | bytes 393224 | tf_op jit(solution)/shard_map/ppermute | solution.py:273
  15.4 1.0 collective-permute-done.16
  16.4 0.1 constant_dynamic-update-slice_fusion.24
  16.5 0.1 collective-permute-start.17
  16.6 1.4 %collective-permute-done.12 = bf16[4,2,64,128]{3,2,1,0:T(8,128)(2,1)S(1)} collective-permute-done((bf16[4,2,64,128]{3,2,1,0:T(8,128)(2,1)S(1)}, bf16[4,2,64,128]{3,2,1,0:T(8,128)(2,1)S(1)}, u32[]{:S(2)}, u32[]{:S(2)}) %collective-permute-start.12) | collective-permute-done | bytes 131104 | tf_op jit(solution)/shard_map/ppermute | solution.py:273
  18.0 0.1 constant_dynamic-update-slice_fusion.6
  18.1 0.1 collective-permute-start.13
  18.2 3.9 %collective-permute-done.17 = bf16[8,2,64,128]{3,2,1,0:T(8,128)(2,1)S(1)} collective-permute-done((bf16[8,2,64,128]{3,2,1,0:T(8,128)(2,1)S(1)}, bf16[8,2,64,128]{3,2,1,0:T(8,128)(2,1)S(1)}, u32[]{:S(2)}, u32[]{:S(2)}) %collective-permute-start.17) | collective-permute-done | bytes 262176 | tf_op jit(solution)/shard_map/ppermute | solution.py:273
  22.1 0.2 constant_dynamic-update-slice_fusion.23
  22.3 1.4 %collective-permute-start.18 = (bf16[16,2,64,128]{3,2,1,0:T(8,128)(2,1)S(1)}, bf16[16,2,64,128]{3,2,1,0:T(8,128)(2,1)S(1)}, u32[]{:S(2)}, u32[]{:S(2)}) collective-permute-start(bf16[16,2,64,128]{3,2,1,0:T(8,128)(2,1)S(1)} %get-tuple-element.37), channel_id=1, source_target_pairs={{0,64},{4,196},{64,0},{68,132},{128,192},{132,68},{192,128},{196,4... | collective-permute-start | bytes 1572872 | tf_op jit(solution)/shard_map/ppermute | solution.py:273
  23.7 0.0 collective-permute-done.13
  23.7 0.2 constant_dynamic-update-slice_fusion.5
  23.9 2.7 %collective-permute-start.14 = (bf16[16,2,64,128]{3,2,1,0:T(8,128)(2,1)S(1)}, bf16[16,2,64,128]{3,2,1,0:T(8,128)(2,1)S(1)}, u32[]{:S(2)}, u32[]{:S(2)}) collective-permute-start(bf16[16,2,64,128]{3,2,1,0:T(8,128)(2,1)S(1)} %get-tuple-element.39), channel_id=1, source_target_pairs={{0,8},{4,28},{8,0},{12,20},{16,24},{20,12},{24,16},{28,4},{1,9},{5... | collective-permute-start | bytes 1572872 | tf_op jit(solution)/shard_map/ppermute | solution.py:273
  26.6 5.0 %collective-permute-done.18 = bf16[16,2,64,128]{3,2,1,0:T(8,128)(2,1)S(1)} collective-permute-done((bf16[16,2,64,128]{3,2,1,0:T(8,128)(2,1)S(1)}, bf16[16,2,64,128]{3,2,1,0:T(8,128)(2,1)S(1)}, u32[]{:S(2)}, u32[]{:S(2)}) %collective-permute-start.18) | collective-permute-done | bytes 524320 | tf_op jit(solution)/shard_map/ppermute | solution.py:273
  31.6 0.1 constant_dynamic-update-slice_fusion.29.a1
  31.7 0.1 collective-permute-start.19
  31.8 1.4 %collective-permute-done.14 = bf16[16,2,64,128]{3,2,1,0:T(8,128)(2,1)S(1)} collective-permute-done((bf16[16,2,64,128]{3,2,1,0:T(8,128)(2,1)S(1)}, bf16[16,2,64,128]{3,2,1,0:T(8,128)(2,1)S(1)}, u32[]{:S(2)}, u32[]{:S(2)}) %collective-permute-start.14) | collective-permute-done | bytes 524320 | tf_op jit(solution)/shard_map/ppermute | solution.py:273
  33.2 0.1 constant_dynamic-update-slice_fusion.11.a0
  33.3 0.1 collective-permute-start.15
  33.4 5.6 %collective-permute-start = (bf16[128,1024]{1,0:T(8,128)(2,1)S(1)}, bf16[128,1024]{1,0:T(8,128)(2,1)}, u32[]{:S(2)}, u32[]{:S(2)}) collective-permute-start(bf16[128,1024]{1,0:T(8,128)(2,1)S(1)} %bitcast.11), channel_id=1, source_target_pairs={{0,1},{4,7},{1,0},{5,6},{2,3},{6,5},{3,2},{7,4},{8,9},{12,15},{9,8... | collective-permute-start | bytes 786440 | tf_op jit(solution)/shard_map/ppermute | solution.py:273
  39.0 1.2 %collective-permute-start.1 = (bf16[128,1024]{1,0:T(8,128)(2,1)S(1)}, bf16[128,1024]{1,0:T(8,128)(2,1)}, u32[]{:S(2)}, u32[]{:S(2)}) collective-permute-start(bf16[128,1024]{1,0:T(8,128)(2,1)S(1)} %bitcast.12), channel_id=1, source_target_pairs={{0,3},{4,5},{1,2},{5,4},{2,1},{6,7},{3,0},{7,6},{8,11},{12,13},{9,... | collective-permute-start | bytes 786440 | tf_op jit(solution)/shard_map/ppermute | solution.py:273
  40.2 4.9 %collective-permute-done.x1 = bf16[128,1024]{1,0:T(8,128)(2,1)} collective-permute-done((bf16[128,1024]{1,0:T(8,128)(2,1)S(1)}, bf16[128,1024]{1,0:T(8,128)(2,1)}, u32[]{:S(2)}, u32[]{:S(2)}) %collective-permute-start) | collective-permute-done | bytes 262176 | tf_op jit(solution)/shard_map/ppermute | solution.py:273
  45.2 1.8 %collective-permute-start.2 = (bf16[128,1024]{1,0:T(8,128)(2,1)}, bf16[128,1024]{1,0:T(8,128)(2,1)}, u32[]{:S(2)}, u32[]{:S(2)}) collective-permute-start(bf16[128,1024]{1,0:T(8,128)(2,1)} %collective-permute-done.x1), channel_id=1, source_target_pairs={{0,3},{4,5},{1,2},{5,4},{2,1},{6,7},{3,0},{7,6},{8,11},{12,13},{9,... | collective-permute-start | bytes 786440 | tf_op jit(solution)/shard_map/ppermute | solution.py:273
  47.0 2.5 %collective-permute-start.3 = (f32[4,1024]{1,0:T(4,128)S(1)}, f32[4,1024]{1,0:T(4,128)S(1)}, u32[]{:S(2)}, u32[]{:S(2)}) collective-permute-start(f32[4,1024]{1,0:T(4,128)S(1)} %maximum_convert_fusion.m0), channel_id=1, source_target_pairs={{0,1},{4,7},{1,0},{5,6},{2,3},{6,5},{3,2},{7,4},{8,9},{12,15},{9,8... | collective-permute-start | bytes 49160 | tf_op jit(solution)/shard_map/ppermute | solution.py:273
  49.5 3.0 %collective-permute-done.3.m1 = f32[4,1024]{1,0:T(4,128)S(1)} collective-permute-done((f32[4,1024]{1,0:T(4,128)S(1)}, f32[4,1024]{1,0:T(4,128)S(1)}, u32[]{:S(2)}, u32[]{:S(2)}) %collective-permute-start.3) | collective-permute-done | bytes 16416 | tf_op jit(solution)/shard_map/ppermute | solution.py:273
  52.5 1.1 %collective-permute-start.4 = (f32[4,1024]{1,0:T(4,128)S(1)}, f32[4,1024]{1,0:T(4,128)S(1)}, u32[]{:S(2)}, u32[]{:S(2)}) collective-permute-start(f32[4,1024]{1,0:T(4,128)S(1)} %maximum_convert_fusion.m0), channel_id=1, source_target_pairs={{0,3},{4,5},{1,2},{5,4},{2,1},{6,7},{3,0},{7,6},{8,11},{12,13},{9,... | collective-permute-start | bytes 49160 | tf_op jit(solution)/shard_map/ppermute | solution.py:273
  53.6 6.1 %collective-permute-done.4.m2 = f32[4,1024]{1,0:T(4,128)S(1)} collective-permute-done((f32[4,1024]{1,0:T(4,128)S(1)}, f32[4,1024]{1,0:T(4,128)S(1)}, u32[]{:S(2)}, u32[]{:S(2)}) %collective-permute-start.4) | collective-permute-done | bytes 16416 | tf_op jit(solution)/shard_map/ppermute | solution.py:273
  59.7 0.0 collective-permute-start.5
  59.7 0.1 stack.26.idx
  59.8 3.8 %collective-permute-done.5.m3 = f32[4,1024]{1,0:T(4,128)S(1)} collective-permute-done((f32[4,1024]{1,0:T(4,128)S(1)}, f32[4,1024]{1,0:T(4,128)S(1)}, u32[]{:S(2)}, u32[]{:S(2)}) %collective-permute-start.5) | collective-permute-done | bytes 16416 | tf_op jit(solution)/shard_map/ppermute | solution.py:273
  63.6 0.0 collective-permute-done.1.x2
  63.6 0.0 copy-start
  63.6 2.2 %copy-done = bf16[4096,512]{1,0:T(8,128)(2,1)S(1)} copy-done((bf16[4096,512]{1,0:T(8,128)(2,1)S(1)}, bf16[4096,512]{1,0:T(8,128)(2,1)}, u32[]{:S(2)}) %copy-start) | copy-done | bytes 4194328
  65.8 2.2 %copy-done.1 = bf16[4096,512]{1,0:T(8,128)(2,1)S(1)} copy-done((bf16[4096,512]{1,0:T(8,128)(2,1)S(1)}, bf16[4096,512]{1,0:T(8,128)(2,1)}, u32[]{:S(2)}) %copy-start.1) | copy-done | bytes 4194328
  68.0 2.2 %copy-done.2 = bf16[4096,512]{1,0:T(8,128)(2,1)S(1)} copy-done((bf16[4096,512]{1,0:T(8,128)(2,1)S(1)}, bf16[4096,512]{1,0:T(8,128)(2,1)}, u32[]{:S(2)}) %copy-start.2) | copy-done | bytes 4194328
  70.2 6.9 %project.1 = (bf16[128,128]{1,0:T(8,128)(2,1)S(1)}, bf16[128,128]{1,0:T(8,128)(2,1)S(1)}, bf16[128,128]{1,0:T(8,128)(2,1)S(1)}, bf16[128,128]{1,0:T(8,128)(2,1)S...) custom-call(s32[5]{0:T(128)S(1)} %stack.26.idx, ...), custom_call_target="tpu_custom_call" | custom-call | tf_op jit(solution)/shard_map/project/pallas_call | solution.py:108
  77.1 10.9 %collective-permute-start.6 = (bf16[128,128]{1,0:T(8,128)(2,1)S(1)}, bf16[128,128]{1,0:T(8,128)(2,1)S(1)}, u32[]{:S(2)}, u32[]{:S(2)}) collective-permute-start(bf16[128,128]{1,0:T(8,128)(2,1)S(1)} %get-tuple-element.21), channel_id=1, source_target_pairs={{0,4},{4,0},{32,36},{36,32},{1,5},{5,1},{33,37},{37,33},{2,6},{6,2... | collective-permute-start | bytes 98312 | tf_op jit(solution)/shard_map/ppermute | solution.py:258
  87.9 0.2 collective-permute-start.7
  88.1 1.5 %collective-permute-start.8 = (bf16[128,128]{1,0:T(8,128)(2,1)S(1)}, bf16[128,128]{1,0:T(8,128)(2,1)S(1)}, u32[]{:S(2)}, u32[]{:S(2)}) collective-permute-start(bf16[128,128]{1,0:T(8,128)(2,1)S(1)} %get-tuple-element.23), channel_id=1, source_target_pairs={{0,36},{4,32},{32,4},{36,0},{1,37},{5,33},{33,5},{37,1},{2,38},{6,... | collective-permute-start | bytes 98312 | tf_op jit(solution)/shard_map/ppermute | solution.py:258
  89.7 0.0 collective-permute-done.6.q1
  89.7 1.0 %collective-permute-done.7.q2 = bf16[128,128]{1,0:T(8,128)(2,1)S(1)} collective-permute-done((bf16[128,128]{1,0:T(8,128)(2,1)S(1)}, bf16[128,128]{1,0:T(8,128)(2,1)S(1)}, u32[]{:S(2)}, u32[]{:S(2)}) %collective-permute-start.7) | collective-permute-done | bytes 32800 | tf_op jit(solution)/shard_map/ppermute | solution.py:258
  90.7 1.1 %collective-permute-done.8.q3 = bf16[128,128]{1,0:T(8,128)(2,1)S(1)} collective-permute-done((bf16[128,128]{1,0:T(8,128)(2,1)S(1)}, bf16[128,128]{1,0:T(8,128)(2,1)S(1)}, u32[]{:S(2)}, u32[]{:S(2)}) %collective-permute-start.8) | collective-permute-done | bytes 32800 | tf_op jit(solution)/shard_map/ppermute | solution.py:258
  91.9 0.0 collective-permute-done.15.b0
  91.9 5.2 %attend.1 = (bf16[144,128]{1,0:T(8,128)(2,1)S(1)}, bf16[144,128]{1,0:T(8,128)(2,1)S(1)}, bf16[144,128]{1,0:T(8,128)(2,1)S(1)}, bf16[144,128]{1,0:T(8,128)(2,1)S(1)}) custom-call(bf16[128,128]{1,0:T(8,128)(2,1)S(1)} %get-tuple-element.20.q0, bf16[128,128]{1,0:T(8,128)(2,1)S(1)} %collective-permute-done.6.q1, bf16[128,128]{1,0:T(8,128)(2,1)S(1)} %collective-permute-done.7.q2, ...), custom_call_target="tpu_custom_call" | custom-call | tf_op jit(solution)/shard_map/attend/pallas_call | solution.py:216
  97.1 0.4 collective-permute-start.20
  97.5 0.9 collective-permute-start.21
  98.4 0.9 collective-permute-start.22
  99.3 1.9 %near.1 = (f32[128,512]{1,0:T(8,128)S(1)}, f32[128,128]{1,0:T(8,128)S(1)}) custom-call(bf16[128,512]{1,0:T(8,128)(2,1)S(1)} %get-tuple-element.32.qa, bf16[128,512]{1,0:T(8,128)(2,1)S(1)} %copy-done.4, bf16[128,512]{1,0:T(8,128)(2,1)S(1)} %copy-done.5), custom_call_target="tpu_custom_call" | custom-call | tf_op jit(solution)/shard_map/near/pallas_call | solution.py:148
  101.2 0.0 collective-permute-done.20.r1
  101.2 0.8 collective-permute-done.22.r3
  102.0 0.9 combine.1
  (25 shorter events, 0.1 us)
Async XLA Ops:
  0.6 32.8 %copy-start.3 = (bf16[2,64,1024]{2,1,0:T(8,128)(2,1)S(1)}, bf16[2,64,1024]{2,1,0:T(8,128)(2,1)}, u32[]{:S(2)}) copy-start(bf16[2,64,1024]{2,1,0:T(8,128)(2,1)} %param.10) | copy-start | bytes 786436
  0.7 0.9 copy-start.6
  1.6 0.9 copy-start.7
  2.5 44.5 %copy-start.10 = (bf16[2,1024]{1,0:T(2,128)(2,1)S(1)}, bf16[2,1024]{1,0:T(2,128)(2,1)}, u32[]{:S(2)}) copy-start(bf16[2,1024]{1,0:T(2,128)(2,1)} %param.12) | copy-start | bytes 12292
  2.5 44.5 %copy-start.11 = (bf16[2,1024]{1,0:T(2,128)(2,1)S(1)}, bf16[2,1024]{1,0:T(2,128)(2,1)}, u32[]{:S(2)}) copy-start(bf16[2,1024]{1,0:T(2,128)(2,1)} %param.11) | copy-start | bytes 12292
  2.5 61.1 %copy-start.8 = (f32[128]{0:T(128)S(1)}, f32[128]{0:T(128)}, u32[]{:S(2)}) copy-start(f32[128]{0:T(128)} %param.16) | copy-start | bytes 1540
  2.5 61.1 %copy-start.9 = (f32[128]{0:T(128)S(1)}, f32[128]{0:T(128)}, u32[]{:S(2)}) copy-start(f32[128]{0:T(128)} %param.17) | copy-start | bytes 1540
  2.6 5.1 %collective-permute-start.9 = (bf16[2,2,64,128]{3,2,1,0:T(8,128)(2,1)S(1)}, bf16[2,2,64,128]{3,2,1,0:T(8,128)(2,1)S(1)}, u32[]{:S(2)}, u32[]{:S(2)}) collective-permute-start(bf16[2,2,64,128]{3,2,1,0:T(8,128)(2,1)S(1)} %get-tuple-element.25), channel_id=1, source_target_pairs={{0,4},{4,0},{32,36},{36,32},{1,5},{5,1},{33,37},{37,33},{2,6},{6,2... | collective-permute-start | bytes 196616 | tf_op jit(solution)/shard_map/ppermute | solution.py:258
  5.9 3.7 %collective-permute-start.10 = (bf16[2,2,64,128]{3,2,1,0:T(8,128)(2,1)S(1)}, bf16[2,2,64,128]{3,2,1,0:T(8,128)(2,1)S(1)}, u32[]{:S(2)}, u32[]{:S(2)}) collective-permute-start(bf16[2,2,64,128]{3,2,1,0:T(8,128)(2,1)S(1)} %get-tuple-element.26), channel_id=1, source_target_pairs={{0,32},{4,36},{32,0},{36,4},{1,33},{5,37},{33,1},{37,5},{2,34},{6,... | collective-permute-start | bytes 196616 | tf_op jit(solution)/shard_map/ppermute | solution.py:258
  5.9 5.2 %collective-permute-start.11 = (bf16[2,2,64,128]{3,2,1,0:T(8,128)(2,1)S(1)}, bf16[2,2,64,128]{3,2,1,0:T(8,128)(2,1)S(1)}, u32[]{:S(2)}, u32[]{:S(2)}) collective-permute-start(bf16[2,2,64,128]{3,2,1,0:T(8,128)(2,1)S(1)} %get-tuple-element.27), channel_id=1, source_target_pairs={{0,36},{4,32},{32,4},{36,0},{1,37},{5,33},{33,5},{37,1},{2,38},{6,... | collective-permute-start | bytes 196616 | tf_op jit(solution)/shard_map/ppermute | solution.py:258
  11.3 5.1 %collective-permute-start.16 = (bf16[4,2,64,128]{3,2,1,0:T(8,128)(2,1)S(1)}, bf16[4,2,64,128]{3,2,1,0:T(8,128)(2,1)S(1)}, u32[]{:S(2)}, u32[]{:S(2)}) collective-permute-start(bf16[4,2,64,128]{3,2,1,0:T(8,128)(2,1)S(1)} %pad_maximum_fusion.1), channel_id=1, source_target_pairs={{0,8},{4,28},{8,0},{12,20},{16,24},{20,12},{24,16},{28,4},{1,9},{5... | collective-permute-start | bytes 393224 | tf_op jit(solution)/shard_map/ppermute | solution.py:273
  12.8 5.1 %collective-permute-start.12 = (bf16[4,2,64,128]{3,2,1,0:T(8,128)(2,1)S(1)}, bf16[4,2,64,128]{3,2,1,0:T(8,128)(2,1)S(1)}, u32[]{:S(2)}, u32[]{:S(2)}) collective-permute-start(bf16[4,2,64,128]{3,2,1,0:T(8,128)(2,1)S(1)} %pad_maximum_fusion), channel_id=1, source_target_pairs={{0,64},{4,196},{64,0},{68,132},{128,192},{132,68},{192,128},{196,4... | collective-permute-start | bytes 393224 | tf_op jit(solution)/shard_map/ppermute | solution.py:273
  16.5 5.6 %collective-permute-start.17 = (bf16[8,2,64,128]{3,2,1,0:T(8,128)(2,1)S(1)}, bf16[8,2,64,128]{3,2,1,0:T(8,128)(2,1)S(1)}, u32[]{:S(2)}, u32[]{:S(2)}) collective-permute-start(bf16[8,2,64,128]{3,2,1,0:T(8,128)(2,1)S(1)} %get-tuple-element.43), channel_id=1, source_target_pairs={{0,24},{4,12},{8,16},{12,4},{16,8},{20,28},{24,0},{28,20},{1,25},{... | collective-permute-start | bytes 786440 | tf_op jit(solution)/shard_map/ppermute | solution.py:273
  18.1 5.6 %collective-permute-start.13 = (bf16[8,2,64,128]{3,2,1,0:T(8,128)(2,1)S(1)}, bf16[8,2,64,128]{3,2,1,0:T(8,128)(2,1)S(1)}, u32[]{:S(2)}, u32[]{:S(2)}) collective-permute-start(bf16[8,2,64,128]{3,2,1,0:T(8,128)(2,1)S(1)} %get-tuple-element.46), channel_id=1, source_target_pairs={{0,192},{4,68},{64,128},{68,4},{128,64},{132,196},{192,0},{196,132... | collective-permute-start | bytes 786440 | tf_op jit(solution)/shard_map/ppermute | solution.py:273
  22.3 9.3 %collective-permute-start.18 = (bf16[16,2,64,128]{3,2,1,0:T(8,128)(2,1)S(1)}, bf16[16,2,64,128]{3,2,1,0:T(8,128)(2,1)S(1)}, u32[]{:S(2)}, u32[]{:S(2)}) collective-permute-start(bf16[16,2,64,128]{3,2,1,0:T(8,128)(2,1)S(1)} %get-tuple-element.37), channel_id=1, source_target_pairs={{0,64},{4,196},{64,0},{68,132},{128,192},{132,68},{192,128},{196,4... | collective-permute-start | bytes 1572872 | tf_op jit(solution)/shard_map/ppermute | solution.py:273
  23.9 9.3 %collective-permute-start.14 = (bf16[16,2,64,128]{3,2,1,0:T(8,128)(2,1)S(1)}, bf16[16,2,64,128]{3,2,1,0:T(8,128)(2,1)S(1)}, u32[]{:S(2)}, u32[]{:S(2)}) collective-permute-start(bf16[16,2,64,128]{3,2,1,0:T(8,128)(2,1)S(1)} %get-tuple-element.39), channel_id=1, source_target_pairs={{0,8},{4,28},{8,0},{12,20},{16,24},{20,12},{24,16},{28,4},{1,9},{5... | collective-permute-start | bytes 1572872 | tf_op jit(solution)/shard_map/ppermute | solution.py:273
  31.7 60.2 %collective-permute-start.19 = (bf16[32,2,64,128]{3,2,1,0:T(8,128)(2,1)S(1)}, bf16[32,2,64,128]{3,2,1,0:T(8,128)(2,1)S(1)}, u32[]{:S(2)}, u32[]{:S(2)}) collective-permute-start(bf16[32,2,64,128]{3,2,1,0:T(8,128)(2,1)S(1)} %constant_dynamic-update-slice_fusion.29.a1), channel_id=1, source_target_pairs={{0,192},{4,68},{64,128},{68,4},{128,64},{132,196},{192,0},{196,132... | collective-permute-start | bytes 3145736 | tf_op jit(solution)/shard_map/ppermute | solution.py:273
  33.3 58.6 %collective-permute-start.15 = (bf16[32,2,64,128]{3,2,1,0:T(8,128)(2,1)S(1)}, bf16[32,2,64,128]{3,2,1,0:T(8,128)(2,1)}, u32[]{:S(2)}, u32[]{:S(2)}) collective-permute-start(bf16[32,2,64,128]{3,2,1,0:T(8,128)(2,1)S(1)} %constant_dynamic-update-slice_fusion.11.a0), channel_id=1, source_target_pairs={{0,24},{4,12},{8,16},{12,4},{16,8},{20,28},{24,0},{28,20},{1,25},{... | collective-permute-start | bytes 3145736 | tf_op jit(solution)/shard_map/ppermute | solution.py:273
  33.4 11.8 %collective-permute-start = (bf16[128,1024]{1,0:T(8,128)(2,1)S(1)}, bf16[128,1024]{1,0:T(8,128)(2,1)}, u32[]{:S(2)}, u32[]{:S(2)}) collective-permute-start(bf16[128,1024]{1,0:T(8,128)(2,1)S(1)} %bitcast.11), channel_id=1, source_target_pairs={{0,1},{4,7},{1,0},{5,6},{2,3},{6,5},{3,2},{7,4},{8,9},{12,15},{9,8... | collective-permute-start | bytes 786440 | tf_op jit(solution)/shard_map/ppermute | solution.py:273
  39.0 24.6 %collective-permute-start.1 = (bf16[128,1024]{1,0:T(8,128)(2,1)S(1)}, bf16[128,1024]{1,0:T(8,128)(2,1)}, u32[]{:S(2)}, u32[]{:S(2)}) collective-permute-start(bf16[128,1024]{1,0:T(8,128)(2,1)S(1)} %bitcast.12), channel_id=1, source_target_pairs={{0,3},{4,5},{1,2},{5,4},{2,1},{6,7},{3,0},{7,6},{8,11},{12,13},{9,... | collective-permute-start | bytes 786440 | tf_op jit(solution)/shard_map/ppermute | solution.py:273
  45.2 18.4 %collective-permute-start.2 = (bf16[128,1024]{1,0:T(8,128)(2,1)}, bf16[128,1024]{1,0:T(8,128)(2,1)}, u32[]{:S(2)}, u32[]{:S(2)}) collective-permute-start(bf16[128,1024]{1,0:T(8,128)(2,1)} %collective-permute-done.x1), channel_id=1, source_target_pairs={{0,3},{4,5},{1,2},{5,4},{2,1},{6,7},{3,0},{7,6},{8,11},{12,13},{9,... | collective-permute-start | bytes 786440 | tf_op jit(solution)/shard_map/ppermute | solution.py:273
  47.0 5.5 %collective-permute-start.3 = (f32[4,1024]{1,0:T(4,128)S(1)}, f32[4,1024]{1,0:T(4,128)S(1)}, u32[]{:S(2)}, u32[]{:S(2)}) collective-permute-start(f32[4,1024]{1,0:T(4,128)S(1)} %maximum_convert_fusion.m0), channel_id=1, source_target_pairs={{0,1},{4,7},{1,0},{5,6},{2,3},{6,5},{3,2},{7,4},{8,9},{12,15},{9,8... | collective-permute-start | bytes 49160 | tf_op jit(solution)/shard_map/ppermute | solution.py:273
  52.5 7.2 %collective-permute-start.4 = (f32[4,1024]{1,0:T(4,128)S(1)}, f32[4,1024]{1,0:T(4,128)S(1)}, u32[]{:S(2)}, u32[]{:S(2)}) collective-permute-start(f32[4,1024]{1,0:T(4,128)S(1)} %maximum_convert_fusion.m0), channel_id=1, source_target_pairs={{0,3},{4,5},{1,2},{5,4},{2,1},{6,7},{3,0},{7,6},{8,11},{12,13},{9,... | collective-permute-start | bytes 49160 | tf_op jit(solution)/shard_map/ppermute | solution.py:273
  59.7 3.9 %collective-permute-start.5 = (f32[4,1024]{1,0:T(4,128)S(1)}, f32[4,1024]{1,0:T(4,128)S(1)}, u32[]{:S(2)}, u32[]{:S(2)}) collective-permute-start(f32[4,1024]{1,0:T(4,128)S(1)} %collective-permute-done.3.m1), channel_id=1, source_target_pairs={{0,3},{4,5},{1,2},{5,4},{2,1},{6,7},{3,0},{7,6},{8,11},{12,13},{9,... | collective-permute-start | bytes 49160 | tf_op jit(solution)/shard_map/ppermute | solution.py:273
  63.6 2.2 %copy-start = (bf16[4096,512]{1,0:T(8,128)(2,1)S(1)}, bf16[4096,512]{1,0:T(8,128)(2,1)}, u32[]{:S(2)}) copy-start(bf16[4096,512]{1,0:T(8,128)(2,1)} %wq.1) | copy-start | bytes 12582916
  65.8 2.2 %copy-start.1 = (bf16[4096,512]{1,0:T(8,128)(2,1)S(1)}, bf16[4096,512]{1,0:T(8,128)(2,1)}, u32[]{:S(2)}) copy-start(bf16[4096,512]{1,0:T(8,128)(2,1)} %wk.1) | copy-start | bytes 12582916
  68.0 2.2 %copy-start.2 = (bf16[4096,512]{1,0:T(8,128)(2,1)S(1)}, bf16[4096,512]{1,0:T(8,128)(2,1)}, u32[]{:S(2)}) copy-start(bf16[4096,512]{1,0:T(8,128)(2,1)} %wv.1) | copy-start | bytes 12582916
  77.1 22.2 %copy-start.4 = (bf16[128,512]{1,0:T(8,128)(2,1)S(1)}, bf16[128,512]{1,0:T(8,128)(2,1)}, u32[]{:S(2)}) copy-start(bf16[128,512]{1,0:T(8,128)(2,1)} %get-tuple-element.33.fk) | copy-start | bytes 393220
  77.1 22.2 %copy-start.5 = (bf16[128,512]{1,0:T(8,128)(2,1)S(1)}, bf16[128,512]{1,0:T(8,128)(2,1)}, u32[]{:S(2)}) copy-start(bf16[128,512]{1,0:T(8,128)(2,1)} %get-tuple-element.34.fv) | copy-start | bytes 393220
  77.1 12.6 %collective-permute-start.6 = (bf16[128,128]{1,0:T(8,128)(2,1)S(1)}, bf16[128,128]{1,0:T(8,128)(2,1)S(1)}, u32[]{:S(2)}, u32[]{:S(2)}) collective-permute-start(bf16[128,128]{1,0:T(8,128)(2,1)S(1)} %get-tuple-element.21), channel_id=1, source_target_pairs={{0,4},{4,0},{32,36},{36,32},{1,5},{5,1},{33,37},{37,33},{2,6},{6,2... | collective-permute-start | bytes 98312 | tf_op jit(solution)/shard_map/ppermute | solution.py:258
  87.9 2.8 %collective-permute-start.7 = (bf16[128,128]{1,0:T(8,128)(2,1)S(1)}, bf16[128,128]{1,0:T(8,128)(2,1)S(1)}, u32[]{:S(2)}, u32[]{:S(2)}) collective-permute-start(bf16[128,128]{1,0:T(8,128)(2,1)S(1)} %get-tuple-element.22), channel_id=1, source_target_pairs={{0,32},{4,36},{32,0},{36,4},{1,33},{5,37},{33,1},{37,5},{2,34},{6,... | collective-permute-start | bytes 98312 | tf_op jit(solution)/shard_map/ppermute | solution.py:258
  88.1 3.7 %collective-permute-start.8 = (bf16[128,128]{1,0:T(8,128)(2,1)S(1)}, bf16[128,128]{1,0:T(8,128)(2,1)S(1)}, u32[]{:S(2)}, u32[]{:S(2)}) collective-permute-start(bf16[128,128]{1,0:T(8,128)(2,1)S(1)} %get-tuple-element.23), channel_id=1, source_target_pairs={{0,36},{4,32},{32,4},{36,0},{1,37},{5,33},{33,5},{37,1},{2,38},{6,... | collective-permute-start | bytes 98312 | tf_op jit(solution)/shard_map/ppermute | solution.py:258
  97.1 4.1 %collective-permute-start.20 = (bf16[144,128]{1,0:T(8,128)(2,1)S(1)}, bf16[144,128]{1,0:T(8,128)(2,1)S(1)}, u32[]{:S(2)}, u32[]{:S(2)}) collective-permute-start(bf16[144,128]{1,0:T(8,128)(2,1)S(1)} %get-tuple-element.29), channel_id=1, source_target_pairs={{0,4},{4,0},{32,36},{36,32},{1,5},{5,1},{33,37},{37,33},{2,6},{6,2... | collective-permute-start | bytes 110600 | tf_op jit(solution)/shard_map/ppermute | solution.py:258
  97.5 3.7 %collective-permute-start.21 = (bf16[144,128]{1,0:T(8,128)(2,1)S(1)}, bf16[144,128]{1,0:T(8,128)(2,1)S(1)}, u32[]{:S(2)}, u32[]{:S(2)}) collective-permute-start(bf16[144,128]{1,0:T(8,128)(2,1)S(1)} %get-tuple-element.30), channel_id=1, source_target_pairs={{0,32},{4,36},{32,0},{36,4},{1,33},{5,37},{33,1},{37,5},{2,34},{6,... | collective-permute-start | bytes 110600 | tf_op jit(solution)/shard_map/ppermute | solution.py:258
  98.4 3.6 %collective-permute-start.22 = (bf16[144,128]{1,0:T(8,128)(2,1)S(1)}, bf16[144,128]{1,0:T(8,128)(2,1)S(1)}, u32[]{:S(2)}, u32[]{:S(2)}) collective-permute-start(bf16[144,128]{1,0:T(8,128)(2,1)S(1)} %get-tuple-element.31), channel_id=1, source_target_pairs={{0,36},{4,32},{32,4},{36,0},{1,37},{5,33},{33,5},{37,1},{2,38},{6,... | collective-permute-start | bytes 110600 | tf_op jit(solution)/shard_map/ppermute | solution.py:258

commit v2 on v1

v2 whole, which is shorter than its diff:
```python
import math

import jax
import jax.numpy as jnp
from jax import lax
from jax.experimental import pallas as pl
from jax.experimental.pallas import tpu as pltpu
from jax.sharding import Mesh, PartitionSpec as P

HEAD = 128
TOK = 64
IMG = 2
WIDTH = 4096
PART = 1024
COLS = 512
ROWS = IMG * TOK
SCORE = math.log2(math.e) / math.sqrt(HEAD)
F32 = jnp.float32
BF16 = jnp.bfloat16
GROUP = ("zl", "core")


def params(limit):
    return pltpu.CompilerParams(vmem_limit_bytes=limit * 1024 * 1024)


def vmem(count):
    return [pl.BlockSpec(memory_space=pltpu.VMEM)] * count


def hbm(count):
    return [pl.BlockSpec(memory_space=pltpu.HBM)] * count


def anywhere(count):
    return [pl.BlockSpec(memory_space=pl.ANY)] * count


def smem():
    return pl.BlockSpec(memory_space=pltpu.SMEM)


def dot_t(a, b):
    return lax.dot_general(a, b, (((1,), (1,)), ((), ())), preferred_element_type=F32)


def head_slice(me, d):
    return pl.ds(pl.multiple_of((me ^ d) * HEAD, HEAD), HEAD)


def pack_kernel(me_ref, keys, values, o0, o1, o2, o3, sems):
    copies = []
    for d, out in enumerate((o0, o1, o2, o3)):
        cut = head_slice(me_ref[0], d)
        for i in range(IMG):
            for j, source in enumerate((keys, values)):
                copies.append(
                    pltpu.make_async_copy(
                        source.at[i, :, cut], out.at[i, j], sems.at[len(copies)]
                    )
                )
    for copy in copies:
        copy.start()
    for copy in copies:
        copy.wait()


def pack(me, keys, values):
    return pl.pallas_call(
        pack_kernel,
        out_shape=[jax.ShapeDtypeStruct((IMG, 2, TOK, HEAD), BF16)] * 4,
        in_specs=[smem()] + hbm(2),
        out_specs=vmem(4),
        scratch_shapes=[pltpu.SemaphoreType.DMA((16,))],
        compiler_params=params(56),
        name="pack_stale",
    )(me, keys, values)


def payload_kernel(x, shift, scale, out, sem):
    copy = pltpu.make_async_copy(x, out.at[:ROWS], sem)
    copy.start()
    out[ROWS:] = jnp.zeros((16, PART), BF16)
    out[ROWS : ROWS + IMG] = shift[...]
    out[ROWS + IMG : ROWS + 2 * IMG] = scale[...]
    copy.wait()


def payload(x, shift, scale):
    return pl.pallas_call(
        payload_kernel,
        out_shape=jax.ShapeDtypeStruct((ROWS + 16, PART), BF16),
        in_specs=hbm(1) + vmem(2),
        out_specs=pl.BlockSpec(memory_space=pltpu.VMEM),
        scratch_shapes=[pltpu.SemaphoreType.DMA],
        compiler_params=params(56),
        name="payload",
    )(x, shift, scale)


def tie(values, deps):
    count = len(values)
    return pl.pallas_call(
        lambda *refs: None,
        out_shape=[jax.ShapeDtypeStruct(v.shape, v.dtype) for v in values],
        in_specs=anywhere(count + len(deps)),
        out_specs=anywhere(count),
        input_output_aliases={i: i for i in range(count)},
        compiler_params=params(4),
        name="tie",
    )(*values, *deps)


def join(groups, deps=()):
    counts = [len(g) for g in groups]

    def kernel(*refs):
        ins, outs = refs[: sum(counts)], refs[sum(counts) + len(deps) :]
        at = 0
        for out, count in zip(outs, counts):
            row = 0
            for r in ins[at : at + count]:
                out[row : row + r.shape[0]] = r[...]
                row += r.shape[0]
            at += count

    def shape(group):
        rows = sum(v.shape[0] for v in group)
        return jax.ShapeDtypeStruct((rows,) + group[0].shape[1:], group[0].dtype)

    return pl.pallas_call(
        kernel,
        out_shape=[shape(g) for g in groups],
        in_specs=vmem(sum(counts)) + anywhere(len(deps)),
        out_specs=vmem(len(groups)),
        compiler_params=params(12),
        name="join",
    )(*[v for g in groups for v in g], *deps)


def stack_kernel(p0, p1, p2, p3, s0, s1):
    for d, p in enumerate((p0, p1, p2, p3)):
        s0[d] = p[0]
        s1[d] = p[1]


def stack_images(packed):
    return pl.pallas_call(
        stack_kernel,
        out_shape=[jax.ShapeDtypeStruct((4, 2, TOK, HEAD), BF16)] * IMG,
        in_specs=vmem(4),
        out_specs=vmem(2),
        compiler_params=params(8),
        name="stack_images",
    )(*packed)


def weight_copies(sources, buffers, sems):
    copies = []
    for n, (source, buffer) in enumerate(zip(sources, buffers)):
        for j in range(4):
            rows = pl.ds(j * PART, PART)
            copies.append(
                pltpu.make_async_copy(source.at[rows, :], buffer.at[j], sems.at[4 * n + j])
            )
    for copy in copies:
        copy.start()
    return copies


def project(xs, buffer, copies):
    acc = jnp.zeros((ROWS, COLS), F32)
    for j in range(4):
        copies[j].wait()
        acc += jnp.dot(xs[j], buffer[j], preferred_element_type=F32)
    return acc


def head_norm(v, gain):
    return v * lax.rsqrt(jnp.mean(v * v, axis=-1, keepdims=True) + 1e-06) * gain


def query_kernel(me_ref, x, wq, qg, q0, q1, q2, q3, qa, xs, buffer, sems):
    copies = weight_copies((wq,), (buffer,), sems)
    blocks = [x.at[j] for j in range(4)]
    total = sum(jnp.sum(b[:ROWS].astype(F32), axis=-1, keepdims=True) for b in blocks)
    mean = total / WIDTH
    square = jnp.zeros_like(mean)
    for b in blocks:
        centred = b[:ROWS].astype(F32) - mean
        square += jnp.sum(centred * centred, axis=-1, keepdims=True)
    rstd = lax.rsqrt(square / WIDTH + 1e-06)
    for j, b in enumerate(blocks):
        mods = b[ROWS : ROWS + 16].astype(F32)
        for i in range(IMG):
            rows = slice(i * TOK, (i + 1) * TOK)
            normed = (b[rows].astype(F32) - mean[rows]) * rstd[rows]
            out = normed * (1.0 + mods[IMG + i : IMG + i + 1, :]) + mods[i : i + 1, :]
            xs[j, rows, :] = out.astype(BF16)
    acc = project(xs, buffer, copies)
    for h in range(4):
        cut = slice(h * HEAD, (h + 1) * HEAD)
        qa[:, cut] = head_norm(acc[:, cut], qg[...]).astype(BF16)
    for d, q in enumerate((q0, q1, q2, q3)):
        q[...] = qa[:, head_slice(me_ref[0], d)]


def project_queries(me, x, wq, gain):
    return pl.pallas_call(
        query_kernel,
        out_shape=[jax.ShapeDtypeStruct((ROWS, HEAD), BF16)] * 4
        + [
            jax.ShapeDtypeStruct((ROWS, COLS), BF16),
            jax.ShapeDtypeStruct((4, ROWS, PART), BF16),
        ],
        in_specs=[smem()] + vmem(1) + hbm(1) + vmem(1),
        out_specs=vmem(6),
        scratch_shapes=[pltpu.VMEM((4, PART, COLS), BF16), pltpu.SemaphoreType.DMA((4,))],
        compiler_params=params(50),
        cost_estimate=pl.CostEstimate(
            flops=2 * ROWS * WIDTH * COLS, bytes_accessed=5 << 20, transcendentals=0
        ),
        name="queries",
    )(me, x, wq, gain)


def keys_kernel(xs, wk, kg, fk, buffer, sems):
    acc = project(xs, buffer, weight_copies((wk,), (buffer,), sems))
    for h in range(4):
        cut = slice(h * HEAD, (h + 1) * HEAD)
        fk[:, cut] = head_norm(acc[:, cut], kg[...]).astype(BF16)


def project_keys(xs, wk, gain):
    return pl.pallas_call(
        keys_kernel,
        out_shape=jax.ShapeDtypeStruct((ROWS, COLS), BF16),
        in_specs=vmem(1) + hbm(1) + vmem(1),
        out_specs=pl.BlockSpec(memory_space=pltpu.VMEM),
        scratch_shapes=[pltpu.VMEM((4, PART, COLS), BF16), pltpu.SemaphoreType.DMA((4,))],
        compiler_params=params(50),
        cost_estimate=pl.CostEstimate(
            flops=2 * ROWS * WIDTH * COLS, bytes_accessed=5 << 20, transcendentals=0
        ),
        name="keys",
    )(xs, wk, gain)


def near_kernel(xs, qa, fk, wv, _, fv, out, lse, buffer, sems):
    copies = weight_copies((wv,), (buffer,), sems)
    fv[...] = project(xs, buffer, copies).astype(BF16)
    lanes = lax.broadcasted_iota(jnp.int32, (TOK, HEAD), 1)
    for i in range(IMG):
        rows = slice(i * TOK, (i + 1) * TOK)
        levels = jnp.zeros((TOK, HEAD), F32)
        for h in range(4):
            cut = slice(h * HEAD, (h + 1) * HEAD)
            s = dot_t(qa[rows, cut], fk[rows, cut]) * SCORE
            top = jnp.max(s, axis=-1, keepdims=True)
            p = jnp.exp2(s - top)
            total = jnp.sum(p, axis=-1, keepdims=True)
            numer = jnp.dot(p.astype(BF16), fv[rows, cut], preferred_element_type=F32)
            out[rows, cut] = numer / total
            levels = jnp.where(lanes == h, top + jnp.log2(total), levels)
        lse[rows, :] = levels


def near(xs, qa, fk, wv, dep):
    return pl.pallas_call(
        near_kernel,
        out_shape=[
            jax.ShapeDtypeStruct((ROWS, COLS), BF16),
            jax.ShapeDtypeStruct((ROWS, COLS), F32),
            jax.ShapeDtypeStruct((ROWS, HEAD), F32),
        ],
        in_specs=vmem(3) + hbm(1) + anywhere(1),
        out_specs=vmem(3),
        scratch_shapes=[pltpu.VMEM((4, PART, COLS), BF16), pltpu.SemaphoreType.DMA((4,))],
        compiler_params=params(50),
        cost_estimate=pl.CostEstimate(
            flops=2 * ROWS * WIDTH * COLS, bytes_accessed=6 << 20, transcendentals=0
        ),
        name="near",
    )(xs, qa, fk, wv, dep)


def attend_part(q, stream, state, mask):
    entries = 16
    count = entries * TOK
    for c in range(stream.shape[0] // entries):
        span = slice(c * entries, (c + 1) * entries)
        k = stream[span, 0].reshape(count, HEAD)
        v = stream[span, 1].reshape(count, HEAD)
        s = dot_t(q, k) * SCORE
        if state is None:
            s = jnp.concatenate(
                [jnp.where(mask, -1e30, s[:, : 4 * TOK]), s[:, 4 * TOK :]], axis=1
            )
            top = jnp.max(s, axis=-1, keepdims=True)
            p = jnp.exp2(s - top)
            total = jnp.sum(p, axis=-1, keepdims=True)
            numer = jnp.dot(p.astype(BF16), v, preferred_element_type=F32)
        else:
            old, total, numer = state
            top = jnp.maximum(old, jnp.max(s, axis=-1, keepdims=True))
            factor = jnp.exp2(old - top)
            p = jnp.exp2(s - top)
            total = total * factor + jnp.sum(p, axis=-1, keepdims=True)
            numer = numer * factor + jnp.dot(p.astype(BF16), v, preferred_element_type=F32)
        state = (top, total, numer)
    return state


def image_queries(qs, i):
    return jnp.concatenate([r[i * TOK : (i + 1) * TOK] for r in qs], axis=0)


def attend_first_kernel(q0, q1, q2, q3, s0, u0, s1, u1, _, tops, totals, numers):
    shape = (4 * TOK, 4 * TOK)
    row_patch = lax.broadcasted_iota(jnp.int32, shape, 0) // TOK
    col_patch = lax.broadcasted_iota(jnp.int32, shape, 1) // TOK
    for i, streams in enumerate(((s0, u0), (s1, u1))):
        state = None
        for stream in streams:
            state = attend_part(
                image_queries((q0, q1, q2, q3), i), stream, state, row_patch == col_patch
            )
        top, total, numer = state
        tops[i] = jnp.broadcast_to(top, (4 * TOK, HEAD))
        totals[i] = jnp.broadcast_to(total, (4 * TOK, HEAD))
        numers[i] = numer


def attend_first(qs, streams, dep):
    return pl.pallas_call(
        attend_first_kernel,
        out_shape=[jax.ShapeDtypeStruct((IMG, 4 * TOK, HEAD), F32)] * 3,
        in_specs=vmem(8) + anywhere(1),
        out_specs=vmem(3),
        compiler_params=params(24),
        name="attend_first",
    )(*qs, *streams, dep)


def attend_last_kernel(q0, q1, q2, q3, s0, u0, s1, u1, tops, totals, numers, *outs):
    lse_rows = [jnp.zeros((1, HEAD), F32) for _ in range(4)]
    row = lax.broadcasted_iota(jnp.int32, (TOK, HEAD), 0)
    lane = lax.broadcasted_iota(jnp.int32, (TOK, HEAD), 1)
    for i, streams in enumerate(((s0, u0), (s1, u1))):
        state = (tops[i, :, :1], totals[i, :, :1], numers[i])
        for stream in streams:
            state = attend_part(image_queries((q0, q1, q2, q3), i), stream, state, None)
        top, total, numer = state
        out = (numer / total).astype(BF16)
        level = top + jnp.log2(total)
        for d in range(4):
            span = slice(d * TOK, (d + 1) * TOK)
            outs[d][i * TOK : (i + 1) * TOK, :] = out[span]
            lse_rows[d] += jnp.sum(
                jnp.where(lane == row + i * TOK, level[span], 0.0), axis=0, keepdims=True
            )
    sub = lax.broadcasted_iota(jnp.int32, (16, HEAD), 0)
    for d in range(4):
        high = lse_rows[d].astype(BF16).astype(F32)
        rest = lse_rows[d] - high
        middle = rest.astype(BF16).astype(F32)
        low = rest - middle
        tail = jnp.where(sub == 0, high, jnp.where(sub == 1, middle, jnp.where(sub == 2, low, 0.0)))
        outs[d][ROWS : ROWS + 16, :] = tail.astype(BF16)


def attend_last(qs, streams, state):
    return pl.pallas_call(
        attend_last_kernel,
        out_shape=[jax.ShapeDtypeStruct((ROWS + 16, HEAD), BF16)] * 4,
        in_specs=vmem(11),
        out_specs=vmem(4),
        compiler_params=params(24),
        name="attend_last",
    )(*qs, *streams, *state)


def combine_kernel(me_ref, r0, r1, r2, r3, near_out, near_lse, att):
    me = me_ref[0]
    row = lax.broadcasted_iota(jnp.int32, (ROWS, HEAD), 0)
    lane = lax.broadcasted_iota(jnp.int32, (ROWS, HEAD), 1)
    for d, r in enumerate((r0, r1, r2, r3)):
        cut = head_slice(me, d)
        tail = r[ROWS : ROWS + 16, :].astype(F32)
        level = tail[0:1] + tail[1:2] + tail[2:3]
        far_lse = jnp.sum(jnp.where(lane == row, level, 0.0), axis=1, keepdims=True)
        own_lse = jnp.sum(
            jnp.where(lane == (me ^ d), near_lse[...], 0.0), axis=1, keepdims=True
        )
        top = jnp.maximum(far_lse, own_lse)
        far_weight = jnp.exp2(far_lse - top)
        own_weight = jnp.exp2(own_lse - top)
        out = r[:ROWS, :].astype(F32) * far_weight + near_out[:, cut] * own_weight
        att[:, cut] = (out / (far_weight + own_weight)).astype(BF16)


def combine(me, rs, near_out, near_lse):
    return pl.pallas_call(
        combine_kernel,
        out_shape=jax.ShapeDtypeStruct((ROWS, COLS), BF16),
        in_specs=[smem()] + vmem(6),
        out_specs=pl.BlockSpec(memory_space=pltpu.VMEM),
        compiler_params=params(8),
        name="combine",
    )(me, *rs, near_out, near_lse)


def group_swap(parts):
    return [parts[0]] + [
        lax.ppermute(parts[d], GROUP, [(i, i ^ d) for i in range(4)]) for d in (1, 2, 3)
    ]


def swap(value, axis, step):
    flips = ((1, 3), (3, 1))[step]
    if axis == "zh":
        names, far, near_ = ("core", axis), 1, 4
    else:
        names, far, near_ = (axis, "core"), 2, 1
    perm = [
        (a * far + c * near_, (a ^ flips[c]) * far + c * near_)
        for a in range(4)
        for c in range(2)
    ]
    return lax.ppermute(value, names, perm)


def on_device(activations, mod_shift, mod_scale, w_query, w_key, w_value,
              query_gain, key_gain, stale_keys, stale_values):
    me = lax.axis_index("zl") * 2 + lax.axis_index("core")
    me1 = me.reshape(1).astype(jnp.int32)

    x0 = payload(activations.reshape(ROWS, PART), mod_shift, mod_scale)
    xall = lax.all_gather(x0, "zh")

    parts = group_swap(pack(me1, stale_keys, stale_values))
    s0, s1 = stack_images(parts)
    s0, s1 = join([(s0, swap(s0, "x", 0)), (s1, swap(s1, "y", 0))])
    s0, s1 = join([(s0, swap(s0, "x", 1)), (s1, swap(s1, "y", 1))])

    u0, u1 = swap(s0, "y", 0), swap(s1, "x", 0)
    v0, v1 = swap(s0, "y", 1), swap(s1, "x", 1)
    w0, w1 = swap(u0, "y", 1), swap(u1, "x", 1)

    q0, q1, q2, q3, qa, xs = project_queries(me1, xall, w_query, query_gain.reshape(1, HEAD))
    qs = group_swap([q0, q1, q2, q3])
    fk = project_keys(xs, w_key, key_gain.reshape(1, HEAD))
    state = attend_first(qs, (s0, u0, s1, u1), fk)
    outs = attend_last(qs, (v0, w0, v1, w1), state)
    fv, near_out, near_lse = near(xs, qa, fk, w_value, outs[0])
    outs = group_swap(outs)
    att = combine(me1, outs, near_out, near_lse)
    shape = (IMG, TOK, COLS)
    return att.reshape(shape), fk.reshape(shape), fv.reshape(shape)


def solution(mesh):
    split = Mesh(mesh.devices.reshape(4, 2, 4, 2, 4), ("x", "zl", "y", "core", "zh"))
    patch = ("x", "zl", "y", "core")
    rows = P(None, patch, "zh")
    cols = P(None, "zh")
    return jax.shard_map(
        on_device,
        mesh=split,
        in_specs=(rows, cols, cols, cols, cols, cols, P(), P(), rows, rows),
        out_specs=(rows, rows, rows),
        check_vma=False,
    )
```

time: 103 us -> 90.9 us (0.88)
  starting transfers between devices: 40.8 us -> 24.6 us
  between operations: 0.87 us -> 14.2 us
  waiting for transfers between devices: 36.8 us -> 27.1 us
  Pallas kernels: 14.9 us -> 21 us
  local copies, waits for them, and re-layouts: 9.51 us -> 3.67 us
    ppermute x14 -> x10, waiting for transfers between devices: 30.5 us -> 16.9 us  [swap(): return lax.ppermute(value, names, perm)]
    ppermute x14 -> x10, starting transfers between devices: 20.9 us -> 8.88 us  [swap(): return lax.ppermute(value, names, perm)]
    unnamed x30 -> x12, local copies, waits for them, and re-layouts: 8.92 us -> 3.67 us
    ppermute x9, starting transfers between devices: 19.9 us -> 15.7 us  [group_swap(): lax.ppermute(parts[d], GROUP, [(i, i ^ d) for i in range(4)])]
    all_gather x0 -> x1, waiting for transfers between devices: none -> 3.71 us  [on_device(): xall = lax.all_gather(x0, 'zh')]
    pallas_call x2 -> x8, Pallas kernels: 12.1 us -> 14.3 us  [the longest x1 3.78 us: attend_last(): pl.pallas_call(attend_last_kernel, out_shape=[jax.ShapeDtypeStruct((ROWS...]
    pallas_call x1, Pallas kernels: 1.86 us -> 4.05 us  [near(): pl.pallas_call(near_kernel, out_shape=[jax.ShapeDtypeStruct((ROWS, COLS),...]
    pallas_call x1, Pallas kernels: 0.05 us -> 1.72 us  [pack(): pl.pallas_call(pack_kernel, out_shape=[jax.ShapeDtypeStruct((IMG, 2, TOK,...]
  transfers between devices with their start and end apart: 23 -> 20, of which waited for: 14 -> 11; matrix products, arithmetic and copies ran while one was open for 1% -> 0% of each run, Pallas kernels for 9% -> 15%
where the time goes in v2:
time: 90.9 us; the launch traced here: 90.6 us
  waiting for transfers between devices  27.1 us (30%)
  starting transfers between devices  24.6 us (27%)
  Pallas kernels  21 us (23%)
  between operations  14.2 us (16%)
  local copies, waits for them, and re-layouts  3.67 us (4%)
    ppermute x10, waiting for transfers between devices, swap(): return lax.ppermute(value, names, perm)  16.9 us
    ppermute x9, starting transfers between devices, group_swap(): lax.ppermute(parts[d], GROUP, [(i, i ^ d) for i in range(4)])  15.7 us
    ppermute x10, starting transfers between devices, swap(): return lax.ppermute(value, names, perm)  8.88 us
    ppermute x9, waiting for transfers between devices, group_swap(): lax.ppermute(parts[d], GROUP, [(i, i ^ d) for i in range(4)])  6.38 us
    pallas_call x1, Pallas kernels, near(): pl.pallas_call(near_kernel, out_shape=[jax.ShapeDtypeStruct((ROWS, COLS),...  4.05 us
    pallas_call x1, Pallas kernels, attend_last(): pl.pallas_call(attend_last_kernel, out_shape=[jax.ShapeDtypeStruct((ROWS...  3.78 us
    all_gather x1, waiting for transfers between devices, on_device(): xall = lax.all_gather(x0, 'zh')  3.71 us
    unnamed x12, local copies, waits for them, and re-layouts  3.67 us
  transfers between devices with their start and end apart: 20, of which 11 were waited for; matrix products, arithmetic and copies ran while one was open for 0% of the time, Pallas kernels for 15%

profile of v2, /device:TPU:1, one launch (start us, length us, event | category | flops | bytes accessed | tf_op | source)
XLA Modules:
  0.0 90.6 jit_solution(1401469105027095029)
XLA Ops:
  7.2 0.0 all-gather.3.cloned.1.call-start
  7.2 0.0 copy-start.5
  7.2 2.4 %payload.1 = bf16[144,1024]{1,0:T(8,128)(2,1)} custom-call(bf16[128,1024]{1,0:T(8,128)(2,1)} %bitcast.12, bf16[2,1024]{1,0:T(2,128)(2,1)} %shift.1, bf16[2,1024]{1,0:T(2,128)(2,1)} %scale.1), custom_call_target="tpu_custom_call" | custom-call | tf_op jit(solution)/shard_map/payload/pallas_call | solution.py:90
  9.6 0.0 all-gather.3.cloned.1.call-update
  9.7 1.7 %pack_stale.1 = (bf16[2,2,64,128]{3,2,1,0:T(8,128)(2,1)}, bf16[2,2,64,128]{3,2,1,0:T(8,128)(2,1)}, bf16[2,2,64,128]{3,2,1,0:T(8,128)(2,1)}, bf16[2,2,64,128]{3,2,1,0:T(8,128)(2,1)}) custom-call(s32[1]{0:T(128)} %bitcast.me_ref, bf16[2,64,512]{2,1,0:T(8,128)(2,1)} %keys.2, bf16[2,64,512]{2,1,0:T(8,128)(2,1)} %values.1), custom_call_target="tpu_custom_call" | custom-call | tf_op jit(solution)/shard_map/pack_stale/pallas_call | solution.py:69
  11.4 3.3 %collective-permute-start.3 = (bf16[2,2,64,128]{3,2,1,0:T(8,128)(2,1)}, bf16[2,2,64,128]{3,2,1,0:T(8,128)(2,1)S(1)}, u32[]{:S(2)}, u32[]{:S(2)}) collective-permute-start(bf16[2,2,64,128]{3,2,1,0:T(8,128)(2,1)} %get-tuple-element.34), channel_id=1, source_target_pairs={{0,4},{4,0},{32,36},{36,32},{1,5},{5,1},{33,37},{37,33},{2,6},{6,2... | collective-permute-start | bytes 196616 | tf_op jit(solution)/shard_map/ppermute | solution.py:415
  14.7 0.0 collective-permute-start.4
  14.7 1.7 %collective-permute-start.5 = (bf16[2,2,64,128]{3,2,1,0:T(8,128)(2,1)}, bf16[2,2,64,128]{3,2,1,0:T(8,128)(2,1)S(1)}, u32[]{:S(2)}, u32[]{:S(2)}) collective-permute-start(bf16[2,2,64,128]{3,2,1,0:T(8,128)(2,1)} %get-tuple-element.36), channel_id=1, source_target_pairs={{0,36},{4,32},{32,4},{36,0},{1,37},{5,33},{33,5},{37,1},{2,38},{6,... | collective-permute-start | bytes 196616 | tf_op jit(solution)/shard_map/ppermute | solution.py:415
  16.4 0.0 collective-permute-done.3.p1
  16.4 2.1 %collective-permute-done.4.p2 = bf16[2,2,64,128]{3,2,1,0:T(8,128)(2,1)S(1)} collective-permute-done((bf16[2,2,64,128]{3,2,1,0:T(8,128)(2,1)}, bf16[2,2,64,128]{3,2,1,0:T(8,128)(2,1)S(1)}, u32[]{:S(2)}, u32[]{:S(2)}) %collective-permute-start.4) | collective-permute-done | bytes 65568 | tf_op jit(solution)/shard_map/ppermute | solution.py:415
  18.6 1.6 %collective-permute-done.5.p3 = bf16[2,2,64,128]{3,2,1,0:T(8,128)(2,1)S(1)} collective-permute-done((bf16[2,2,64,128]{3,2,1,0:T(8,128)(2,1)}, bf16[2,2,64,128]{3,2,1,0:T(8,128)(2,1)S(1)}, u32[]{:S(2)}, u32[]{:S(2)}) %collective-permute-start.5) | collective-permute-done | bytes 65568 | tf_op jit(solution)/shard_map/ppermute | solution.py:415
  20.2 0.0 copy-start.3
  20.2 0.8 copy-done.3
  21.0 1.3 %collective-permute-start.6 = (bf16[4,2,64,128]{3,2,1,0:T(8,128)(2,1)S(1)}, bf16[4,2,64,128]{3,2,1,0:T(8,128)(2,1)S(1)}, u32[]{:S(2)}, u32[]{:S(2)}) collective-permute-start(bf16[4,2,64,128]{3,2,1,0:T(8,128)(2,1)S(1)} %get-tuple-element.37.refs_0_), channel_id=1, source_target_pairs={{0,64},{4,196},{64,0},{68,132},{128,192},{132,68},{192,128},{196,4... | collective-permute-start | bytes 393224 | tf_op jit(solution)/shard_map/ppermute | solution.py:430
  22.3 2.7 %collective-permute-start.7 = (bf16[4,2,64,128]{3,2,1,0:T(8,128)(2,1)S(1)}, bf16[4,2,64,128]{3,2,1,0:T(8,128)(2,1)S(1)}, u32[]{:S(2)}, u32[]{:S(2)}) collective-permute-start(bf16[4,2,64,128]{3,2,1,0:T(8,128)(2,1)S(1)} %get-tuple-element.38.refs_2_), channel_id=1, source_target_pairs={{0,8},{4,28},{8,0},{12,20},{16,24},{20,12},{24,16},{28,4},{1,9},{5... | collective-permute-start | bytes 393224 | tf_op jit(solution)/shard_map/ppermute | solution.py:430
  25.1 1.1 %collective-permute-done.6.refs_1_ = bf16[4,2,64,128]{3,2,1,0:T(8,128)(2,1)S(1)} collective-permute-done((bf16[4,2,64,128]{3,2,1,0:T(8,128)(2,1)S(1)}, bf16[4,2,64,128]{3,2,1,0:T(8,128)(2,1)S(1)}, u32[]{:S(2)}, u32[]{:S(2)}) %collective-permute-start.6) | collective-permute-done | bytes 131104 | tf_op jit(solution)/shard_map/ppermute | solution.py:430
  26.1 1.3 %collective-permute-done.7.refs_3_ = bf16[4,2,64,128]{3,2,1,0:T(8,128)(2,1)S(1)} collective-permute-done((bf16[4,2,64,128]{3,2,1,0:T(8,128)(2,1)S(1)}, bf16[4,2,64,128]{3,2,1,0:T(8,128)(2,1)S(1)}, u32[]{:S(2)}, u32[]{:S(2)}) %collective-permute-start.7) | collective-permute-done | bytes 131104 | tf_op jit(solution)/shard_map/ppermute | solution.py:430
  27.5 0.1 collective-permute-start.8
  27.6 0.3 collective-permute-start.9
  27.8 5.4 %collective-permute-done.8.refs_1_ = bf16[8,2,64,128]{3,2,1,0:T(8,128)(2,1)S(1)} collective-permute-done((bf16[8,2,64,128]{3,2,1,0:T(8,128)(2,1)S(1)}, bf16[8,2,64,128]{3,2,1,0:T(8,128)(2,1)S(1)}, u32[]{:S(2)}, u32[]{:S(2)}) %collective-permute-start.8) | collective-permute-done | bytes 262176 | tf_op jit(solution)/shard_map/ppermute | solution.py:430
  33.2 0.1 collective-permute-done.9.refs_3_
  33.3 0.1 join.3
  33.3 2.8 %collective-permute-start.11 = (bf16[16,2,64,128]{3,2,1,0:T(8,128)(2,1)S(1)}, bf16[16,2,64,128]{3,2,1,0:T(8,128)(2,1)S(1)}, u32[]{:S(2)}, u32[]{:S(2)}) collective-permute-start(bf16[16,2,64,128]{3,2,1,0:T(8,128)(2,1)S(1)} %get-tuple-element.41.s0), channel_id=1, source_target_pairs={{0,8},{4,28},{8,0},{12,20},{16,24},{20,12},{24,16},{28,4},{1,9},{5... | collective-permute-start | bytes 1572872 | tf_op jit(solution)/shard_map/ppermute | solution.py:430
  36.1 0.7 collective-permute-start.14
  36.8 0.0 collective-permute-start.10
  36.8 0.7 collective-permute-start.13
  37.5 6.5 %collective-permute-done.11.u0 = bf16[16,2,64,128]{3,2,1,0:T(8,128)(2,1)S(1)} collective-permute-done((bf16[16,2,64,128]{3,2,1,0:T(8,128)(2,1)S(1)}, bf16[16,2,64,128]{3,2,1,0:T(8,128)(2,1)S(1)}, u32[]{:S(2)}, u32[]{:S(2)}) %collective-permute-start.11) | collective-permute-done | bytes 524320 | tf_op jit(solution)/shard_map/ppermute | solution.py:430
  44.0 0.0 collective-permute-start.12
  44.0 2.6 %collective-permute-done.14.u1 = bf16[16,2,64,128]{3,2,1,0:T(8,128)(2,1)S(1)} collective-permute-done((bf16[16,2,64,128]{3,2,1,0:T(8,128)(2,1)S(1)}, bf16[16,2,64,128]{3,2,1,0:T(8,128)(2,1)S(1)}, u32[]{:S(2)}, u32[]{:S(2)}) %collective-permute-start.14) | collective-permute-done | bytes 524320 | tf_op jit(solution)/shard_map/ppermute | solution.py:430
  46.6 0.4 collective-permute-start.15
  47.0 3.7 %all-gather.3.cloned.1.call-done = bf16[576,1024]{1,0:T(8,128)(2,1)} async-done(((bf16[144,1024]{1,0:T(8,128)(2,1)}), bf16[576,1024]{1,0:T(8,128)(2,1)}) %all-gather.3.cloned.1.call-update) | async-done | bytes 1179664 | tf_op jit(solution)/shard_map/all_gather | solution.py:439
  50.7 0.0 copy-start.2
  50.7 1.3 %copy-done.2 = bf16[576,1024]{1,0:T(8,128)(2,1)S(1)} copy-done((bf16[576,1024]{1,0:T(8,128)(2,1)S(1)}, bf16[576,1024]{1,0:T(8,128)(2,1)}, u32[]{:S(2)}) %copy-start.2) | copy-done | bytes 1179672
  51.9 0.0 copy-start.4
  52.0 0.7 copy-done.4
  52.6 2.7 %queries.1 = (bf16[128,128]{1,0:T(8,128)(2,1)S(1)}, bf16[128,128]{1,0:T(8,128)(2,1)S(1)}, bf16[128,128]{1,0:T(8,128)(2,1)S(1)}, bf16[128,128]{1,0:T(8,128)(2,1)S...) custom-call(s32[1]{0:T(128)} %bitcast.me_ref, bf16[4,144,1024]{2,1,0:T(8,128)(2,1)S(1)} %bitcast.9, ...), custom_call_target="tpu_custom_call" | custom-call | flops 536870912 | bytes 5242880 | tf_op jit(solution)/shard_map/queries/pallas_call | solution.py:209
  55.3 5.1 %collective-permute-start = (bf16[128,128]{1,0:T(8,128)(2,1)S(1)}, bf16[128,128]{1,0:T(8,128)(2,1)S(1)}, u32[]{:S(2)}, u32[]{:S(2)}) collective-permute-start(bf16[128,128]{1,0:T(8,128)(2,1)S(1)} %get-tuple-element.30), channel_id=1, source_target_pairs={{0,4},{4,0},{32,36},{36,32},{1,5},{5,1},{33,37},{37,33},{2,6},{6,2... | collective-permute-start | bytes 98312 | tf_op jit(solution)/shard_map/ppermute | solution.py:415
  60.4 0.9 collective-permute-done.q1
  61.2 1.0 %collective-permute-start.1 = (bf16[128,128]{1,0:T(8,128)(2,1)S(1)}, bf16[128,128]{1,0:T(8,128)(2,1)S(1)}, u32[]{:S(2)}, u32[]{:S(2)}) collective-permute-start(bf16[128,128]{1,0:T(8,128)(2,1)S(1)} %get-tuple-element.31), channel_id=1, source_target_pairs={{0,32},{4,36},{32,0},{36,4},{1,33},{5,37},{33,1},{37,5},{2,34},{6,... | collective-permute-start | bytes 98312 | tf_op jit(solution)/shard_map/ppermute | solution.py:415
  62.2 1.8 %collective-permute-done.1.q2 = bf16[128,128]{1,0:T(8,128)(2,1)S(1)} collective-permute-done((bf16[128,128]{1,0:T(8,128)(2,1)S(1)}, bf16[128,128]{1,0:T(8,128)(2,1)S(1)}, u32[]{:S(2)}, u32[]{:S(2)}) %collective-permute-start.1) | collective-permute-done | bytes 32800 | tf_op jit(solution)/shard_map/ppermute | solution.py:415
  64.0 2.4 %collective-permute-start.2 = (bf16[128,128]{1,0:T(8,128)(2,1)S(1)}, bf16[128,128]{1,0:T(8,128)(2,1)S(1)}, u32[]{:S(2)}, u32[]{:S(2)}) collective-permute-start(bf16[128,128]{1,0:T(8,128)(2,1)S(1)} %get-tuple-element.32), channel_id=1, source_target_pairs={{0,36},{4,32},{32,4},{36,0},{1,37},{5,33},{33,5},{37,1},{2,38},{6,... | collective-permute-start | bytes 98312 | tf_op jit(solution)/shard_map/ppermute | solution.py:415
  66.4 0.0 copy-done.5
  66.4 3.3 %keys.3._.fk = bf16[128,512]{1,0:T(8,128)(2,1)} custom-call(bf16[4,128,1024]{2,1,0:T(8,128)(2,1)S(1)} %get-tuple-element.43.xs, bf16[4096,512]{1,0:T(8,128)(2,1)} %wk.1, f32[1,128]{1,0:T(1,128)S(1)} %bitcast.11), custom_call_target="tpu_custom_call" | custom-call | flops 536870912 | bytes 5242880 | tf_op jit(solution)/shard_map/keys/pallas_call | solution.py:235
  69.7 0.0 collective-permute-done.2.q3
  69.7 0.0 copy-start
  69.7 0.9 copy-done
  70.6 0.0 copy-start.1
  70.6 2.1 %attend_first.1 = (f32[2,256,128]{2,1,0:T(8,128)S(1)}, f32[2,256,128]{2,1,0:T(8,128)S(1)}, f32[2,256,128]{2,1,0:T(8,128)S(1)}) custom-call(bf16[128,128]{1,0:T(8,128)(2,1)S(1)} %get-tuple-element.29.q0, bf16[128,128]{1,0:T(8,128)(2,1)S(1)} %collective-permute-done.q1, bf16[128,128]{1,0:T(8,128)(2,1)S(1)} %collective-permute-done.1.q2, ...), custom_call_target="tpu_custom_call" | custom-call | tf_op jit(solution)/shard_map/attend_first/pallas_call | solution.py:335
  72.7 0.0 collective-permute-done.10.s0
  72.7 0.0 collective-permute-done.13.s1
  72.7 0.0 collective-permute-done.12.u0
  72.7 0.0 collective-permute-done.15.u1
  72.7 3.8 %attend_last.1 = (bf16[144,128]{1,0:T(8,128)(2,1)S(1)}, bf16[144,128]{1,0:T(8,128)(2,1)S(1)}, bf16[144,128]{1,0:T(8,128)(2,1)S(1)}, bf16[144,128]{1,0:T(8,128)(2,1)S(1)}) custom-call(bf16[128,128]{1,0:T(8,128)(2,1)S(1)} %get-tuple-element.29.q0, bf16[128,128]{1,0:T(8,128)(2,1)S(1)} %collective-permute-done.q1, ...), custom_call_target="tpu_custom_call" | custom-call | tf_op jit(solution)/shard_map/attend_last/pallas_call | solution.py:373
  76.5 0.1 collective-permute-start.16
  76.6 0.6 collective-permute-start.17
  77.2 1.6 %collective-permute-start.18 = (bf16[144,128]{1,0:T(8,128)(2,1)S(1)}, bf16[144,128]{1,0:T(8,128)(2,1)S(1)}, u32[]{:S(2)}, u32[]{:S(2)}) collective-permute-start(bf16[144,128]{1,0:T(8,128)(2,1)S(1)} %get-tuple-element.50), channel_id=1, source_target_pairs={{0,36},{4,32},{32,4},{36,0},{1,37},{5,33},{33,5},{37,1},{2,38},{6,... | collective-permute-start | bytes 110600 | tf_op jit(solution)/shard_map/ppermute | solution.py:415
  78.7 0.0 copy-done.1
  78.7 4.1 %near.1 = (bf16[128,512]{1,0:T(8,128)(2,1)}, f32[128,512]{1,0:T(8,128)S(1)}, f32[128,128]{1,0:T(8,128)S(1)}) custom-call(bf16[4,128,1024]{2,1,0:T(8,128)(2,1)S(1)} %get-tuple-element.43.xs, bf16[128,512]{1,0:T(8,128)(2,1)S(1)} %get-tuple-element.51.qa, bf16[128,512]{1,0:T(8,128)(2,1)S(1)} %copy-done.1, bf16[4096,512]{1,0:T(8,128)(2,1)} %wv.1, ...), custom_call_target="tpu_custom_call" | custom-call | flops 536870912 | bytes 6291456 | tf_op jit(solution)/shard_map/near/pallas_call | solution.py:269
  82.8 0.0 collective-permute-done.16.r1
  82.8 0.0 collective-permute-done.17.r2
  82.8 0.0 collective-permute-done.18.r3
  82.8 0.9 combine.1
  (2 shorter events, 0.1 us)
Async XLA Ops:
  7.2 43.5 %all-gather.3.cloned.1.call-start = ((), (), s32[]{:S(2)}) async-start(), calls=%async_computation | async-start | bytes 1474560 | tf_op jit(solution)/shard_map/all_gather | solution.py:439
  7.2 59.2 %copy-start.5 = (f32[128]{0:T(128)S(1)}, f32[128]{0:T(128)}, u32[]{:S(2)}) copy-start(f32[128]{0:T(128)} %param.17) | copy-start | bytes 1540
  11.4 5.1 %collective-permute-start.3 = (bf16[2,2,64,128]{3,2,1,0:T(8,128)(2,1)}, bf16[2,2,64,128]{3,2,1,0:T(8,128)(2,1)S(1)}, u32[]{:S(2)}, u32[]{:S(2)}) collective-permute-start(bf16[2,2,64,128]{3,2,1,0:T(8,128)(2,1)} %get-tuple-element.34), channel_id=1, source_target_pairs={{0,4},{4,0},{32,36},{36,32},{1,5},{5,1},{33,37},{37,33},{2,6},{6,2... | collective-permute-start | bytes 196616 | tf_op jit(solution)/shard_map/ppermute | solution.py:415
  14.7 3.9 %collective-permute-start.4 = (bf16[2,2,64,128]{3,2,1,0:T(8,128)(2,1)}, bf16[2,2,64,128]{3,2,1,0:T(8,128)(2,1)S(1)}, u32[]{:S(2)}, u32[]{:S(2)}) collective-permute-start(bf16[2,2,64,128]{3,2,1,0:T(8,128)(2,1)} %get-tuple-element.35), channel_id=1, source_target_pairs={{0,32},{4,36},{32,0},{36,4},{1,33},{5,37},{33,1},{37,5},{2,34},{6,... | collective-permute-start | bytes 196616 | tf_op jit(solution)/shard_map/ppermute | solution.py:415
  14.7 5.4 %collective-permute-start.5 = (bf16[2,2,64,128]{3,2,1,0:T(8,128)(2,1)}, bf16[2,2,64,128]{3,2,1,0:T(8,128)(2,1)S(1)}, u32[]{:S(2)}, u32[]{:S(2)}) collective-permute-start(bf16[2,2,64,128]{3,2,1,0:T(8,128)(2,1)} %get-tuple-element.36), channel_id=1, source_target_pairs={{0,36},{4,32},{32,4},{36,0},{1,37},{5,33},{33,5},{37,1},{2,38},{6,... | collective-permute-start | bytes 196616 | tf_op jit(solution)/shard_map/ppermute | solution.py:415
  20.2 0.8 copy-start.3
  21.0 5.1 %collective-permute-start.6 = (bf16[4,2,64,128]{3,2,1,0:T(8,128)(2,1)S(1)}, bf16[4,2,64,128]{3,2,1,0:T(8,128)(2,1)S(1)}, u32[]{:S(2)}, u32[]{:S(2)}) collective-permute-start(bf16[4,2,64,128]{3,2,1,0:T(8,128)(2,1)S(1)} %get-tuple-element.37.refs_0_), channel_id=1, source_target_pairs={{0,64},{4,196},{64,0},{68,132},{128,192},{132,68},{192,128},{196,4... | collective-permute-start | bytes 393224 | tf_op jit(solution)/shard_map/ppermute | solution.py:430
  22.3 5.1 %collective-permute-start.7 = (bf16[4,2,64,128]{3,2,1,0:T(8,128)(2,1)S(1)}, bf16[4,2,64,128]{3,2,1,0:T(8,128)(2,1)S(1)}, u32[]{:S(2)}, u32[]{:S(2)}) collective-permute-start(bf16[4,2,64,128]{3,2,1,0:T(8,128)(2,1)S(1)} %get-tuple-element.38.refs_2_), channel_id=1, source_target_pairs={{0,8},{4,28},{8,0},{12,20},{16,24},{20,12},{24,16},{28,4},{1,9},{5... | collective-permute-start | bytes 393224 | tf_op jit(solution)/shard_map/ppermute | solution.py:430
  27.5 5.7 %collective-permute-start.8 = (bf16[8,2,64,128]{3,2,1,0:T(8,128)(2,1)S(1)}, bf16[8,2,64,128]{3,2,1,0:T(8,128)(2,1)S(1)}, u32[]{:S(2)}, u32[]{:S(2)}) collective-permute-start(bf16[8,2,64,128]{3,2,1,0:T(8,128)(2,1)S(1)} %get-tuple-element.39.refs_0_), channel_id=1, source_target_pairs={{0,192},{4,68},{64,128},{68,4},{128,64},{132,196},{192,0},{196,132... | collective-permute-start | bytes 786440 | tf_op jit(solution)/shard_map/ppermute | solution.py:430
  27.6 5.7 %collective-permute-start.9 = (bf16[8,2,64,128]{3,2,1,0:T(8,128)(2,1)S(1)}, bf16[8,2,64,128]{3,2,1,0:T(8,128)(2,1)S(1)}, u32[]{:S(2)}, u32[]{:S(2)}) collective-permute-start(bf16[8,2,64,128]{3,2,1,0:T(8,128)(2,1)S(1)} %get-tuple-element.40.refs_2_), channel_id=1, source_target_pairs={{0,24},{4,12},{8,16},{12,4},{16,8},{20,28},{24,0},{28,20},{1,25},{... | collective-permute-start | bytes 786440 | tf_op jit(solution)/shard_map/ppermute | solution.py:430
  33.3 10.7 %collective-permute-start.11 = (bf16[16,2,64,128]{3,2,1,0:T(8,128)(2,1)S(1)}, bf16[16,2,64,128]{3,2,1,0:T(8,128)(2,1)S(1)}, u32[]{:S(2)}, u32[]{:S(2)}) collective-permute-start(bf16[16,2,64,128]{3,2,1,0:T(8,128)(2,1)S(1)} %get-tuple-element.41.s0), channel_id=1, source_target_pairs={{0,8},{4,28},{8,0},{12,20},{16,24},{20,12},{24,16},{28,4},{1,9},{5... | collective-permute-start | bytes 1572872 | tf_op jit(solution)/shard_map/ppermute | solution.py:430
  36.1 10.5 %collective-permute-start.14 = (bf16[16,2,64,128]{3,2,1,0:T(8,128)(2,1)S(1)}, bf16[16,2,64,128]{3,2,1,0:T(8,128)(2,1)S(1)}, u32[]{:S(2)}, u32[]{:S(2)}) collective-permute-start(bf16[16,2,64,128]{3,2,1,0:T(8,128)(2,1)S(1)} %get-tuple-element.42.s1), channel_id=1, source_target_pairs={{0,64},{4,196},{64,0},{68,132},{128,192},{132,68},{192,128},{196,4... | collective-permute-start | bytes 1572872 | tf_op jit(solution)/shard_map/ppermute | solution.py:430
  36.8 35.9 %collective-permute-start.10 = (bf16[16,2,64,128]{3,2,1,0:T(8,128)(2,1)S(1)}, bf16[16,2,64,128]{3,2,1,0:T(8,128)(2,1)S(1)}, u32[]{:S(2)}, u32[]{:S(2)}) collective-permute-start(bf16[16,2,64,128]{3,2,1,0:T(8,128)(2,1)S(1)} %get-tuple-element.41.s0), channel_id=1, source_target_pairs={{0,24},{4,12},{8,16},{12,4},{16,8},{20,28},{24,0},{28,20},{1,25},{... | collective-permute-start | bytes 1572872 | tf_op jit(solution)/shard_map/ppermute | solution.py:430
  36.8 35.9 %collective-permute-start.13 = (bf16[16,2,64,128]{3,2,1,0:T(8,128)(2,1)S(1)}, bf16[16,2,64,128]{3,2,1,0:T(8,128)(2,1)S(1)}, u32[]{:S(2)}, u32[]{:S(2)}) collective-permute-start(bf16[16,2,64,128]{3,2,1,0:T(8,128)(2,1)S(1)} %get-tuple-element.42.s1), channel_id=1, source_target_pairs={{0,192},{4,68},{64,128},{68,4},{128,64},{132,196},{192,0},{196,132... | collective-permute-start | bytes 1572872 | tf_op jit(solution)/shard_map/ppermute | solution.py:430
  44.0 28.7 %collective-permute-start.12 = (bf16[16,2,64,128]{3,2,1,0:T(8,128)(2,1)S(1)}, bf16[16,2,64,128]{3,2,1,0:T(8,128)(2,1)}, u32[]{:S(2)}, u32[]{:S(2)}) collective-permute-start(bf16[16,2,64,128]{3,2,1,0:T(8,128)(2,1)S(1)} %collective-permute-done.11.u0), channel_id=1, source_target_pairs={{0,24},{4,12},{8,16},{12,4},{16,8},{20,28},{24,0},{28,20},{1,25},{... | collective-permute-start | bytes 1572872 | tf_op jit(solution)/shard_map/ppermute | solution.py:430
  46.6 26.1 %collective-permute-start.15 = (bf16[16,2,64,128]{3,2,1,0:T(8,128)(2,1)S(1)}, bf16[16,2,64,128]{3,2,1,0:T(8,128)(2,1)}, u32[]{:S(2)}, u32[]{:S(2)}) collective-permute-start(bf16[16,2,64,128]{3,2,1,0:T(8,128)(2,1)S(1)} %collective-permute-done.14.u1), channel_id=1, source_target_pairs={{0,192},{4,68},{64,128},{68,4},{128,64},{132,196},{192,0},{196,132... | collective-permute-start | bytes 1572872 | tf_op jit(solution)/shard_map/ppermute | solution.py:430
  50.7 1.3 %copy-start.2 = (bf16[576,1024]{1,0:T(8,128)(2,1)S(1)}, bf16[576,1024]{1,0:T(8,128)(2,1)}, u32[]{:S(2)}) copy-start(bf16[576,1024]{1,0:T(8,128)(2,1)} %all-gather.3.cloned.1.call-done) | copy-start | bytes 3538948
  51.9 0.7 copy-start.4
  55.3 5.9 %collective-permute-start = (bf16[128,128]{1,0:T(8,128)(2,1)S(1)}, bf16[128,128]{1,0:T(8,128)(2,1)S(1)}, u32[]{:S(2)}, u32[]{:S(2)}) collective-permute-start(bf16[128,128]{1,0:T(8,128)(2,1)S(1)} %get-tuple-element.30), channel_id=1, source_target_pairs={{0,4},{4,0},{32,36},{36,32},{1,5},{5,1},{33,37},{37,33},{2,6},{6,2... | collective-permute-start | bytes 98312 | tf_op jit(solution)/shard_map/ppermute | solution.py:415
  61.2 2.8 %collective-permute-start.1 = (bf16[128,128]{1,0:T(8,128)(2,1)S(1)}, bf16[128,128]{1,0:T(8,128)(2,1)S(1)}, u32[]{:S(2)}, u32[]{:S(2)}) collective-permute-start(bf16[128,128]{1,0:T(8,128)(2,1)S(1)} %get-tuple-element.31), channel_id=1, source_target_pairs={{0,32},{4,36},{32,0},{36,4},{1,33},{5,37},{33,1},{37,5},{2,34},{6,... | collective-permute-start | bytes 98312 | tf_op jit(solution)/shard_map/ppermute | solution.py:415
  64.0 5.7 %collective-permute-start.2 = (bf16[128,128]{1,0:T(8,128)(2,1)S(1)}, bf16[128,128]{1,0:T(8,128)(2,1)S(1)}, u32[]{:S(2)}, u32[]{:S(2)}) collective-permute-start(bf16[128,128]{1,0:T(8,128)(2,1)S(1)} %get-tuple-element.32), channel_id=1, source_target_pairs={{0,36},{4,32},{32,4},{36,0},{1,37},{5,33},{33,5},{37,1},{2,38},{6,... | collective-permute-start | bytes 98312 | tf_op jit(solution)/shard_map/ppermute | solution.py:415
  69.7 0.9 %copy-start = (bf16[128,512]{1,0:T(8,128)(2,1)S(1)}, bf16[128,512]{1,0:T(8,128)(2,1)}, u32[]{:S(2)}) copy-start(bf16[128,512]{1,0:T(8,128)(2,1)} %keys.3._.fk) | copy-start | bytes 393220
  70.6 8.1 %copy-start.1 = (bf16[128,512]{1,0:T(8,128)(2,1)S(1)}, bf16[128,512]{1,0:T(8,128)(2,1)}, u32[]{:S(2)}) copy-start(bf16[128,512]{1,0:T(8,128)(2,1)} %keys.3._.fk) | copy-start | bytes 393220
  76.5 6.3 %collective-permute-start.16 = (bf16[144,128]{1,0:T(8,128)(2,1)S(1)}, bf16[144,128]{1,0:T(8,128)(2,1)S(1)}, u32[]{:S(2)}, u32[]{:S(2)}) collective-permute-start(bf16[144,128]{1,0:T(8,128)(2,1)S(1)} %get-tuple-element.48), channel_id=1, source_target_pairs={{0,4},{4,0},{32,36},{36,32},{1,5},{5,1},{33,37},{37,33},{2,6},{6,2... | collective-permute-start | bytes 110600 | tf_op jit(solution)/shard_map/ppermute | solution.py:415
  76.6 6.2 %collective-permute-start.17 = (bf16[144,128]{1,0:T(8,128)(2,1)S(1)}, bf16[144,128]{1,0:T(8,128)(2,1)S(1)}, u32[]{:S(2)}, u32[]{:S(2)}) collective-permute-start(bf16[144,128]{1,0:T(8,128)(2,1)S(1)} %get-tuple-element.49), channel_id=1, source_target_pairs={{0,32},{4,36},{32,0},{36,4},{1,33},{5,37},{33,1},{37,5},{2,34},{6,... | collective-permute-start | bytes 110600 | tf_op jit(solution)/shard_map/ppermute | solution.py:415
  77.2 5.7 %collective-permute-start.18 = (bf16[144,128]{1,0:T(8,128)(2,1)S(1)}, bf16[144,128]{1,0:T(8,128)(2,1)S(1)}, u32[]{:S(2)}, u32[]{:S(2)}) collective-permute-start(bf16[144,128]{1,0:T(8,128)(2,1)S(1)} %get-tuple-element.50), channel_id=1, source_target_pairs={{0,36},{4,32},{32,4},{36,0},{1,37},{5,33},{33,5},{37,1},{2,38},{6,... | collective-permute-start | bytes 110600 | tf_op jit(solution)/shard_map/ppermute | solution.py:415
Sparse Core Ops, SparseCore 0:
  9.8 40.8 all-gather.2

commit v3 on v2

v3 whole, which is shorter than its diff:
```python
import math

import jax
import jax.numpy as jnp
from jax import lax
from jax.experimental import pallas as pl
from jax.experimental.pallas import tpu as pltpu
from jax.sharding import Mesh, PartitionSpec as P

HEAD = 128
TOK = 64
IMG = 2
WIDTH = 4096
PART = 1024
COLS = 512
ROWS = IMG * TOK
SCORE = math.log2(math.e) / math.sqrt(HEAD)
F32 = jnp.float32
BF16 = jnp.bfloat16
FLIP = [(0, 1), (1, 0)]


def params(limit):
    return pltpu.CompilerParams(vmem_limit_bytes=limit * 1024 * 1024)


def vmem(count):
    return [pl.BlockSpec(memory_space=pltpu.VMEM)] * count


def hbm(count):
    return [pl.BlockSpec(memory_space=pltpu.HBM)] * count


def anywhere(count):
    return [pl.BlockSpec(memory_space=pl.ANY)] * count


def smem():
    return pl.BlockSpec(memory_space=pltpu.SMEM)


def dot_t(a, b):
    return lax.dot_general(a, b, (((1,), (1,)), ((), ())), preferred_element_type=F32)


def head_of(code, d):
    core, y = code[0] & 1, (code[0] >> 1) & 3
    side = core ^ (d >> 1)
    bit = jnp.where(side == 0, (y ^ (y >> 1)) & 1, y >> 1)
    return 2 * side + (bit ^ (d & 1))


def head_slice(code, d):
    return pl.ds(pl.multiple_of(head_of(code, d) * HEAD, HEAD), HEAD)


def rank_of(code, j):
    flips = (0, jnp.where(code[0] & 1 == 0, 1, 3), jnp.where(code[0] & 1 == 0, 3, 1), 2)
    return (code[0] >> 3) ^ flips[j]


def pack_kernel(heads, keys, values, x, shift, scale, own, next_, other, pay, sems):
    copies = []

    def copy(source, target):
        copies.append(pltpu.make_async_copy(source, target, sems.at[len(copies)]))
        copies[-1].start()

    copy(x, pay.at[:ROWS])
    for d, out in ((2, other.at[0]), (3, other.at[1]), (1, next_), (0, own)):
        cut = head_slice(heads, d)
        for i in range(IMG):
            for j, source in enumerate((keys, values)):
                copy(source.at[i, :, cut], out.at[i, j])
    pay[ROWS:] = jnp.zeros((16, PART), BF16)
    pay[ROWS : ROWS + IMG] = shift[...]
    pay[ROWS + IMG : ROWS + 2 * IMG] = scale[...]
    for one in copies:
        one.wait()


def pack(heads, keys, values, x, shift, scale):
    shape = (IMG, 2, TOK, HEAD)
    return pl.pallas_call(
        pack_kernel,
        out_shape=[
            jax.ShapeDtypeStruct(shape, BF16),
            jax.ShapeDtypeStruct(shape, BF16),
            jax.ShapeDtypeStruct((2,) + shape, BF16),
            jax.ShapeDtypeStruct((ROWS + 16, PART), BF16),
        ],
        in_specs=[smem()] + hbm(3) + vmem(2),
        out_specs=vmem(4),
        scratch_shapes=[pltpu.SemaphoreType.DMA((17,))],
        compiler_params=params(56),
        name="pack",
    )(heads, keys, values, x, shift, scale)


def call(kernel, name, limit, shapes, operands, deps=()):
    return pl.pallas_call(
        kernel,
        out_shape=[jax.ShapeDtypeStruct(s, BF16) for s in shapes],
        in_specs=vmem(len(operands)) + anywhere(len(deps)),
        out_specs=vmem(len(shapes)),
        compiler_params=params(limit),
        name=name,
    )(*operands, *deps)


def join(groups, deps=()):
    counts = [len(g) for g in groups]

    def kernel(*refs):
        ins, outs = refs[: sum(counts)], refs[sum(counts) + len(deps) :]
        at = 0
        for out, count in zip(outs, counts):
            row = 0
            for r in ins[at : at + count]:
                out[row : row + r.shape[0]] = r[...]
                row += r.shape[0]
            at += count

    def shape(group):
        rows = sum(v.shape[0] for v in group)
        return jax.ShapeDtypeStruct((rows,) + group[0].shape[1:], group[0].dtype)

    return pl.pallas_call(
        kernel,
        out_shape=[shape(g) for g in groups],
        in_specs=vmem(sum(counts)) + anywhere(len(deps)),
        out_specs=vmem(len(groups)),
        compiler_params=params(12),
        name="join",
    )(*[v for g in groups for v in g], *deps)


def pair_kernel(a, b, out):
    out[0] = a[...]
    out[1] = b[1]


def stack_kernel(own, other, far, s0, s1):
    for i, s in enumerate((s0, s1)):
        s[0] = own[i]
        s[1] = other[0, i]
        s[2] = far[0, i]
        s[3] = far[1, i]


def query_pairs_kernel(own, next_, other, g, n):
    g[0] = own[...]
    g[1] = other[0]
    n[0] = next_[...]
    n[1] = other[1]


def back_kernel(g, y, z, d, _, out):
    for j, r in enumerate((g, z, y, d)):
        out[j] = r[1]


def weight_copies(idx, sources, buffers, sems):
    copies = []
    for n, (source, buffer) in enumerate(zip(sources, buffers)):
        for j in range(4):
            rows = pl.ds(pl.multiple_of(rank_of(idx, j) * PART, PART), PART)
            copies.append(
                pltpu.make_async_copy(source.at[rows, :], buffer.at[j], sems.at[4 * n + j])
            )
    for copy in copies:
        copy.start()
    return copies


def project(xs, buffer, copies):
    acc = jnp.zeros((ROWS, COLS), F32)
    for j in range(4):
        copies[j].wait()
        acc += jnp.dot(xs[j], buffer[j], preferred_element_type=F32)
    return acc


def head_norm(v, gain):
    return v * lax.rsqrt(jnp.mean(v * v, axis=-1, keepdims=True) + 1e-06) * gain


def query_kernel(idx, x0, x1, x2, x3, wq, qg, own, next_, other, qa, xs, buffer, sems):
    copies = weight_copies(idx, (wq,), (buffer,), sems)
    blocks = (x0, x1, x2, x3)
    total = sum(jnp.sum(b[:ROWS].astype(F32), axis=-1, keepdims=True) for b in blocks)
    mean = total / WIDTH
    square = jnp.zeros_like(mean)
    for b in blocks:
        centred = b[:ROWS].astype(F32) - mean
        square += jnp.sum(centred * centred, axis=-1, keepdims=True)
    rstd = lax.rsqrt(square / WIDTH + 1e-06)
    for j, b in enumerate(blocks):
        mods = b[ROWS : ROWS + 16].astype(F32)
        for i in range(IMG):
            rows = slice(i * TOK, (i + 1) * TOK)
            normed = (b[rows].astype(F32) - mean[rows]) * rstd[rows]
            out = normed * (1.0 + mods[IMG + i : IMG + i + 1, :]) + mods[i : i + 1, :]
            xs[j, rows, :] = out.astype(BF16)
    acc = project(xs, buffer, copies)
    for h in range(4):
        cut = slice(h * HEAD, (h + 1) * HEAD)
        qa[:, cut] = head_norm(acc[:, cut], qg[:1]).astype(BF16)
    own[...] = qa[:, head_slice(idx, 0)]
    next_[...] = qa[:, head_slice(idx, 1)]
    for j in range(2):
        other[j] = qa[:, head_slice(idx, 2 + j)]


def project_queries(idx, xs, wq, gain):
    return pl.pallas_call(
        query_kernel,
        out_shape=[
            jax.ShapeDtypeStruct((ROWS, HEAD), BF16),
            jax.ShapeDtypeStruct((ROWS, HEAD), BF16),
            jax.ShapeDtypeStruct((2, ROWS, HEAD), BF16),
            jax.ShapeDtypeStruct((ROWS, COLS), BF16),
            jax.ShapeDtypeStruct((4, ROWS, PART), BF16),
        ],
        in_specs=[smem()] + vmem(4) + hbm(1) + vmem(1),
        out_specs=vmem(5),
        scratch_shapes=[pltpu.VMEM((4, PART, COLS), BF16), pltpu.SemaphoreType.DMA((4,))],
        compiler_params=params(50),
        cost_estimate=pl.CostEstimate(
            flops=2 * ROWS * WIDTH * COLS, bytes_accessed=5 << 20, transcendentals=0
        ),
        name="queries",
    )(idx, *xs, wq, gain)


def fresh_kernel(idx, xs, qa, wk, wv, kg, _, fk, fv, out, lse, kbuf, vbuf, sems):
    copies = weight_copies(idx, (wk, wv), (kbuf, vbuf), sems)
    acc = project(xs, kbuf, copies[:4])
    for h in range(4):
        cut = slice(h * HEAD, (h + 1) * HEAD)
        fk[:, cut] = head_norm(acc[:, cut], kg[1:]).astype(BF16)
    fv[...] = project(xs, vbuf, copies[4:]).astype(BF16)
    lanes = lax.broadcasted_iota(jnp.int32, (TOK, HEAD), 1)
    for i in range(IMG):
        rows = slice(i * TOK, (i + 1) * TOK)
        levels = jnp.zeros((TOK, HEAD), F32)
        for h in range(4):
            cut = slice(h * HEAD, (h + 1) * HEAD)
            s = dot_t(qa[rows, cut], fk[rows, cut]) * SCORE
            top = jnp.max(s, axis=-1, keepdims=True)
            p = jnp.exp2(s - top)
            total = jnp.sum(p, axis=-1, keepdims=True)
            numer = jnp.dot(p.astype(BF16), fv[rows, cut], preferred_element_type=F32)
            out[rows, cut] = numer / total
            levels = jnp.where(lanes == h, top + jnp.log2(total), levels)
        lse[rows, :] = levels


def fresh(idx, xs, qa, wk, wv, gain, dep):
    return pl.pallas_call(
        fresh_kernel,
        out_shape=[jax.ShapeDtypeStruct((ROWS, COLS), BF16)] * 2
        + [
            jax.ShapeDtypeStruct((ROWS, COLS), F32),
            jax.ShapeDtypeStruct((ROWS, HEAD), F32),
        ],
        in_specs=[smem()] + vmem(2) + hbm(2) + vmem(1) + anywhere(1),
        out_specs=vmem(4),
        scratch_shapes=[pltpu.VMEM((4, PART, COLS), BF16)] * 2
        + [pltpu.SemaphoreType.DMA((8,))],
        compiler_params=params(50),
        cost_estimate=pl.CostEstimate(
            flops=4 * ROWS * WIDTH * COLS, bytes_accessed=9 << 20, transcendentals=0
        ),
        name="fresh",
    )(idx, xs, qa, wk, wv, gain, dep)


def attend_part(q, stream, state, mask):
    entries = 16
    count = entries * TOK
    for c in range(stream.shape[0] // entries):
        span = slice(c * entries, (c + 1) * entries)
        k = stream[span, 0].reshape(count, HEAD)
        v = stream[span, 1].reshape(count, HEAD)
        s = dot_t(q, k) * SCORE
        if state is None:
            s = jnp.concatenate(
                [jnp.where(mask, -1e30, s[:, : 4 * TOK]), s[:, 4 * TOK :]], axis=1
            )
            top = jnp.max(s, axis=-1, keepdims=True)
            p = jnp.exp2(s - top)
            total = jnp.sum(p, axis=-1, keepdims=True)
            numer = jnp.dot(p.astype(BF16), v, preferred_element_type=F32)
        else:
            old, total, numer = state
            top = jnp.maximum(old, jnp.max(s, axis=-1, keepdims=True))
            factor = jnp.exp2(old - top)
            p = jnp.exp2(s - top)
            total = total * factor + jnp.sum(p, axis=-1, keepdims=True)
            numer = numer * factor + jnp.dot(p.astype(BF16), v, preferred_element_type=F32)
        state = (top, total, numer)
    return state


def attend_kernel(g, n, gz, nd, s0, t0, s1, t1, *outs):
    groups = (g, n, gz, nd)
    count = 2 * len(groups)
    shape = (count * TOK, 4 * TOK)
    row_patch = lax.broadcasted_iota(jnp.int32, shape, 0) // TOK
    col_patch = lax.broadcasted_iota(jnp.int32, shape, 1) // TOK
    lse_rows = [jnp.zeros((1, HEAD), F32) for _ in range(count)]
    row = lax.broadcasted_iota(jnp.int32, (TOK, HEAD), 0)
    lane = lax.broadcasted_iota(jnp.int32, (TOK, HEAD), 1)
    for i, streams in enumerate(((s0, t0), (s1, t1))):
        q = jnp.concatenate(
            [r[j, i * TOK : (i + 1) * TOK] for r in groups for j in range(2)], axis=0
        )
        state = None
        for stream in streams:
            state = attend_part(q, stream, state, row_patch == col_patch)
        top, total, numer = state
        out = (numer / total).astype(BF16)
        level = top + jnp.log2(total)
        for d in range(count):
            span = slice(d * TOK, (d + 1) * TOK)
            outs[d // 2][d % 2, i * TOK : (i + 1) * TOK, :] = out[span]
            lse_rows[d] += jnp.sum(
                jnp.where(lane == row + i * TOK, level[span], 0.0), axis=0, keepdims=True
            )
    sub = lax.broadcasted_iota(jnp.int32, (16, HEAD), 0)
    for d in range(count):
        high = lse_rows[d].astype(BF16).astype(F32)
        rest = lse_rows[d] - high
        middle = rest.astype(BF16).astype(F32)
        low = rest - middle
        tail = jnp.where(sub == 0, high, jnp.where(sub == 1, middle, jnp.where(sub == 2, low, 0.0)))
        outs[d // 2][d % 2, ROWS : ROWS + 16, :] = tail.astype(BF16)


def attend(groups, streams):
    return pl.pallas_call(
        attend_kernel,
        out_shape=[jax.ShapeDtypeStruct((2, ROWS + 16, HEAD), BF16)] * 4,
        in_specs=vmem(8),
        out_specs=vmem(4),
        compiler_params=params(32),
        name="attend",
    )(*groups, *streams)


def combine_kernel(heads, g, z, y, d, other, near_out, near_lse, att):
    row = lax.broadcasted_iota(jnp.int32, (ROWS, HEAD), 0)
    lane = lax.broadcasted_iota(jnp.int32, (ROWS, HEAD), 1)
    halves = ((g.at[0], z.at[0]), (y.at[0], d.at[0]), (other.at[0], other.at[1]),
              (other.at[2], other.at[3]))
    for h, pair in enumerate(halves):
        cut = head_slice(heads, h)
        levels = [
            jnp.sum(jnp.where(lane == head_of(heads, h), near_lse[...], 0.0), axis=1, keepdims=True)
        ]
        parts = [near_out[:, cut]]
        for r in pair:
            tail = r[ROWS : ROWS + 16, :].astype(F32)
            level = tail[0:1] + tail[1:2] + tail[2:3]
            levels.append(jnp.sum(jnp.where(lane == row, level, 0.0), axis=1, keepdims=True))
            parts.append(r[:ROWS, :].astype(F32))
        top = jnp.maximum(jnp.maximum(levels[0], levels[1]), levels[2])
        weights = [jnp.exp2(level - top) for level in levels]
        out = sum(w * p for w, p in zip(weights, parts))
        att[:, cut] = (out / sum(weights)).astype(BF16)


def combine(heads, parts, near_out, near_lse):
    return pl.pallas_call(
        combine_kernel,
        out_shape=jax.ShapeDtypeStruct((ROWS, COLS), BF16),
        in_specs=[smem()] + vmem(7),
        out_specs=pl.BlockSpec(memory_space=pltpu.VMEM),
        compiler_params=params(8),
        name="combine",
    )(heads, *parts, near_out, near_lse)


def swap(value, axis, step):
    flips = ((1, 3), (3, 1))[step]
    if axis == "zh":
        names, far, near_ = ("core", axis), 1, 4
    else:
        names, far, near_ = (axis, "core"), 2, 1
    perm = [
        (a * far + c * near_, (a ^ flips[c]) * far + c * near_)
        for a in range(4)
        for c in range(2)
    ]
    return lax.ppermute(value, names, perm)


def diagonal(value):
    perm = [
        (z * 8 + y * 2 + c, (z ^ 1) * 8 + (y ^ (1, 3)[c]) * 2 + c)
        for z in range(2)
        for y in range(4)
        for c in range(2)
    ]
    return lax.ppermute(value, ("zl", "y", "core"), perm)


def on_device(activations, mod_shift, mod_scale, w_query, w_key, w_value,
              query_gain, key_gain, stale_keys, stale_values):
    code = lax.axis_index("zh") * 8 + lax.axis_index("y") * 2 + lax.axis_index("core")
    code = code.astype(jnp.int32).reshape(1)

    own, next_, other, x0 = pack(
        code, stale_keys, stale_values, activations.reshape(ROWS, PART), mod_shift, mod_scale
    )
    x1, x2 = swap(x0, "zh", 0), swap(x0, "zh", 1)
    other = lax.ppermute(other, "core", FLIP)
    shape = (IMG, 2, TOK, HEAD)
    (far,) = call(pair_kernel, "pair", 8, [(2,) + shape], (next_, other))
    far = swap(far, "y", 0)
    s0, s1 = call(stack_kernel, "stack", 8, [(4,) + shape[1:]] * 2, (own, other, far))
    gains = (query_gain.reshape(1, HEAD), key_gain.reshape(1, HEAD))
    s0, s1, x0, gains = join(
        [(s0, swap(s0, "y", 1)), (s1, swap(s1, "x", 0)), (x0,), gains], (x1, x2)
    )
    x3 = swap(x1, "zh", 1)
    own, next_, other, qa, xs = project_queries(
        code, (x0, x1, x2, x3), w_query, gains
    )
    s0, s1 = join([(s0, swap(s0, "x", 0)), (s1, swap(s1, "x", 1))], (own,))
    t0, t1 = swap(s0, "x", 1), swap(s1, "y", 1)

    other = lax.ppermute(other, "core", FLIP)
    g, n = call(query_pairs_kernel, "query_pairs", 8, [(2, ROWS, HEAD)] * 2, (own, next_, other))
    groups = (g, swap(n, "y", 0), lax.ppermute(g, "zl", FLIP), diagonal(n))
    pg, py, pz, pd = attend(groups, (s0, t0, s1, t1))
    fk, fv, near_out, near_lse = fresh(
        code, xs, qa, w_key, w_value, gains, py
    )
    py, pz, pd = swap(py, "y", 0), lax.ppermute(pz, "zl", FLIP), diagonal(pd)
    (back,) = call(
        back_kernel, "back", 8, [(4, ROWS + 16, HEAD)], (pg, py, pz, pd), (near_lse,)
    )
    back = lax.ppermute(back, "core", FLIP)
    att = combine(code, (pg, pz, py, pd, back), near_out, near_lse)
    shape = (IMG, TOK, COLS)
    return att.reshape(shape), fk.reshape(shape), fv.reshape(shape)


def solution(mesh):
    split = Mesh(mesh.devices.reshape(4, 2, 4, 2, 4), ("x", "zl", "y", "core", "zh"))
    patch = ("x", "zl", "y", "core")
    rows = P(None, patch, "zh")
    cols = P(None, "zh")
    return jax.shard_map(
        on_device,
        mesh=split,
        in_specs=(rows, cols, cols, cols, cols, cols, P(), P(), rows, rows),
        out_specs=(rows, rows, rows),
        check_vma=False,
    )
```

time: 90.9 us -> 67.9 us (0.75)
  between operations: 14.2 us -> 0.76 us
  waiting for transfers between devices: 27.1 us -> 13.8 us
  starting transfers between devices: 24.6 us -> 34.1 us
  Pallas kernels: 21 us -> 14.9 us
    ppermute x10 -> x12, starting transfers between devices: 8.88 us -> 21.8 us  [swap(): return lax.ppermute(value, names, perm)]
    ppermute x10 -> x12, waiting for transfers between devices: 16.9 us -> 8.79 us  [swap(): return lax.ppermute(value, names, perm)]
    pallas_call x7, Pallas kernels: 17.3 us -> 11.1 us  [the longest x1 5.32 us: fresh(): pl.pallas_call(fresh_kernel, out_shape=[jax.ShapeDtypeStruct((ROWS, COLS)...]
    all_gather x1 -> x0, waiting for transfers between devices: 3.71 us -> none  [on_device(): xall = lax.all_gather(x0, 'zh')]
    ppermute x9 -> x7, starting transfers between devices: 15.7 us -> 12.3 us  [the longest x2 6.97 us: on_device(): other = lax.ppermute(other, 'core', FLIP)]
    ppermute x9 -> x7, waiting for transfers between devices: 6.38 us -> 5.04 us  [the longest x2 2.84 us: diagonal(): return lax.ppermute(value, ('zl', 'y', 'core'), perm)]
    unnamed x12 -> x10, local copies, waits for them, and re-layouts: 3.67 us -> 3.94 us
  transfers between devices with their start and end apart: 20 -> 19, of which waited for: 11 -> 7; matrix products, arithmetic and copies ran while one was open for 0% -> 0% of each run, Pallas kernels for 15% -> 12%
where the time goes in v3:
time: 67.9 us; the launch traced here: 67.6 us
  starting transfers between devices  34.1 us (50%)
  Pallas kernels  14.9 us (22%)
  waiting for transfers between devices  13.8 us (20%)
  local copies, waits for them, and re-layouts  3.94 us (6%)
  between operations  0.76 us (1%)
    ppermute x12, starting transfers between devices, swap(): return lax.ppermute(value, names, perm)  21.8 us
    ppermute x12, waiting for transfers between devices, swap(): return lax.ppermute(value, names, perm)  8.79 us
    ppermute x2, starting transfers between devices, on_device(): other = lax.ppermute(other, 'core', FLIP)  6.97 us
    pallas_call x1, Pallas kernels, fresh(): pl.pallas_call(fresh_kernel, out_shape=[jax.ShapeDtypeStruct((ROWS, COLS)...  5.32 us
    unnamed x10, local copies, waits for them, and re-layouts  3.94 us
    pallas_call x1, Pallas kernels, attend(): pl.pallas_call(attend_kernel, out_shape=[jax.ShapeDtypeStruct((2, ROWS +...  3.15 us
    ppermute x2, waiting for transfers between devices, diagonal(): return lax.ppermute(value, ('zl', 'y', 'core'), perm)  2.84 us
    pallas_call x1, Pallas kernels, project_queries(): pl.pallas_call(query_kernel, out_shape=[jax.ShapeDtypeStruct((ROWS, HEAD)...  2.68 us
  transfers between devices with their start and end apart: 19, of which 7 were waited for; matrix products, arithmetic and copies ran while one was open for 0% of the time, Pallas kernels for 12%

profile of v3, /device:TPU:1, one launch (start us, length us, event | category | flops | bytes accessed | tf_op | source)
XLA Modules:
  0.0 67.6 jit_solution(1197688249344610047)
XLA Ops:
  0.6 2.6 %pack.1 = (bf16[2,2,64,128]{3,2,1,0:T(8,128)(2,1)}, bf16[2,2,64,128]{3,2,1,0:T(8,128)(2,1)}, bf16[2,2,2,64,128]{4,3,2,1,0:T(8,128)(2,1)}, bf16[144,1024]{1,0:T(8,128)(2,1)}) custom-call(s32[1]{0:T(128)} %bitcast.heads.idx, bf16[2,64,512]{2,1,0:T(8,128)(2,1)} %keys.1, bf16[2,64,512]{2,1,0:T(8,128)(2,1)} %values.1, bf16[128,1024]{1,0:T(8,128)(2,1)} %bitcast.9, ...), custom_call_target="tpu_custom_call" | custom-call | tf_op jit(solution)/shard_map/pack/pallas_call | solution.py:85
  3.3 3.3 %collective-permute-start = (bf16[2,2,2,64,128]{4,3,2,1,0:T(8,128)(2,1)}, bf16[2,2,2,64,128]{4,3,2,1,0:T(8,128)(2,1)S(1)}, u32[]{:S(2)}, u32[]{:S(2)}) collective-permute-start(bf16[2,2,2,64,128]{4,3,2,1,0:T(8,128)(2,1)} %get-tuple-element.31), channel_id=1, source_target_pairs={{0,4},{4,0},{1,5},{5,1},{2,6},{6,2},{3,7},{7,3},{8,12},{12,8},{9,1... | collective-permute-start | bytes 393224 | tf_op jit(solution)/shard_map/ppermute | solution.py:419
  6.6 4.3 %collective-permute-start.4 = (bf16[144,1024]{1,0:T(8,128)(2,1)}, bf16[144,1024]{1,0:T(8,128)(2,1)S(1)}, u32[]{:S(2)}, u32[]{:S(2)}) collective-permute-start(bf16[144,1024]{1,0:T(8,128)(2,1)} %get-tuple-element.35.refs_4_), channel_id=1, source_target_pairs={{0,1},{4,7},{1,0},{5,6},{2,3},{6,5},{3,2},{7,4},{8,9},{12,15},{9,8... | collective-permute-start | bytes 884744 | tf_op jit(solution)/shard_map/ppermute | solution.py:397
  10.9 1.2 %collective-permute-start.5 = (bf16[144,1024]{1,0:T(8,128)(2,1)}, bf16[144,1024]{1,0:T(8,128)(2,1)S(1)}, u32[]{:S(2)}, u32[]{:S(2)}) collective-permute-start(bf16[144,1024]{1,0:T(8,128)(2,1)} %get-tuple-element.35.refs_4_), channel_id=1, source_target_pairs={{0,3},{4,5},{1,2},{5,4},{2,1},{6,7},{3,0},{7,6},{8,11},{12,13},{9,... | collective-permute-start | bytes 884744 | tf_op jit(solution)/shard_map/ppermute | solution.py:397
  12.1 0.0 collective-permute-done.b.other
  12.1 0.0 copy-start.2
  12.1 0.8 %copy-done.2 = bf16[2,2,64,128]{3,2,1,0:T(8,128)(2,1)S(1)} copy-done((bf16[2,2,64,128]{3,2,1,0:T(8,128)(2,1)S(1)}, bf16[2,2,64,128]{3,2,1,0:T(8,128)(2,1)}, u32[]{:S(2)}) %copy-start.2) | copy-done | bytes 65560
  12.9 2.8 %collective-permute-start.1 = (bf16[2,2,2,64,128]{4,3,2,1,0:T(8,128)(2,1)S(1)}, bf16[2,2,2,64,128]{4,3,2,1,0:T(8,128)(2,1)S(1)}, u32[]{:S(2)}, u32[]{:S(2)}) collective-permute-start(bf16[2,2,2,64,128]{4,3,2,1,0:T(8,128)(2,1)S(1)} %pair.1), channel_id=1, source_target_pairs={{0,8},{4,28},{8,0},{12,20},{16,24},{20,12},{24,16},{28,4},{1,9},{5... | collective-permute-start | bytes 393224 | tf_op jit(solution)/shard_map/ppermute | solution.py:397
  15.7 2.7 %collective-permute-done.1.far = bf16[2,2,2,64,128]{4,3,2,1,0:T(8,128)(2,1)S(1)} collective-permute-done((bf16[2,2,2,64,128]{4,3,2,1,0:T(8,128)(2,1)S(1)}, bf16[2,2,2,64,128]{4,3,2,1,0:T(8,128)(2,1)S(1)}, u32[]{:S(2)}, u32[]{:S(2)}) %collective-permute-start.1) | collective-permute-done | bytes 131104 | tf_op jit(solution)/shard_map/ppermute | solution.py:397
  18.4 0.0 copy-start.1
  18.4 0.8 %copy-done.1 = bf16[2,2,64,128]{3,2,1,0:T(8,128)(2,1)S(1)} copy-done((bf16[2,2,64,128]{3,2,1,0:T(8,128)(2,1)S(1)}, bf16[2,2,64,128]{3,2,1,0:T(8,128)(2,1)}, u32[]{:S(2)}) %copy-start.1) | copy-done | bytes 65560
  19.3 0.1 collective-permute-start.2
  19.4 2.6 %collective-permute-start.3 = (bf16[4,2,64,128]{3,2,1,0:T(8,128)(2,1)S(1)}, bf16[4,2,64,128]{3,2,1,0:T(8,128)(2,1)S(1)}, u32[]{:S(2)}, u32[]{:S(2)}) collective-permute-start(bf16[4,2,64,128]{3,2,1,0:T(8,128)(2,1)S(1)} %get-tuple-element.34.refs_2_), channel_id=1, source_target_pairs={{0,64},{4,196},{64,0},{68,132},{128,192},{132,68},{192,128},{196,4... | collective-permute-start | bytes 393224 | tf_op jit(solution)/shard_map/ppermute | solution.py:397
  21.9 0.0 collective-permute-done.4.refs_7_.x1
  21.9 3.3 %collective-permute-start.6 = (bf16[144,1024]{1,0:T(8,128)(2,1)S(1)}, bf16[144,1024]{1,0:T(8,128)(2,1)S(1)}, u32[]{:S(2)}, u32[]{:S(2)}) collective-permute-start(bf16[144,1024]{1,0:T(8,128)(2,1)S(1)} %collective-permute-done.4.refs_7_.x1), channel_id=1, source_target_pairs={{0,3},{4,5},{1,2},{5,4},{2,1},{6,7},{3,0},{7,6},{8,11},{12,13},{9,... | collective-permute-start | bytes 884744 | tf_op jit(solution)/shard_map/ppermute | solution.py:397
  25.3 0.0 collective-permute-done.5.refs_8_.x2
  25.3 0.0 collective-permute-done.2.refs_1_
  25.3 0.0 collective-permute-done.3.refs_3_
  25.3 0.0 copy-start
  25.3 1.0 %copy-done = bf16[144,1024]{1,0:T(8,128)(2,1)S(1)} copy-done((bf16[144,1024]{1,0:T(8,128)(2,1)S(1)}, bf16[144,1024]{1,0:T(8,128)(2,1)}, u32[]{:S(2)}) %copy-start) | copy-done | bytes 294936
  26.2 0.0 copy-start.3
  26.2 0.7 copy-done.3
  26.9 0.0 copy-start.4
  26.9 0.7 copy-done.4
  27.6 0.1 join.2
  27.6 2.6 %collective-permute-start.11 = (bf16[8,2,64,128]{3,2,1,0:T(8,128)(2,1)S(1)}, bf16[8,2,64,128]{3,2,1,0:T(8,128)(2,1)S(1)}, u32[]{:S(2)}, u32[]{:S(2)}) collective-permute-start(bf16[8,2,64,128]{3,2,1,0:T(8,128)(2,1)S(1)} %get-tuple-element.43.refs_0_), channel_id=1, source_target_pairs={{0,64},{4,196},{64,0},{68,132},{128,192},{132,68},{192,128},{196,4... | collective-permute-start | bytes 786440 | tf_op jit(solution)/shard_map/ppermute | solution.py:397
  30.2 0.0 collective-permute-start.12
  30.2 2.7 %collective-permute-done.6.x3 = bf16[144,1024]{1,0:T(8,128)(2,1)S(1)} collective-permute-done((bf16[144,1024]{1,0:T(8,128)(2,1)S(1)}, bf16[144,1024]{1,0:T(8,128)(2,1)S(1)}, u32[]{:S(2)}, u32[]{:S(2)}) %collective-permute-start.6) | collective-permute-done | bytes 294944 | tf_op jit(solution)/shard_map/ppermute | solution.py:397
  32.8 2.7 %queries.1 = (bf16[128,128]{1,0:T(8,128)(2,1)S(1)}, bf16[128,128]{1,0:T(8,128)(2,1)S(1)}, bf16[2,128,128]{2,1,0:T(8,128)(2,1)S(1)}, bf16[128,512]{1,0:T(8,128)(2,1)S(1)}, bf16[4,128,1024]{2,1,0:T(8,128)(2,1)S(1)}) custom-call(s32[1]{0:T(128)} %bitcast.heads.idx, bf16[144,1024]{1,0:T(8,128)(2,1)S(1)} %get-tuple-element.36.x0, ...), custom_call_target="tpu_custom_call" | custom-call | flops 536870912 | bytes 5242880 | tf_op jit(solution)/shard_map/queries/pallas_call | solution.py:217
  35.5 0.0 collective-permute-done.11.refs_1_
  35.5 2.7 %collective-permute-done.12.refs_3_ = bf16[8,2,64,128]{3,2,1,0:T(8,128)(2,1)S(1)} collective-permute-done((bf16[8,2,64,128]{3,2,1,0:T(8,128)(2,1)S(1)}, bf16[8,2,64,128]{3,2,1,0:T(8,128)(2,1)S(1)}, u32[]{:S(2)}, u32[]{:S(2)}) %collective-permute-start.12) | collective-permute-done | bytes 262176 | tf_op jit(solution)/shard_map/ppermute | solution.py:397
  38.2 0.1 join.3
  38.3 0.1 collective-permute-start.13
  38.4 1.5 %collective-permute-start.14 = (bf16[16,2,64,128]{3,2,1,0:T(8,128)(2,1)S(1)}, bf16[16,2,64,128]{3,2,1,0:T(8,128)(2,1)S(1)}, u32[]{:S(2)}, u32[]{:S(2)}) collective-permute-start(bf16[16,2,64,128]{3,2,1,0:T(8,128)(2,1)S(1)} %get-tuple-element.46.s1), channel_id=1, source_target_pairs={{0,24},{4,12},{8,16},{12,4},{16,8},{20,28},{24,0},{28,20},{1,25},{... | collective-permute-start | bytes 1572872 | tf_op jit(solution)/shard_map/ppermute | solution.py:397
  39.9 3.6 %collective-permute-start.7 = (bf16[2,128,128]{2,1,0:T(8,128)(2,1)S(1)}, bf16[2,128,128]{2,1,0:T(8,128)(2,1)S(1)}, u32[]{:S(2)}, u32[]{:S(2)}) collective-permute-start(bf16[2,128,128]{2,1,0:T(8,128)(2,1)S(1)} %get-tuple-element.40), channel_id=1, source_target_pairs={{0,4},{4,0},{1,5},{5,1},{2,6},{6,2},{3,7},{7,3},{8,12},{12,8},{9,1... | collective-permute-start | bytes 196616 | tf_op jit(solution)/shard_map/ppermute | solution.py:435
  43.6 0.9 %collective-permute-done.7.other = bf16[2,128,128]{2,1,0:T(8,128)(2,1)S(1)} collective-permute-done((bf16[2,128,128]{2,1,0:T(8,128)(2,1)S(1)}, bf16[2,128,128]{2,1,0:T(8,128)(2,1)S(1)}, u32[]{:S(2)}, u32[]{:S(2)}) %collective-permute-start.7) | collective-permute-done | bytes 65568 | tf_op jit(solution)/shard_map/ppermute | solution.py:435
  44.5 2.1 %collective-permute-start.9 = (bf16[2,128,128]{2,1,0:T(8,128)(2,1)S(1)}, bf16[2,128,128]{2,1,0:T(8,128)(2,1)S(1)}, u32[]{:S(2)}, u32[]{:S(2)}) collective-permute-start(bf16[2,128,128]{2,1,0:T(8,128)(2,1)S(1)} %get-tuple-element.41.g), channel_id=1, source_target_pairs={{0,32},{32,0},{1,33},{33,1},{2,34},{34,2},{3,35},{35,3},{4,36},{36... | collective-permute-start | bytes 196616 | tf_op jit(solution)/shard_map/ppermute | solution.py:437
  46.6 0.0 collective-permute-start.10
  46.6 2.5 %collective-permute-start.8 = (bf16[2,128,128]{2,1,0:T(8,128)(2,1)S(1)}, bf16[2,128,128]{2,1,0:T(8,128)(2,1)S(1)}, u32[]{:S(2)}, u32[]{:S(2)}) collective-permute-start(bf16[2,128,128]{2,1,0:T(8,128)(2,1)S(1)} %get-tuple-element.42), channel_id=1, source_target_pairs={{0,8},{4,28},{8,0},{12,20},{16,24},{20,12},{24,16},{28,4},{1,9},{5... | collective-permute-start | bytes 196616 | tf_op jit(solution)/shard_map/ppermute | solution.py:397
  49.0 0.0 collective-permute-done.9.gz
  49.0 2.8 %collective-permute-done.10.nd = bf16[2,128,128]{2,1,0:T(8,128)(2,1)S(1)} collective-permute-done((bf16[2,128,128]{2,1,0:T(8,128)(2,1)S(1)}, bf16[2,128,128]{2,1,0:T(8,128)(2,1)S(1)}, u32[]{:S(2)}, u32[]{:S(2)}) %collective-permute-start.10) | collective-permute-done | bytes 65568 | tf_op jit(solution)/shard_map/ppermute | solution.py:407
  51.9 0.8 %collective-permute-done.8.n = bf16[2,128,128]{2,1,0:T(8,128)(2,1)S(1)} collective-permute-done((bf16[2,128,128]{2,1,0:T(8,128)(2,1)S(1)}, bf16[2,128,128]{2,1,0:T(8,128)(2,1)S(1)}, u32[]{:S(2)}, u32[]{:S(2)}) %collective-permute-start.8) | collective-permute-done | bytes 65568 | tf_op jit(solution)/shard_map/ppermute | solution.py:397
  52.6 0.0 collective-permute-done.13.t0
  52.6 0.0 collective-permute-done.14.t1
  52.7 3.1 %attend.1 = (bf16[2,144,128]{2,1,0:T(8,128)(2,1)S(1)}, bf16[2,144,128]{2,1,0:T(8,128)(2,1)S(1)}, bf16[2,144,128]{2,1,0:T(8,128)(2,1)S(1)}, bf16[2,144,128]{2,1,0:T(8,128)(2,1)S(1)}) custom-call(bf16[2,128,128]{2,1,0:T(8,128)(2,1)S(1)} %get-tuple-element.41.g, bf16[2,128,128]{2,1,0:T(8,128)(2,1)S(1)} %collective-permute-done.8.n, ...), custom_call_target="tpu_custom_call" | custom-call | tf_op jit(solution)/shard_map/attend/pallas_call | solution.py:343
  55.8 1.2 %collective-permute-start.15 = (bf16[2,144,128]{2,1,0:T(8,128)(2,1)S(1)}, bf16[2,144,128]{2,1,0:T(8,128)(2,1)S(1)}, u32[]{:S(2)}, u32[]{:S(2)}) collective-permute-start(bf16[2,144,128]{2,1,0:T(8,128)(2,1)S(1)} %get-tuple-element.48), channel_id=1, source_target_pairs={{0,32},{32,0},{1,33},{33,1},{2,34},{34,2},{3,35},{35,3},{4,36},{36... | collective-permute-start | bytes 221192 | tf_op jit(solution)/shard_map/ppermute | solution.py:442
  57.0 1.9 %collective-permute-start.17 = (bf16[2,144,128]{2,1,0:T(8,128)(2,1)S(1)}, bf16[2,144,128]{2,1,0:T(8,128)(2,1)S(1)}, u32[]{:S(2)}, u32[]{:S(2)}) collective-permute-start(bf16[2,144,128]{2,1,0:T(8,128)(2,1)S(1)} %get-tuple-element.50), channel_id=1, source_target_pairs={{0,40},{4,60},{8,32},{12,52},{16,56},{20,44},{24,48},{28,36},{32,8... | collective-permute-start | bytes 221192 | tf_op jit(solution)/shard_map/ppermute | solution.py:407
  58.9 0.9 %collective-permute-start.16 = (bf16[2,144,128]{2,1,0:T(8,128)(2,1)S(1)}, bf16[2,144,128]{2,1,0:T(8,128)(2,1)S(1)}, u32[]{:S(2)}, u32[]{:S(2)}) collective-permute-start(bf16[2,144,128]{2,1,0:T(8,128)(2,1)S(1)} %get-tuple-element.49._), channel_id=1, source_target_pairs={{0,8},{4,28},{8,0},{12,20},{16,24},{20,12},{24,16},{28,4},{1,9},{5... | collective-permute-start | bytes 221192 | tf_op jit(solution)/shard_map/ppermute | solution.py:397
  59.8 5.3 %fresh.1 = (bf16[128,512]{1,0:T(8,128)(2,1)}, bf16[128,512]{1,0:T(8,128)(2,1)}, f32[128,512]{1,0:T(8,128)S(1)}, f32[128,128]{1,0:T(8,128)S(1)}) custom-call(s32[1]{0:T(128)} %bitcast.heads.idx, bf16[4,128,1024]{2,1,0:T(8,128)(2,1)S(1)} %get-tuple-element.51.xs, bf16[128,512]{1,0:T(8,128)(2,1)S(1)} %get-tuple-element.52.qa, bf16[4096,512]{1,0:T(8,128)(2,1)} %wk.1, ...), custom_call_target="tpu_custom_call" | custom-call | flops 1073741824 | bytes 9437184 | tf_op jit(solution)/shard_map/fresh/pallas_call | solution.py:261
  65.1 0.0 collective-permute-done.15.z
  65.1 0.0 collective-permute-done.17.d
  65.1 0.0 collective-permute-done.16.y
  65.1 0.2 collective-permute-start.18
  65.3 1.3 %collective-permute-done.18.other = bf16[4,144,128]{2,1,0:T(8,128)(2,1)S(1)} collective-permute-done((bf16[4,144,128]{2,1,0:T(8,128)(2,1)S(1)}, bf16[4,144,128]{2,1,0:T(8,128)(2,1)S(1)}, u32[]{:S(2)}, u32[]{:S(2)}) %collective-permute-start.18) | collective-permute-done | bytes 147488 | tf_op jit(solution)/shard_map/ppermute | solution.py:446
  66.6 1.0 %combine.1 = bf16[128,512]{1,0:T(8,128)(2,1)} custom-call(s32[1]{0:T(128)} %bitcast.heads.idx, bf16[2,144,128]{2,1,0:T(8,128)(2,1)S(1)} %get-tuple-element.47.g, bf16[2,144,128]{2,1,0:T(8,128)(2,1)S(1)} %collective-permute-done.15.z, bf16[2,144,128]{2,1,0:T(8,128)(2,1)S(1)} %collective-permute-done.16.y, bf16[2,144,128]{2,1,0:T(8,128)(2,1)S(1)} %collective-permute-done.17.d, ...), custom_call_target="tpu_custom_call" | custom-call | tf_op jit(solution)/shard_map/combine/pallas_call | solution.py:376
  (4 shorter events, 0.1 us)
Async XLA Ops:
  3.3 8.8 %collective-permute-start = (bf16[2,2,2,64,128]{4,3,2,1,0:T(8,128)(2,1)}, bf16[2,2,2,64,128]{4,3,2,1,0:T(8,128)(2,1)S(1)}, u32[]{:S(2)}, u32[]{:S(2)}) collective-permute-start(bf16[2,2,2,64,128]{4,3,2,1,0:T(8,128)(2,1)} %get-tuple-element.31), channel_id=1, source_target_pairs={{0,4},{4,0},{1,5},{5,1},{2,6},{6,2},{3,7},{7,3},{8,12},{12,8},{9,1... | collective-permute-start | bytes 393224 | tf_op jit(solution)/shard_map/ppermute | solution.py:419
  6.6 15.3 %collective-permute-start.4 = (bf16[144,1024]{1,0:T(8,128)(2,1)}, bf16[144,1024]{1,0:T(8,128)(2,1)S(1)}, u32[]{:S(2)}, u32[]{:S(2)}) collective-permute-start(bf16[144,1024]{1,0:T(8,128)(2,1)} %get-tuple-element.35.refs_4_), channel_id=1, source_target_pairs={{0,1},{4,7},{1,0},{5,6},{2,3},{6,5},{3,2},{7,4},{8,9},{12,15},{9,8... | collective-permute-start | bytes 884744 | tf_op jit(solution)/shard_map/ppermute | solution.py:397
  10.9 14.4 %collective-permute-start.5 = (bf16[144,1024]{1,0:T(8,128)(2,1)}, bf16[144,1024]{1,0:T(8,128)(2,1)S(1)}, u32[]{:S(2)}, u32[]{:S(2)}) collective-permute-start(bf16[144,1024]{1,0:T(8,128)(2,1)} %get-tuple-element.35.refs_4_), channel_id=1, source_target_pairs={{0,3},{4,5},{1,2},{5,4},{2,1},{6,7},{3,0},{7,6},{8,11},{12,13},{9,... | collective-permute-start | bytes 884744 | tf_op jit(solution)/shard_map/ppermute | solution.py:397
  12.1 0.8 %copy-start.2 = (bf16[2,2,64,128]{3,2,1,0:T(8,128)(2,1)S(1)}, bf16[2,2,64,128]{3,2,1,0:T(8,128)(2,1)}, u32[]{:S(2)}) copy-start(bf16[2,2,64,128]{3,2,1,0:T(8,128)(2,1)} %get-tuple-element.32.a) | copy-start | bytes 196612
  12.9 5.5 %collective-permute-start.1 = (bf16[2,2,2,64,128]{4,3,2,1,0:T(8,128)(2,1)S(1)}, bf16[2,2,2,64,128]{4,3,2,1,0:T(8,128)(2,1)S(1)}, u32[]{:S(2)}, u32[]{:S(2)}) collective-permute-start(bf16[2,2,2,64,128]{4,3,2,1,0:T(8,128)(2,1)S(1)} %pair.1), channel_id=1, source_target_pairs={{0,8},{4,28},{8,0},{12,20},{16,24},{20,12},{24,16},{28,4},{1,9},{5... | collective-permute-start | bytes 393224 | tf_op jit(solution)/shard_map/ppermute | solution.py:397
  18.4 0.8 %copy-start.1 = (bf16[2,2,64,128]{3,2,1,0:T(8,128)(2,1)S(1)}, bf16[2,2,64,128]{3,2,1,0:T(8,128)(2,1)}, u32[]{:S(2)}) copy-start(bf16[2,2,64,128]{3,2,1,0:T(8,128)(2,1)} %get-tuple-element.30.own) | copy-start | bytes 196612
  19.3 6.0 %collective-permute-start.2 = (bf16[4,2,64,128]{3,2,1,0:T(8,128)(2,1)S(1)}, bf16[4,2,64,128]{3,2,1,0:T(8,128)(2,1)S(1)}, u32[]{:S(2)}, u32[]{:S(2)}) collective-permute-start(bf16[4,2,64,128]{3,2,1,0:T(8,128)(2,1)S(1)} %get-tuple-element.33.refs_0_), channel_id=1, source_target_pairs={{0,24},{4,12},{8,16},{12,4},{16,8},{20,28},{24,0},{28,20},{1,25},{... | collective-permute-start | bytes 393224 | tf_op jit(solution)/shard_map/ppermute | solution.py:397
  19.4 5.9 %collective-permute-start.3 = (bf16[4,2,64,128]{3,2,1,0:T(8,128)(2,1)S(1)}, bf16[4,2,64,128]{3,2,1,0:T(8,128)(2,1)S(1)}, u32[]{:S(2)}, u32[]{:S(2)}) collective-permute-start(bf16[4,2,64,128]{3,2,1,0:T(8,128)(2,1)S(1)} %get-tuple-element.34.refs_2_), channel_id=1, source_target_pairs={{0,64},{4,196},{64,0},{68,132},{128,192},{132,68},{192,128},{196,4... | collective-permute-start | bytes 393224 | tf_op jit(solution)/shard_map/ppermute | solution.py:397
  21.9 10.9 %collective-permute-start.6 = (bf16[144,1024]{1,0:T(8,128)(2,1)S(1)}, bf16[144,1024]{1,0:T(8,128)(2,1)S(1)}, u32[]{:S(2)}, u32[]{:S(2)}) collective-permute-start(bf16[144,1024]{1,0:T(8,128)(2,1)S(1)} %collective-permute-done.4.refs_7_.x1), channel_id=1, source_target_pairs={{0,3},{4,5},{1,2},{5,4},{2,1},{6,7},{3,0},{7,6},{8,11},{12,13},{9,... | collective-permute-start | bytes 884744 | tf_op jit(solution)/shard_map/ppermute | solution.py:397
  25.3 1.0 %copy-start = (bf16[144,1024]{1,0:T(8,128)(2,1)S(1)}, bf16[144,1024]{1,0:T(8,128)(2,1)}, u32[]{:S(2)}) copy-start(bf16[144,1024]{1,0:T(8,128)(2,1)} %get-tuple-element.35.refs_4_) | copy-start | bytes 884740
  26.2 0.7 copy-start.3
  26.9 0.7 copy-start.4
  27.6 7.9 %collective-permute-start.11 = (bf16[8,2,64,128]{3,2,1,0:T(8,128)(2,1)S(1)}, bf16[8,2,64,128]{3,2,1,0:T(8,128)(2,1)S(1)}, u32[]{:S(2)}, u32[]{:S(2)}) collective-permute-start(bf16[8,2,64,128]{3,2,1,0:T(8,128)(2,1)S(1)} %get-tuple-element.43.refs_0_), channel_id=1, source_target_pairs={{0,64},{4,196},{64,0},{68,132},{128,192},{132,68},{192,128},{196,4... | collective-permute-start | bytes 786440 | tf_op jit(solution)/shard_map/ppermute | solution.py:397
  30.2 8.1 %collective-permute-start.12 = (bf16[8,2,64,128]{3,2,1,0:T(8,128)(2,1)S(1)}, bf16[8,2,64,128]{3,2,1,0:T(8,128)(2,1)S(1)}, u32[]{:S(2)}, u32[]{:S(2)}) collective-permute-start(bf16[8,2,64,128]{3,2,1,0:T(8,128)(2,1)S(1)} %get-tuple-element.44.refs_2_), channel_id=1, source_target_pairs={{0,192},{4,68},{64,128},{68,4},{128,64},{132,196},{192,0},{196,132... | collective-permute-start | bytes 786440 | tf_op jit(solution)/shard_map/ppermute | solution.py:397
  38.3 14.3 %collective-permute-start.13 = (bf16[16,2,64,128]{3,2,1,0:T(8,128)(2,1)S(1)}, bf16[16,2,64,128]{3,2,1,0:T(8,128)(2,1)S(1)}, u32[]{:S(2)}, u32[]{:S(2)}) collective-permute-start(bf16[16,2,64,128]{3,2,1,0:T(8,128)(2,1)S(1)} %get-tuple-element.45.s0), channel_id=1, source_target_pairs={{0,192},{4,68},{64,128},{68,4},{128,64},{132,196},{192,0},{196,132... | collective-permute-start | bytes 1572872 | tf_op jit(solution)/shard_map/ppermute | solution.py:397
  38.4 14.2 %collective-permute-start.14 = (bf16[16,2,64,128]{3,2,1,0:T(8,128)(2,1)S(1)}, bf16[16,2,64,128]{3,2,1,0:T(8,128)(2,1)S(1)}, u32[]{:S(2)}, u32[]{:S(2)}) collective-permute-start(bf16[16,2,64,128]{3,2,1,0:T(8,128)(2,1)S(1)} %get-tuple-element.46.s1), channel_id=1, source_target_pairs={{0,24},{4,12},{8,16},{12,4},{16,8},{20,28},{24,0},{28,20},{1,25},{... | collective-permute-start | bytes 1572872 | tf_op jit(solution)/shard_map/ppermute | solution.py:397
  39.9 4.5 %collective-permute-start.7 = (bf16[2,128,128]{2,1,0:T(8,128)(2,1)S(1)}, bf16[2,128,128]{2,1,0:T(8,128)(2,1)S(1)}, u32[]{:S(2)}, u32[]{:S(2)}) collective-permute-start(bf16[2,128,128]{2,1,0:T(8,128)(2,1)S(1)} %get-tuple-element.40), channel_id=1, source_target_pairs={{0,4},{4,0},{1,5},{5,1},{2,6},{6,2},{3,7},{7,3},{8,12},{12,8},{9,1... | collective-permute-start | bytes 196616 | tf_op jit(solution)/shard_map/ppermute | solution.py:435
  44.5 4.6 %collective-permute-start.9 = (bf16[2,128,128]{2,1,0:T(8,128)(2,1)S(1)}, bf16[2,128,128]{2,1,0:T(8,128)(2,1)S(1)}, u32[]{:S(2)}, u32[]{:S(2)}) collective-permute-start(bf16[2,128,128]{2,1,0:T(8,128)(2,1)S(1)} %get-tuple-element.41.g), channel_id=1, source_target_pairs={{0,32},{32,0},{1,33},{33,1},{2,34},{34,2},{3,35},{35,3},{4,36},{36... | collective-permute-start | bytes 196616 | tf_op jit(solution)/shard_map/ppermute | solution.py:437
  46.6 5.3 %collective-permute-start.10 = (bf16[2,128,128]{2,1,0:T(8,128)(2,1)S(1)}, bf16[2,128,128]{2,1,0:T(8,128)(2,1)S(1)}, u32[]{:S(2)}, u32[]{:S(2)}) collective-permute-start(bf16[2,128,128]{2,1,0:T(8,128)(2,1)S(1)} %get-tuple-element.42), channel_id=1, source_target_pairs={{0,40},{4,60},{8,32},{12,52},{16,56},{20,44},{24,48},{28,36},{32,8... | collective-permute-start | bytes 196616 | tf_op jit(solution)/shard_map/ppermute | solution.py:407
  46.6 6.1 %collective-permute-start.8 = (bf16[2,128,128]{2,1,0:T(8,128)(2,1)S(1)}, bf16[2,128,128]{2,1,0:T(8,128)(2,1)S(1)}, u32[]{:S(2)}, u32[]{:S(2)}) collective-permute-start(bf16[2,128,128]{2,1,0:T(8,128)(2,1)S(1)} %get-tuple-element.42), channel_id=1, source_target_pairs={{0,8},{4,28},{8,0},{12,20},{16,24},{20,12},{24,16},{28,4},{1,9},{5... | collective-permute-start | bytes 196616 | tf_op jit(solution)/shard_map/ppermute | solution.py:397
  55.8 9.3 %collective-permute-start.15 = (bf16[2,144,128]{2,1,0:T(8,128)(2,1)S(1)}, bf16[2,144,128]{2,1,0:T(8,128)(2,1)S(1)}, u32[]{:S(2)}, u32[]{:S(2)}) collective-permute-start(bf16[2,144,128]{2,1,0:T(8,128)(2,1)S(1)} %get-tuple-element.48), channel_id=1, source_target_pairs={{0,32},{32,0},{1,33},{33,1},{2,34},{34,2},{3,35},{35,3},{4,36},{36... | collective-permute-start | bytes 221192 | tf_op jit(solution)/shard_map/ppermute | solution.py:442
  57.0 8.1 %collective-permute-start.17 = (bf16[2,144,128]{2,1,0:T(8,128)(2,1)S(1)}, bf16[2,144,128]{2,1,0:T(8,128)(2,1)S(1)}, u32[]{:S(2)}, u32[]{:S(2)}) collective-permute-start(bf16[2,144,128]{2,1,0:T(8,128)(2,1)S(1)} %get-tuple-element.50), channel_id=1, source_target_pairs={{0,40},{4,60},{8,32},{12,52},{16,56},{20,44},{24,48},{28,36},{32,8... | collective-permute-start | bytes 221192 | tf_op jit(solution)/shard_map/ppermute | solution.py:407
  58.9 6.2 %collective-permute-start.16 = (bf16[2,144,128]{2,1,0:T(8,128)(2,1)S(1)}, bf16[2,144,128]{2,1,0:T(8,128)(2,1)S(1)}, u32[]{:S(2)}, u32[]{:S(2)}) collective-permute-start(bf16[2,144,128]{2,1,0:T(8,128)(2,1)S(1)} %get-tuple-element.49._), channel_id=1, source_target_pairs={{0,8},{4,28},{8,0},{12,20},{16,24},{20,12},{24,16},{28,4},{1,9},{5... | collective-permute-start | bytes 221192 | tf_op jit(solution)/shard_map/ppermute | solution.py:397
  65.1 1.5 %collective-permute-start.18 = (bf16[4,144,128]{2,1,0:T(8,128)(2,1)S(1)}, bf16[4,144,128]{2,1,0:T(8,128)(2,1)S(1)}, u32[]{:S(2)}, u32[]{:S(2)}) collective-permute-start(bf16[4,144,128]{2,1,0:T(8,128)(2,1)S(1)} %back.1), channel_id=1, source_target_pairs={{0,4},{4,0},{1,5},{5,1},{2,6},{6,2},{3,7},{7,3},{8,12},{12,8},{9,1... | collective-permute-start | bytes 442376 | tf_op jit(solution)/shard_map/ppermute | solution.py:446

commit v4 on v3

--- a/solution.py
+++ b/solution.py
@@ -1,3 +1,4 @@
+import functools
 import math
 
 import jax
@@ -60,23 +61,27 @@
     return (code[0] >> 3) ^ flips[j]
 
 
-def pack_kernel(heads, keys, values, x, shift, scale, own, next_, other, pay, sems):
+def pack_kernel(heads, keys, values, x, shift, scale, own, next_, other, pay, mods, sems):
     copies = []
 
     def copy(source, target):
         copies.append(pltpu.make_async_copy(source, target, sems.at[len(copies)]))
         copies[-1].start()
 
+    copy(shift, mods.at[0])
+    copy(scale, mods.at[1])
     copy(x, pay.at[:ROWS])
     for d, out in ((2, other.at[0]), (3, other.at[1]), (1, next_), (0, own)):
         cut = head_slice(heads, d)
         for i in range(IMG):
             for j, source in enumerate((keys, values)):
                 copy(source.at[i, :, cut], out.at[i, j])
+    for one in copies[:2]:
+        one.wait()
     pay[ROWS:] = jnp.zeros((16, PART), BF16)
-    pay[ROWS : ROWS + IMG] = shift[...]
-    pay[ROWS + IMG : ROWS + 2 * IMG] = scale[...]
-    for one in copies:
+    pay[ROWS : ROWS + IMG] = mods[0]
+    pay[ROWS + IMG : ROWS + 2 * IMG] = mods[1]
+    for one in copies[2:]:
         one.wait()
 
 
@@ -90,9 +95,9 @@
             jax.ShapeDtypeStruct((2,) + shape, BF16),
             jax.ShapeDtypeStruct((ROWS + 16, PART), BF16),
         ],
-        in_specs=[smem()] + hbm(3) + vmem(2),
+        in_specs=[smem()] + hbm(5),
         out_specs=vmem(4),
-        scratch_shapes=[pltpu.SemaphoreType.DMA((17,))],
+        scratch_shapes=[pltpu.VMEM((2, IMG, PART), BF16), pltpu.SemaphoreType.DMA((19,))],
         compiler_params=params(56),
         name="pack",
     )(heads, keys, values, x, shift, scale)
@@ -136,12 +141,38 @@
     )(*[v for g in groups for v in g], *deps)
 
 
+def hold(x0, own, gains):
+    def kernel(x_in, own_in, qg, kg, x_out, own_out, gains_out):
+        x_out[...] = x_in[...]
+        own_out[...] = own_in[...]
+        gains_out[:1] = qg[...]
+        gains_out[1:] = kg[...]
+
+    return pl.pallas_call(
+        kernel,
+        out_shape=[
+            jax.ShapeDtypeStruct(x0.shape, BF16),
+            jax.ShapeDtypeStruct(own.shape, BF16),
+            jax.ShapeDtypeStruct((2, HEAD), F32),
+        ],
+        in_specs=vmem(4),
+        out_specs=vmem(3),
+        compiler_params=params(8),
+        cost_estimate=pl.CostEstimate(flops=0, bytes_accessed=32 << 20, transcendentals=0),
+        name="hold",
+    )(x0, own, *gains)
+
+
+def mods_kernel(x, out):
+    out[...] = x[ROWS:]
+
+
 def pair_kernel(a, b, out):
     out[0] = a[...]
     out[1] = b[1]
 
 
-def stack_kernel(own, other, far, s0, s1):
+def stack_kernel(own, other, far, _, s0, s1):
     for i, s in enumerate((s0, s1)):
         s[0] = own[i]
         s[1] = other[0, i]
@@ -174,7 +205,7 @@
     return copies
 
 
-def project(xs, buffer, copies):
+def project_copied(xs, buffer, copies):
     acc = jnp.zeros((ROWS, COLS), F32)
     for j in range(4):
         copies[j].wait()
@@ -182,11 +213,19 @@
     return acc
 
 
+def project(code, xs, w):
+    acc = jnp.zeros((ROWS, COLS), F32)
+    for j in range(4):
+        rows = pl.ds(pl.multiple_of(rank_of(code, j) * PART, PART), PART)
+        acc += jnp.dot(xs[j], w[rows, :], preferred_element_type=F32)
+    return acc
+
+
 def head_norm(v, gain):
     return v * lax.rsqrt(jnp.mean(v * v, axis=-1, keepdims=True) + 1e-06) * gain
 
 
-def query_kernel(idx, x0, x1, x2, x3, wq, qg, own, next_, other, qa, xs, buffer, sems):
+def query_kernel(idx, x0, x1, x2, x3, m2, wq, qg, own, next_, other, qa, xs, buffer, sems):
     copies = weight_copies(idx, (wq,), (buffer,), sems)
     blocks = (x0, x1, x2, x3)
     total = sum(jnp.sum(b[:ROWS].astype(F32), axis=-1, keepdims=True) for b in blocks)
@@ -197,13 +236,13 @@
         square += jnp.sum(centred * centred, axis=-1, keepdims=True)
     rstd = lax.rsqrt(square / WIDTH + 1e-06)
     for j, b in enumerate(blocks):
-        mods = b[ROWS : ROWS + 16].astype(F32)
+        mods = (m2[...] if j == 2 else b[ROWS : ROWS + 16]).astype(F32)
         for i in range(IMG):
             rows = slice(i * TOK, (i + 1) * TOK)
             normed = (b[rows].astype(F32) - mean[rows]) * rstd[rows]
             out = normed * (1.0 + mods[IMG + i : IMG + i + 1, :]) + mods[i : i + 1, :]
             xs[j, rows, :] = out.astype(BF16)
-    acc = project(xs, buffer, copies)
+    acc = project_copied(xs, buffer, copies)
     for h in range(4):
         cut = slice(h * HEAD, (h + 1) * HEAD)
         qa[:, cut] = head_norm(acc[:, cut], qg[:1]).astype(BF16)
@@ -223,7 +262,7 @@
             jax.ShapeDtypeStruct((ROWS, COLS), BF16),
             jax.ShapeDtypeStruct((4, ROWS, PART), BF16),
         ],
-        in_specs=[smem()] + vmem(4) + hbm(1) + vmem(1),
+        in_specs=[smem()] + vmem(5) + hbm(1) + vmem(1),
         out_specs=vmem(5),
         scratch_shapes=[pltpu.VMEM((4, PART, COLS), BF16), pltpu.SemaphoreType.DMA((4,))],
         compiler_params=params(50),
@@ -234,27 +273,28 @@
     )(idx, *xs, wq, gain)
 
 
-def fresh_kernel(idx, xs, qa, wk, wv, kg, _, fk, fv, out, lse, kbuf, vbuf, sems):
-    copies = weight_copies(idx, (wk, wv), (kbuf, vbuf), sems)
-    acc = project(xs, kbuf, copies[:4])
+def fresh_kernel(idx, xs, qa, wk, wv, kg, _, fk, fv, out, lse):
+    acc = project(idx, xs, wk)
     for h in range(4):
         cut = slice(h * HEAD, (h + 1) * HEAD)
         fk[:, cut] = head_norm(acc[:, cut], kg[1:]).astype(BF16)
-    fv[...] = project(xs, vbuf, copies[4:]).astype(BF16)
-    lanes = lax.broadcasted_iota(jnp.int32, (TOK, HEAD), 1)
-    for i in range(IMG):
-        rows = slice(i * TOK, (i + 1) * TOK)
-        levels = jnp.zeros((TOK, HEAD), F32)
-        for h in range(4):
-            cut = slice(h * HEAD, (h + 1) * HEAD)
-            s = dot_t(qa[rows, cut], fk[rows, cut]) * SCORE
-            top = jnp.max(s, axis=-1, keepdims=True)
-            p = jnp.exp2(s - top)
-            total = jnp.sum(p, axis=-1, keepdims=True)
-            numer = jnp.dot(p.astype(BF16), fv[rows, cut], preferred_element_type=F32)
-            out[rows, cut] = numer / total
-            levels = jnp.where(lanes == h, top + jnp.log2(total), levels)
-        lse[rows, :] = levels
+    fv[...] = project(idx, xs, wv).astype(BF16)
+    shape = (ROWS, ROWS)
+    row_image = lax.broadcasted_iota(jnp.int32, shape, 0) // TOK
+    col_image = lax.broadcasted_iota(jnp.int32, shape, 1) // TOK
+    lanes = lax.broadcasted_iota(jnp.int32, (ROWS, HEAD), 1)
+    levels = jnp.zeros((ROWS, HEAD), F32)
+    for h in range(4):
+        cut = slice(h * HEAD, (h + 1) * HEAD)
+        s = dot_t(qa[:, cut], fk[:, cut]) * SCORE
+        s = jnp.where(row_image == col_image, s, -1e30)
+        top = jnp.max(s, axis=-1, keepdims=True)
+        p = jnp.exp2(s - top)
+        total = jnp.sum(p, axis=-1, keepdims=True)
+        numer = jnp.dot(p.astype(BF16), fv[:, cut], preferred_element_type=F32)
+        out[:, cut] = numer / total
+        levels = jnp.where(lanes == h, top + jnp.log2(total), levels)
+    lse[...] = levels
 
 
 def fresh(idx, xs, qa, wk, wv, gain, dep):
@@ -265,11 +305,9 @@
             jax.ShapeDtypeStruct((ROWS, COLS), F32),
             jax.ShapeDtypeStruct((ROWS, HEAD), F32),
         ],
-        in_specs=[smem()] + vmem(2) + hbm(2) + vmem(1) + anywhere(1),
+        in_specs=[smem()] + vmem(5) + anywhere(1),
         out_specs=vmem(4),
-        scratch_shapes=[pltpu.VMEM((4, PART, COLS), BF16)] * 2
-        + [pltpu.SemaphoreType.DMA((8,))],
-        compiler_params=params(50),
+        compiler_params=params(16),
         cost_estimate=pl.CostEstimate(
             flops=4 * ROWS * WIDTH * COLS, bytes_accessed=9 << 20, transcendentals=0
         ),
@@ -304,11 +342,12 @@
     return state
 
 
-def attend_kernel(g, n, gz, nd, s0, t0, s1, t1, *outs):
-    groups = (g, n, gz, nd)
+def attend_kernel(number, first_patch, *refs):
+    groups, (s0, t0, s1, t1) = refs[:number], refs[number : number + 4]
+    outs = refs[-number:]
     count = 2 * len(groups)
     shape = (count * TOK, 4 * TOK)
-    row_patch = lax.broadcasted_iota(jnp.int32, shape, 0) // TOK
+    row_patch = lax.broadcasted_iota(jnp.int32, shape, 0) // TOK + first_patch
     col_patch = lax.broadcasted_iota(jnp.int32, shape, 1) // TOK
     lse_rows = [jnp.zeros((1, HEAD), F32) for _ in range(count)]
     row = lax.broadcasted_iota(jnp.int32, (TOK, HEAD), 0)
@@ -339,15 +378,19 @@
         outs[d // 2][d % 2, ROWS : ROWS + 16, :] = tail.astype(BF16)
 
 
-def attend(groups, streams):
-    return pl.pallas_call(
-        attend_kernel,
-        out_shape=[jax.ShapeDtypeStruct((2, ROWS + 16, HEAD), BF16)] * 4,
-        in_specs=vmem(8),
-        out_specs=vmem(4),
+def attend(groups, streams, first_patch, deps=()):
+    number = len(groups)
+    return pl.pallas_call(
+        functools.partial(attend_kernel, number, first_patch),
+        out_shape=[jax.ShapeDtypeStruct((2, ROWS + 16, HEAD), BF16)] * number,
+        in_specs=vmem(number + 4) + anywhere(len(deps)),
+        out_specs=vmem(number),
         compiler_params=params(32),
+        cost_estimate=pl.CostEstimate(
+            flops=2 * number << 30, bytes_accessed=8 << 20, transcendentals=1 << 22
+        ),
         name="attend",
-    )(*groups, *streams)
+    )(*groups, *streams, *deps)
 
 
 def combine_kernel(heads, g, z, y, d, other, near_out, near_lse, att):
@@ -415,27 +458,33 @@
     own, next_, other, x0 = pack(
         code, stale_keys, stale_values, activations.reshape(ROWS, PART), mod_shift, mod_scale
     )
-    x1, x2 = swap(x0, "zh", 0), swap(x0, "zh", 1)
+    x1 = swap(x0, "zh", 0)
+    x2 = swap(activations.reshape(ROWS, PART), "zh", 1)
     other = lax.ppermute(other, "core", FLIP)
     shape = (IMG, 2, TOK, HEAD)
     (far,) = call(pair_kernel, "pair", 8, [(2,) + shape], (next_, other))
     far = swap(far, "y", 0)
-    s0, s1 = call(stack_kernel, "stack", 8, [(4,) + shape[1:]] * 2, (own, other, far))
     gains = (query_gain.reshape(1, HEAD), key_gain.reshape(1, HEAD))
-    s0, s1, x0, gains = join(
-        [(s0, swap(s0, "y", 1)), (s1, swap(s1, "x", 0)), (x0,), gains], (x1, x2)
+    x0, own, gains = hold(x0, own, gains)
+    s0, s1 = call(
+        stack_kernel, "stack", 8, [(4,) + shape[1:]] * 2, (own, other, far), (gains,)
     )
+    s0, s1 = join([(s0, swap(s0, "y", 1)), (s1, swap(s1, "x", 0))], (x1, x2))
     x3 = swap(x1, "zh", 1)
+    (m2,) = call(mods_kernel, "mods", 8, [(16, PART)], (x1,))
+    m2 = lax.ppermute(m2, "core", FLIP)
     own, next_, other, qa, xs = project_queries(
-        code, (x0, x1, x2, x3), w_query, gains
+        code, (x0, x1, x2, x3, m2), w_query, gains
     )
     s0, s1 = join([(s0, swap(s0, "x", 0)), (s1, swap(s1, "x", 1))], (own,))
     t0, t1 = swap(s0, "x", 1), swap(s1, "y", 1)
 
     other = lax.ppermute(other, "core", FLIP)
     g, n = call(query_pairs_kernel, "query_pairs", 8, [(2, ROWS, HEAD)] * 2, (own, next_, other))
-    groups = (g, swap(n, "y", 0), lax.ppermute(g, "zl", FLIP), diagonal(n))
-    pg, py, pz, pd = attend(groups, (s0, t0, s1, t1))
+    groups = (swap(n, "y", 0), lax.ppermute(g, "zl", FLIP), diagonal(n))
+    streams = (s0, t0, s1, t1)
+    py, pz, pd = attend(groups, streams, 2)
+    (pg,) = attend((g,), streams, 0, (py,))
     fk, fv, near_out, near_lse = fresh(
         code, xs, qa, w_key, w_value, gains, py
     )

time: 67.9 us -> 62.9 us (0.926)
  waiting for transfers between devices: 13.8 us -> 8.48 us
  starting transfers between devices: 34.1 us -> 36.6 us
  Pallas kernels: 14.9 us -> 12.8 us
    ppermute x12, waiting for transfers between devices: 8.79 us -> 2.69 us  [swap(): return lax.ppermute(value, names, perm)]
    ppermute x1 -> x2, starting transfers between devices: 2.08 us -> 5.7 us  [the longest x1 3.37 us: on_device(): groups = (swap(n, 'y', 0), lax.ppermute(g, 'zl', FLIP), diagonal(n))]
    pallas_call x1, Pallas kernels: 5.32 us -> 2.32 us  [fresh(): pl.pallas_call(fresh_kernel, out_shape=[jax.ShapeDtypeStruct((ROWS, COLS)...]
    pallas_call x1 -> x3, Pallas kernels: 3.15 us -> 4.09 us  [the longest x2 4.07 us: attend(): pl.pallas_call(functools.partial(attend_kernel, number, first_patch), out...]
    ppermute x2, starting transfers between devices: 6.97 us -> 6.04 us  [on_device(): other = lax.ppermute(other, 'core', FLIP)]
    ppermute x1 -> x2, waiting for transfers between devices: 0.01 us -> 0.86 us  [the longest x1 0.86 us: on_device(): m2 = lax.ppermute(m2, 'core', FLIP)]
    unnamed x10 -> x14, local copies, waits for them, and re-layouts: 3.94 us -> 3.96 us
  transfers between devices with their start and end apart: 19 -> 20, of which waited for: 7 -> 7; matrix products, arithmetic and copies ran while one was open for 0% -> 0% of each run, Pallas kernels for 12% -> 12%
where the time goes in v4:
time: 62.9 us; the launch traced here: 62.6 us
  starting transfers between devices  36.6 us (58%)
  Pallas kernels  12.8 us (20%)
  waiting for transfers between devices  8.48 us (13%)
  local copies, waits for them, and re-layouts  3.96 us (6%)
  between operations  0.79 us (1%)
    ppermute x12, starting transfers between devices, swap(): return lax.ppermute(value, names, perm)  21.6 us
    ppermute x2, starting transfers between devices, on_device(): other = lax.ppermute(other, 'core', FLIP)  6.04 us
    pallas_call x2, Pallas kernels, attend(): pl.pallas_call(functools.partial(attend_kernel, number, first_patch), out...  4.07 us
    unnamed x14, local copies, waits for them, and re-layouts  3.96 us
    ppermute x1, starting transfers between devices, on_device(): groups = (swap(n, 'y', 0), lax.ppermute(g, 'zl', FLIP), diagonal(n))  3.37 us
    pallas_call x1, Pallas kernels, project_queries(): pl.pallas_call(query_kernel, out_shape=[jax.ShapeDtypeStruct((ROWS, HEAD)...  3.23 us
    ppermute x2, waiting for transfers between devices, diagonal(): return lax.ppermute(value, ('zl', 'y', 'core'), perm)  2.84 us
    ppermute x12, waiting for transfers between devices, swap(): return lax.ppermute(value, names, perm)  2.69 us
  transfers between devices with their start and end apart: 20, of which 7 were waited for; matrix products, arithmetic and copies ran while one was open for 0% of the time, Pallas kernels for 12%

profile of v4, /device:TPU:1, one launch (start us, length us, event | category | flops | bytes accessed | tf_op | source)
XLA Modules:
  0.0 62.6 jit_solution(15487097199529753907)
XLA Ops:
  0.6 2.0 %pack.1 = (bf16[2,2,64,128]{3,2,1,0:T(8,128)(2,1)}, bf16[2,2,64,128]{3,2,1,0:T(8,128)(2,1)}, bf16[2,2,2,64,128]{4,3,2,1,0:T(8,128)(2,1)}, bf16[144,1024]{1,0:T(8,128)(2,1)}) custom-call(s32[1]{0:T(128)} %bitcast.heads.idx, bf16[2,64,512]{2,1,0:T(8,128)(2,1)} %keys.1, bf16[2,64,512]{2,1,0:T(8,128)(2,1)} %values.1, bf16[128,1024]{1,0:T(8,128)(2,1)} %bitcast.9, ...), custom_call_target="tpu_custom_call" | custom-call | tf_op jit(solution)/shard_map/pack/pallas_call | solution.py:90
  2.6 3.3 %collective-permute-start.5 = (bf16[2,2,2,64,128]{4,3,2,1,0:T(8,128)(2,1)}, bf16[2,2,2,64,128]{4,3,2,1,0:T(8,128)(2,1)S(1)}, u32[]{:S(2)}, u32[]{:S(2)}) collective-permute-start(bf16[2,2,2,64,128]{4,3,2,1,0:T(8,128)(2,1)} %get-tuple-element.39), channel_id=1, source_target_pairs={{0,4},{4,0},{1,5},{5,1},{2,6},{6,2},{3,7},{7,3},{8,12},{12,8},{9,1... | collective-permute-start | bytes 393224 | tf_op jit(solution)/shard_map/ppermute | solution.py:463
  5.9 4.3 %collective-permute-start = (bf16[144,1024]{1,0:T(8,128)(2,1)}, bf16[144,1024]{1,0:T(8,128)(2,1)S(1)}, u32[]{:S(2)}, u32[]{:S(2)}) collective-permute-start(bf16[144,1024]{1,0:T(8,128)(2,1)} %get-tuple-element.30.x_in), channel_id=1, source_target_pairs={{0,1},{4,7},{1,0},{5,6},{2,3},{6,5},{3,2},{7,4},{8,9},{12,15},{9,8... | collective-permute-start | bytes 884744 | tf_op jit(solution)/shard_map/ppermute | solution.py:440
  10.2 0.0 collective-permute-done.5.b.other
  10.2 0.0 copy-start.3
  10.2 0.8 %copy-done.3 = bf16[2,2,64,128]{3,2,1,0:T(8,128)(2,1)S(1)} copy-done((bf16[2,2,64,128]{3,2,1,0:T(8,128)(2,1)S(1)}, bf16[2,2,64,128]{3,2,1,0:T(8,128)(2,1)}, u32[]{:S(2)}) %copy-start.3) | copy-done | bytes 65560
  11.1 2.8 %collective-permute-start.6 = (bf16[2,2,2,64,128]{4,3,2,1,0:T(8,128)(2,1)S(1)}, bf16[2,2,2,64,128]{4,3,2,1,0:T(8,128)(2,1)S(1)}, u32[]{:S(2)}, u32[]{:S(2)}) collective-permute-start(bf16[2,2,2,64,128]{4,3,2,1,0:T(8,128)(2,1)S(1)} %pair.1), channel_id=1, source_target_pairs={{0,8},{4,28},{8,0},{12,20},{16,24},{20,12},{24,16},{28,4},{1,9},{5... | collective-permute-start | bytes 393224 | tf_op jit(solution)/shard_map/ppermute | solution.py:440
  13.9 1.2 %collective-permute-start.1 = (bf16[128,1024]{1,0:T(8,128)(2,1)}, bf16[128,1024]{1,0:T(8,128)(2,1)S(1)}, u32[]{:S(2)}, u32[]{:S(2)}) collective-permute-start(bf16[128,1024]{1,0:T(8,128)(2,1)} %bitcast.10), channel_id=1, source_target_pairs={{0,3},{4,5},{1,2},{5,4},{2,1},{6,7},{3,0},{7,6},{8,11},{12,13},{9,... | collective-permute-start | bytes 786440 | tf_op jit(solution)/shard_map/ppermute | solution.py:440
  15.1 0.0 copy-start.2
  15.1 1.0 %copy-done.2 = bf16[144,1024]{1,0:T(8,128)(2,1)S(1)} copy-done((bf16[144,1024]{1,0:T(8,128)(2,1)S(1)}, bf16[144,1024]{1,0:T(8,128)(2,1)}, u32[]{:S(2)}) %copy-start.2) | copy-done | bytes 294936
  16.0 0.0 copy-start.4
  16.0 0.8 %copy-done.4 = bf16[2,2,64,128]{3,2,1,0:T(8,128)(2,1)S(1)} copy-done((bf16[2,2,64,128]{3,2,1,0:T(8,128)(2,1)S(1)}, bf16[2,2,64,128]{3,2,1,0:T(8,128)(2,1)}, u32[]{:S(2)}) %copy-start.4) | copy-done | bytes 65560
  16.9 0.0 copy-start.5
  16.9 0.7 %copy-done.5 = f32[128]{0:T(128)S(1)} copy-done((f32[128]{0:T(128)S(1)}, f32[128]{0:T(128)}, u32[]{:S(2)}) %copy-start.5) | copy-done | bytes 536
  17.5 0.0 copy-start.6
  17.5 0.7 %copy-done.6 = f32[128]{0:T(128)S(1)} copy-done((f32[128]{0:T(128)S(1)}, f32[128]{0:T(128)}, u32[]{:S(2)}) %copy-start.6) | copy-done | bytes 536
  18.2 0.0 collective-permute-done.6.far
  18.3 0.1 collective-permute-start.7
  18.4 2.6 %collective-permute-start.8 = (bf16[4,2,64,128]{3,2,1,0:T(8,128)(2,1)S(1)}, bf16[4,2,64,128]{3,2,1,0:T(8,128)(2,1)S(1)}, u32[]{:S(2)}, u32[]{:S(2)}) collective-permute-start(bf16[4,2,64,128]{3,2,1,0:T(8,128)(2,1)S(1)} %get-tuple-element.42.refs_2_), channel_id=1, source_target_pairs={{0,64},{4,196},{64,0},{68,132},{128,192},{132,68},{192,128},{196,4... | collective-permute-start | bytes 393224 | tf_op jit(solution)/shard_map/ppermute | solution.py:440
  20.9 0.0 collective-permute-done.x.x1.refs_4_
  20.9 2.2 %collective-permute-start.2 = (bf16[144,1024]{1,0:T(8,128)(2,1)S(1)}, bf16[144,1024]{1,0:T(8,128)(2,1)S(1)}, u32[]{:S(2)}, u32[]{:S(2)}) collective-permute-start(bf16[144,1024]{1,0:T(8,128)(2,1)S(1)} %collective-permute-done.x.x1.refs_4_), channel_id=1, source_target_pairs={{0,3},{4,5},{1,2},{5,4},{2,1},{6,7},{3,0},{7,6},{8,11},{12,13},{9,... | collective-permute-start | bytes 884744 | tf_op jit(solution)/shard_map/ppermute | solution.py:440
  23.1 0.0 collective-permute-done.1.x2.refs_5_
  23.1 0.0 collective-permute-done.7.refs_1_
  23.1 0.5 collective-permute-done.8.refs_3_
  23.7 2.7 %collective-permute-start.9 = (bf16[8,2,64,128]{3,2,1,0:T(8,128)(2,1)S(1)}, bf16[8,2,64,128]{3,2,1,0:T(8,128)(2,1)S(1)}, u32[]{:S(2)}, u32[]{:S(2)}) collective-permute-start(bf16[8,2,64,128]{3,2,1,0:T(8,128)(2,1)S(1)} %get-tuple-element.43.refs_0_), channel_id=1, source_target_pairs={{0,64},{4,196},{64,0},{68,132},{128,192},{132,68},{192,128},{196,4... | collective-permute-start | bytes 786440 | tf_op jit(solution)/shard_map/ppermute | solution.py:440
  26.4 0.0 collective-permute-start.10
  26.4 2.3 %collective-permute-start.3 = (bf16[16,1024]{1,0:T(8,128)(2,1)S(1)}, bf16[16,1024]{1,0:T(8,128)(2,1)S(1)}, u32[]{:S(2)}, u32[]{:S(2)}) collective-permute-start(bf16[16,1024]{1,0:T(8,128)(2,1)S(1)} %mods.1), channel_id=1, source_target_pairs={{0,4},{4,0},{1,5},{5,1},{2,6},{6,2},{3,7},{7,3},{8,12},{12,8},{9,1... | collective-permute-start | bytes 98312 | tf_op jit(solution)/shard_map/ppermute | solution.py:475
  28.7 0.9 %collective-permute-done.3.m2 = bf16[16,1024]{1,0:T(8,128)(2,1)S(1)} collective-permute-done((bf16[16,1024]{1,0:T(8,128)(2,1)S(1)}, bf16[16,1024]{1,0:T(8,128)(2,1)S(1)}, u32[]{:S(2)}, u32[]{:S(2)}) %collective-permute-start.3) | collective-permute-done | bytes 32800 | tf_op jit(solution)/shard_map/ppermute | solution.py:475
  29.6 1.3 %collective-permute-done.2.x3 = bf16[144,1024]{1,0:T(8,128)(2,1)S(1)} collective-permute-done((bf16[144,1024]{1,0:T(8,128)(2,1)S(1)}, bf16[144,1024]{1,0:T(8,128)(2,1)S(1)}, u32[]{:S(2)}, u32[]{:S(2)}) %collective-permute-start.2) | collective-permute-done | bytes 294944 | tf_op jit(solution)/shard_map/ppermute | solution.py:440
  30.9 3.2 %queries.1 = (bf16[128,128]{1,0:T(8,128)(2,1)S(1)}, bf16[128,128]{1,0:T(8,128)(2,1)S(1)}, bf16[2,128,128]{2,1,0:T(8,128)(2,1)S(1)}, bf16[128,512]{1,0:T(8,128)(2,1)S(1)}, bf16[4,128,1024]{2,1,0:T(8,128)(2,1)S(1)}) custom-call(s32[1]{0:T(128)} %bitcast.heads.idx, bf16[144,1024]{1,0:T(8,128)(2,1)S(1)} %get-tuple-element.32.x0, ...), custom_call_target="tpu_custom_call" | custom-call | flops 536870912 | bytes 5242880 | tf_op jit(solution)/shard_map/queries/pallas_call | solution.py:256
  34.1 0.0 collective-permute-done.9.refs_1_
  34.1 0.0 collective-permute-done.10.refs_3_
  34.1 0.1 join.3
  34.2 1.8 %collective-permute-start.11 = (bf16[16,2,64,128]{3,2,1,0:T(8,128)(2,1)S(1)}, bf16[16,2,64,128]{3,2,1,0:T(8,128)(2,1)S(1)}, u32[]{:S(2)}, u32[]{:S(2)}) collective-permute-start(bf16[16,2,64,128]{3,2,1,0:T(8,128)(2,1)S(1)} %get-tuple-element.45.refs_3_.refs_1_), channel_id=1, source_target_pairs={{0,192},{4,68},{64,128},{68,4},{128,64},{132,196},{192,0},{196,132... | collective-permute-start | bytes 1572872 | tf_op jit(solution)/shard_map/ppermute | solution.py:440
  36.0 0.5 collective-permute-start.12
  36.5 2.7 %collective-permute-start.4 = (bf16[2,128,128]{2,1,0:T(8,128)(2,1)S(1)}, bf16[2,128,128]{2,1,0:T(8,128)(2,1)S(1)}, u32[]{:S(2)}, u32[]{:S(2)}) collective-permute-start(bf16[2,128,128]{2,1,0:T(8,128)(2,1)S(1)} %get-tuple-element.36), channel_id=1, source_target_pairs={{0,4},{4,0},{1,5},{5,1},{2,6},{6,2},{3,7},{7,3},{8,12},{12,8},{9,1... | collective-permute-start | bytes 196616 | tf_op jit(solution)/shard_map/ppermute | solution.py:482
  39.2 0.9 %collective-permute-done.4.other = bf16[2,128,128]{2,1,0:T(8,128)(2,1)S(1)} collective-permute-done((bf16[2,128,128]{2,1,0:T(8,128)(2,1)S(1)}, bf16[2,128,128]{2,1,0:T(8,128)(2,1)S(1)}, u32[]{:S(2)}, u32[]{:S(2)}) %collective-permute-start.4) | collective-permute-done | bytes 65568 | tf_op jit(solution)/shard_map/ppermute | solution.py:482
  40.1 3.4 %collective-permute-start.14 = (bf16[2,128,128]{2,1,0:T(8,128)(2,1)S(1)}, bf16[2,128,128]{2,1,0:T(8,128)(2,1)S(1)}, u32[]{:S(2)}, u32[]{:S(2)}) collective-permute-start(bf16[2,128,128]{2,1,0:T(8,128)(2,1)S(1)} %get-tuple-element.37.refs_0_), channel_id=1, source_target_pairs={{0,32},{32,0},{1,33},{33,1},{2,34},{34,2},{3,35},{35,3},{4,36},{36... | collective-permute-start | bytes 196616 | tf_op jit(solution)/shard_map/ppermute | solution.py:484
  43.5 0.1 collective-permute-start.15
  43.7 2.3 %collective-permute-start.13 = (bf16[2,128,128]{2,1,0:T(8,128)(2,1)S(1)}, bf16[2,128,128]{2,1,0:T(8,128)(2,1)S(1)}, u32[]{:S(2)}, u32[]{:S(2)}) collective-permute-start(bf16[2,128,128]{2,1,0:T(8,128)(2,1)S(1)} %get-tuple-element.47), channel_id=1, source_target_pairs={{0,8},{4,28},{8,0},{12,20},{16,24},{20,12},{24,16},{28,4},{1,9},{5... | collective-permute-start | bytes 196616 | tf_op jit(solution)/shard_map/ppermute | solution.py:440
  46.0 0.0 collective-permute-done.14.refs_1_
  46.0 2.8 %collective-permute-done.15.refs_2_ = bf16[2,128,128]{2,1,0:T(8,128)(2,1)S(1)} collective-permute-done((bf16[2,128,128]{2,1,0:T(8,128)(2,1)S(1)}, bf16[2,128,128]{2,1,0:T(8,128)(2,1)S(1)}, u32[]{:S(2)}, u32[]{:S(2)}) %collective-permute-start.15) | collective-permute-done | bytes 65568 | tf_op jit(solution)/shard_map/ppermute | solution.py:450
  48.8 0.9 %collective-permute-done.13.refs_0_ = bf16[2,128,128]{2,1,0:T(8,128)(2,1)S(1)} collective-permute-done((bf16[2,128,128]{2,1,0:T(8,128)(2,1)S(1)}, bf16[2,128,128]{2,1,0:T(8,128)(2,1)S(1)}, u32[]{:S(2)}, u32[]{:S(2)}) %collective-permute-start.13) | collective-permute-done | bytes 65568 | tf_op jit(solution)/shard_map/ppermute | solution.py:440
  49.7 0.0 collective-permute-done.11.refs_4_.refs_2_
  49.7 0.0 collective-permute-done.12.refs_6_.refs_4_
  49.7 0.0 copy-start.1
  49.8 2.5 %attend.2 = (bf16[2,144,128]{2,1,0:T(8,128)(2,1)S(1)}, bf16[2,144,128]{2,1,0:T(8,128)(2,1)S(1)}, bf16[2,144,128]{2,1,0:T(8,128)(2,1)S(1)}) custom-call(bf16[2,128,128]{2,1,0:T(8,128)(2,1)S(1)} %collective-permute-done.13.refs_0_, bf16[2,128,128]{2,1,0:T(8,128)(2,1)S(1)} %collective-permute-done.14.refs_1_, ...), custom_call_target="tpu_custom_call" | custom-call | flops 6442450944 | bytes 8388608 | tf_op jit(solution)/shard_map/attend/pallas_call | solution.py:383
  52.3 0.0 copy-start
  52.3 1.0 %collective-permute-start.16 = (bf16[2,144,128]{2,1,0:T(8,128)(2,1)S(1)}, bf16[2,144,128]{2,1,0:T(8,128)(2,1)S(1)}, u32[]{:S(2)}, u32[]{:S(2)}) collective-permute-start(bf16[2,144,128]{2,1,0:T(8,128)(2,1)S(1)} %get-tuple-element.49), channel_id=1, source_target_pairs={{0,32},{32,0},{1,33},{33,1},{2,34},{34,2},{3,35},{35,3},{4,36},{36... | collective-permute-start | bytes 221192 | tf_op jit(solution)/shard_map/ppermute | solution.py:491
  53.3 1.9 %collective-permute-start.18 = (bf16[2,144,128]{2,1,0:T(8,128)(2,1)S(1)}, bf16[2,144,128]{2,1,0:T(8,128)(2,1)S(1)}, u32[]{:S(2)}, u32[]{:S(2)}) collective-permute-start(bf16[2,144,128]{2,1,0:T(8,128)(2,1)S(1)} %get-tuple-element.50), channel_id=1, source_target_pairs={{0,40},{4,60},{8,32},{12,52},{16,56},{20,44},{24,48},{28,36},{32,8... | collective-permute-start | bytes 221192 | tf_op jit(solution)/shard_map/ppermute | solution.py:450
  55.2 1.0 %collective-permute-start.17 = (bf16[2,144,128]{2,1,0:T(8,128)(2,1)S(1)}, bf16[2,144,128]{2,1,0:T(8,128)(2,1)S(1)}, u32[]{:S(2)}, u32[]{:S(2)}) collective-permute-start(bf16[2,144,128]{2,1,0:T(8,128)(2,1)S(1)} %get-tuple-element.48.refs_5_._), channel_id=1, source_target_pairs={{0,8},{4,28},{8,0},{12,20},{16,24},{20,12},{24,16},{28,4},{1,9},{5... | collective-permute-start | bytes 221192 | tf_op jit(solution)/shard_map/ppermute | solution.py:440
  56.2 1.6 %attend.3.g = bf16[2,144,128]{2,1,0:T(8,128)(2,1)S(1)} custom-call(bf16[2,128,128]{2,1,0:T(8,128)(2,1)S(1)} %get-tuple-element.37.refs_0_, bf16[16,2,64,128]{3,2,1,0:T(8,128)(2,1)S(1)} %get-tuple-element.45.refs_3_.refs_1_, bf16[16,2,64,128]{3,2,1,0:T(8,128)(2,1)S(1)} %collective-permute-done.11.refs_4_.refs_2_, ...), custom_call_target="tpu_custom_call" | custom-call | flops 2147483648 | bytes 8388608 | tf_op jit(solution)/shard_map/attend/pallas_call | solution.py:383
  57.8 0.0 copy-done.1
  57.8 0.0 copy-done
  57.8 2.3 %fresh.1 = (bf16[128,512]{1,0:T(8,128)(2,1)}, bf16[128,512]{1,0:T(8,128)(2,1)}, f32[128,512]{1,0:T(8,128)S(1)}, f32[128,128]{1,0:T(8,128)S(1)}) custom-call(s32[1]{0:T(128)} %bitcast.heads.idx, bf16[4,128,1024]{2,1,0:T(8,128)(2,1)S(1)} %get-tuple-element.51.xs, bf16[128,512]{1,0:T(8,128)(2,1)S(1)} %get-tuple-element.52.qa, bf16[4096,512]{1,0:T(8,128)(2,1)S(1)} %copy-done, ...), custom_call_target="tpu_custom_call" | custom-call | flops 1073741824 | bytes 9437184 | tf_op jit(solution)/shard_map/fresh/pallas_call | solution.py:301
  60.1 0.0 collective-permute-done.16.z
  60.1 0.0 collective-permute-done.18.d
  60.1 0.0 collective-permute-done.17.y
  60.2 0.3 collective-permute-start.19
  60.4 1.2 %collective-permute-done.19.other = bf16[4,144,128]{2,1,0:T(8,128)(2,1)S(1)} collective-permute-done((bf16[4,144,128]{2,1,0:T(8,128)(2,1)S(1)}, bf16[4,144,128]{2,1,0:T(8,128)(2,1)S(1)}, u32[]{:S(2)}, u32[]{:S(2)}) %collective-permute-start.19) | collective-permute-done | bytes 147488 | tf_op jit(solution)/shard_map/ppermute | solution.py:495
  61.6 1.0 %combine.1 = bf16[128,512]{1,0:T(8,128)(2,1)} custom-call(s32[1]{0:T(128)} %bitcast.heads.idx, bf16[2,144,128]{2,1,0:T(8,128)(2,1)S(1)} %attend.3.g, bf16[2,144,128]{2,1,0:T(8,128)(2,1)S(1)} %collective-permute-done.16.z, bf16[2,144,128]{2,1,0:T(8,128)(2,1)S(1)} %collective-permute-done.17.y, bf16[2,144,128]{2,1,0:T(8,128)(2,1)S(1)} %collective-permute-done.18.d, ...), custom_call_target="tpu_custom_call" | custom-call | tf_op jit(solution)/shard_map/combine/pallas_call | solution.py:419
  (7 shorter events, 0.1 us)
Async XLA Ops:
  2.6 7.6 %collective-permute-start.5 = (bf16[2,2,2,64,128]{4,3,2,1,0:T(8,128)(2,1)}, bf16[2,2,2,64,128]{4,3,2,1,0:T(8,128)(2,1)S(1)}, u32[]{:S(2)}, u32[]{:S(2)}) collective-permute-start(bf16[2,2,2,64,128]{4,3,2,1,0:T(8,128)(2,1)} %get-tuple-element.39), channel_id=1, source_target_pairs={{0,4},{4,0},{1,5},{5,1},{2,6},{6,2},{3,7},{7,3},{8,12},{12,8},{9,1... | collective-permute-start | bytes 393224 | tf_op jit(solution)/shard_map/ppermute | solution.py:463
  5.9 15.0 %collective-permute-start = (bf16[144,1024]{1,0:T(8,128)(2,1)}, bf16[144,1024]{1,0:T(8,128)(2,1)S(1)}, u32[]{:S(2)}, u32[]{:S(2)}) collective-permute-start(bf16[144,1024]{1,0:T(8,128)(2,1)} %get-tuple-element.30.x_in), channel_id=1, source_target_pairs={{0,1},{4,7},{1,0},{5,6},{2,3},{6,5},{3,2},{7,4},{8,9},{12,15},{9,8... | collective-permute-start | bytes 884744 | tf_op jit(solution)/shard_map/ppermute | solution.py:440
  10.2 0.8 %copy-start.3 = (bf16[2,2,64,128]{3,2,1,0:T(8,128)(2,1)S(1)}, bf16[2,2,64,128]{3,2,1,0:T(8,128)(2,1)}, u32[]{:S(2)}) copy-start(bf16[2,2,64,128]{3,2,1,0:T(8,128)(2,1)} %get-tuple-element.40.a) | copy-start | bytes 196612
  11.1 7.1 %collective-permute-start.6 = (bf16[2,2,2,64,128]{4,3,2,1,0:T(8,128)(2,1)S(1)}, bf16[2,2,2,64,128]{4,3,2,1,0:T(8,128)(2,1)S(1)}, u32[]{:S(2)}, u32[]{:S(2)}) collective-permute-start(bf16[2,2,2,64,128]{4,3,2,1,0:T(8,128)(2,1)S(1)} %pair.1), channel_id=1, source_target_pairs={{0,8},{4,28},{8,0},{12,20},{16,24},{20,12},{24,16},{28,4},{1,9},{5... | collective-permute-start | bytes 393224 | tf_op jit(solution)/shard_map/ppermute | solution.py:440
  13.9 9.2 %collective-permute-start.1 = (bf16[128,1024]{1,0:T(8,128)(2,1)}, bf16[128,1024]{1,0:T(8,128)(2,1)S(1)}, u32[]{:S(2)}, u32[]{:S(2)}) collective-permute-start(bf16[128,1024]{1,0:T(8,128)(2,1)} %bitcast.10), channel_id=1, source_target_pairs={{0,3},{4,5},{1,2},{5,4},{2,1},{6,7},{3,0},{7,6},{8,11},{12,13},{9,... | collective-permute-start | bytes 786440 | tf_op jit(solution)/shard_map/ppermute | solution.py:440
  15.1 1.0 %copy-start.2 = (bf16[144,1024]{1,0:T(8,128)(2,1)S(1)}, bf16[144,1024]{1,0:T(8,128)(2,1)}, u32[]{:S(2)}) copy-start(bf16[144,1024]{1,0:T(8,128)(2,1)} %get-tuple-element.30.x_in) | copy-start | bytes 884740
  16.0 0.8 %copy-start.4 = (bf16[2,2,64,128]{3,2,1,0:T(8,128)(2,1)S(1)}, bf16[2,2,64,128]{3,2,1,0:T(8,128)(2,1)}, u32[]{:S(2)}) copy-start(bf16[2,2,64,128]{3,2,1,0:T(8,128)(2,1)} %get-tuple-element.31.own_in) | copy-start | bytes 196612
  16.9 0.7 %copy-start.5 = (f32[128]{0:T(128)S(1)}, f32[128]{0:T(128)}, u32[]{:S(2)}) copy-start(f32[128]{0:T(128)} %param.16) | copy-start | bytes 1540
  17.5 0.7 %copy-start.6 = (f32[128]{0:T(128)S(1)}, f32[128]{0:T(128)}, u32[]{:S(2)}) copy-start(f32[128]{0:T(128)} %param.17) | copy-start | bytes 1540
  18.3 4.9 %collective-permute-start.7 = (bf16[4,2,64,128]{3,2,1,0:T(8,128)(2,1)S(1)}, bf16[4,2,64,128]{3,2,1,0:T(8,128)(2,1)S(1)}, u32[]{:S(2)}, u32[]{:S(2)}) collective-permute-start(bf16[4,2,64,128]{3,2,1,0:T(8,128)(2,1)S(1)} %get-tuple-element.41.refs_0_), channel_id=1, source_target_pairs={{0,24},{4,12},{8,16},{12,4},{16,8},{20,28},{24,0},{28,20},{1,25},{... | collective-permute-start | bytes 393224 | tf_op jit(solution)/shard_map/ppermute | solution.py:440
  18.4 5.3 %collective-permute-start.8 = (bf16[4,2,64,128]{3,2,1,0:T(8,128)(2,1)S(1)}, bf16[4,2,64,128]{3,2,1,0:T(8,128)(2,1)S(1)}, u32[]{:S(2)}, u32[]{:S(2)}) collective-permute-start(bf16[4,2,64,128]{3,2,1,0:T(8,128)(2,1)S(1)} %get-tuple-element.42.refs_2_), channel_id=1, source_target_pairs={{0,64},{4,196},{64,0},{68,132},{128,192},{132,68},{192,128},{196,4... | collective-permute-start | bytes 393224 | tf_op jit(solution)/shard_map/ppermute | solution.py:440
  20.9 9.9 %collective-permute-start.2 = (bf16[144,1024]{1,0:T(8,128)(2,1)S(1)}, bf16[144,1024]{1,0:T(8,128)(2,1)S(1)}, u32[]{:S(2)}, u32[]{:S(2)}) collective-permute-start(bf16[144,1024]{1,0:T(8,128)(2,1)S(1)} %collective-permute-done.x.x1.refs_4_), channel_id=1, source_target_pairs={{0,3},{4,5},{1,2},{5,4},{2,1},{6,7},{3,0},{7,6},{8,11},{12,13},{9,... | collective-permute-start | bytes 884744 | tf_op jit(solution)/shard_map/ppermute | solution.py:440
  23.7 10.4 %collective-permute-start.9 = (bf16[8,2,64,128]{3,2,1,0:T(8,128)(2,1)S(1)}, bf16[8,2,64,128]{3,2,1,0:T(8,128)(2,1)S(1)}, u32[]{:S(2)}, u32[]{:S(2)}) collective-permute-start(bf16[8,2,64,128]{3,2,1,0:T(8,128)(2,1)S(1)} %get-tuple-element.43.refs_0_), channel_id=1, source_target_pairs={{0,64},{4,196},{64,0},{68,132},{128,192},{132,68},{192,128},{196,4... | collective-permute-start | bytes 786440 | tf_op jit(solution)/shard_map/ppermute | solution.py:440
  26.4 7.7 %collective-permute-start.10 = (bf16[8,2,64,128]{3,2,1,0:T(8,128)(2,1)S(1)}, bf16[8,2,64,128]{3,2,1,0:T(8,128)(2,1)S(1)}, u32[]{:S(2)}, u32[]{:S(2)}) collective-permute-start(bf16[8,2,64,128]{3,2,1,0:T(8,128)(2,1)S(1)} %get-tuple-element.44.refs_2_), channel_id=1, source_target_pairs={{0,192},{4,68},{64,128},{68,4},{128,64},{132,196},{192,0},{196,132... | collective-permute-start | bytes 786440 | tf_op jit(solution)/shard_map/ppermute | solution.py:440
  26.4 3.2 %collective-permute-start.3 = (bf16[16,1024]{1,0:T(8,128)(2,1)S(1)}, bf16[16,1024]{1,0:T(8,128)(2,1)S(1)}, u32[]{:S(2)}, u32[]{:S(2)}) collective-permute-start(bf16[16,1024]{1,0:T(8,128)(2,1)S(1)} %mods.1), channel_id=1, source_target_pairs={{0,4},{4,0},{1,5},{5,1},{2,6},{6,2},{3,7},{7,3},{8,12},{12,8},{9,1... | collective-permute-start | bytes 98312 | tf_op jit(solution)/shard_map/ppermute | solution.py:475
  34.2 15.6 %collective-permute-start.11 = (bf16[16,2,64,128]{3,2,1,0:T(8,128)(2,1)S(1)}, bf16[16,2,64,128]{3,2,1,0:T(8,128)(2,1)S(1)}, u32[]{:S(2)}, u32[]{:S(2)}) collective-permute-start(bf16[16,2,64,128]{3,2,1,0:T(8,128)(2,1)S(1)} %get-tuple-element.45.refs_3_.refs_1_), channel_id=1, source_target_pairs={{0,192},{4,68},{64,128},{68,4},{128,64},{132,196},{192,0},{196,132... | collective-permute-start | bytes 1572872 | tf_op jit(solution)/shard_map/ppermute | solution.py:440
  36.0 13.7 %collective-permute-start.12 = (bf16[16,2,64,128]{3,2,1,0:T(8,128)(2,1)S(1)}, bf16[16,2,64,128]{3,2,1,0:T(8,128)(2,1)S(1)}, u32[]{:S(2)}, u32[]{:S(2)}) collective-permute-start(bf16[16,2,64,128]{3,2,1,0:T(8,128)(2,1)S(1)} %get-tuple-element.46.refs_5_.refs_3_), channel_id=1, source_target_pairs={{0,24},{4,12},{8,16},{12,4},{16,8},{20,28},{24,0},{28,20},{1,25},{... | collective-permute-start | bytes 1572872 | tf_op jit(solution)/shard_map/ppermute | solution.py:440
  36.5 3.6 %collective-permute-start.4 = (bf16[2,128,128]{2,1,0:T(8,128)(2,1)S(1)}, bf16[2,128,128]{2,1,0:T(8,128)(2,1)S(1)}, u32[]{:S(2)}, u32[]{:S(2)}) collective-permute-start(bf16[2,128,128]{2,1,0:T(8,128)(2,1)S(1)} %get-tuple-element.36), channel_id=1, source_target_pairs={{0,4},{4,0},{1,5},{5,1},{2,6},{6,2},{3,7},{7,3},{8,12},{12,8},{9,1... | collective-permute-start | bytes 196616 | tf_op jit(solution)/shard_map/ppermute | solution.py:482
  40.1 5.9 %collective-permute-start.14 = (bf16[2,128,128]{2,1,0:T(8,128)(2,1)S(1)}, bf16[2,128,128]{2,1,0:T(8,128)(2,1)S(1)}, u32[]{:S(2)}, u32[]{:S(2)}) collective-permute-start(bf16[2,128,128]{2,1,0:T(8,128)(2,1)S(1)} %get-tuple-element.37.refs_0_), channel_id=1, source_target_pairs={{0,32},{32,0},{1,33},{33,1},{2,34},{34,2},{3,35},{35,3},{4,36},{36... | collective-permute-start | bytes 196616 | tf_op jit(solution)/shard_map/ppermute | solution.py:484
  43.5 5.3 %collective-permute-start.15 = (bf16[2,128,128]{2,1,0:T(8,128)(2,1)S(1)}, bf16[2,128,128]{2,1,0:T(8,128)(2,1)S(1)}, u32[]{:S(2)}, u32[]{:S(2)}) collective-permute-start(bf16[2,128,128]{2,1,0:T(8,128)(2,1)S(1)} %get-tuple-element.47), channel_id=1, source_target_pairs={{0,40},{4,60},{8,32},{12,52},{16,56},{20,44},{24,48},{28,36},{32,8... | collective-permute-start | bytes 196616 | tf_op jit(solution)/shard_map/ppermute | solution.py:450
  43.7 6.1 %collective-permute-start.13 = (bf16[2,128,128]{2,1,0:T(8,128)(2,1)S(1)}, bf16[2,128,128]{2,1,0:T(8,128)(2,1)S(1)}, u32[]{:S(2)}, u32[]{:S(2)}) collective-permute-start(bf16[2,128,128]{2,1,0:T(8,128)(2,1)S(1)} %get-tuple-element.47), channel_id=1, source_target_pairs={{0,8},{4,28},{8,0},{12,20},{16,24},{20,12},{24,16},{28,4},{1,9},{5... | collective-permute-start | bytes 196616 | tf_op jit(solution)/shard_map/ppermute | solution.py:440
  49.7 8.0 %copy-start.1 = (bf16[4096,512]{1,0:T(8,128)(2,1)S(1)}, bf16[4096,512]{1,0:T(8,128)(2,1)}, u32[]{:S(2)}) copy-start(bf16[4096,512]{1,0:T(8,128)(2,1)} %wv.1) | copy-start | bytes 12582916
  52.3 5.5 %copy-start = (bf16[4096,512]{1,0:T(8,128)(2,1)S(1)}, bf16[4096,512]{1,0:T(8,128)(2,1)}, u32[]{:S(2)}) copy-start(bf16[4096,512]{1,0:T(8,128)(2,1)} %wk.1) | copy-start | bytes 12582916
  52.3 7.9 %collective-permute-start.16 = (bf16[2,144,128]{2,1,0:T(8,128)(2,1)S(1)}, bf16[2,144,128]{2,1,0:T(8,128)(2,1)S(1)}, u32[]{:S(2)}, u32[]{:S(2)}) collective-permute-start(bf16[2,144,128]{2,1,0:T(8,128)(2,1)S(1)} %get-tuple-element.49), channel_id=1, source_target_pairs={{0,32},{32,0},{1,33},{33,1},{2,34},{34,2},{3,35},{35,3},{4,36},{36... | collective-permute-start | bytes 221192 | tf_op jit(solution)/shard_map/ppermute | solution.py:491
  53.3 6.8 %collective-permute-start.18 = (bf16[2,144,128]{2,1,0:T(8,128)(2,1)S(1)}, bf16[2,144,128]{2,1,0:T(8,128)(2,1)S(1)}, u32[]{:S(2)}, u32[]{:S(2)}) collective-permute-start(bf16[2,144,128]{2,1,0:T(8,128)(2,1)S(1)} %get-tuple-element.50), channel_id=1, source_target_pairs={{0,40},{4,60},{8,32},{12,52},{16,56},{20,44},{24,48},{28,36},{32,8... | collective-permute-start | bytes 221192 | tf_op jit(solution)/shard_map/ppermute | solution.py:450
  55.2 4.9 %collective-permute-start.17 = (bf16[2,144,128]{2,1,0:T(8,128)(2,1)S(1)}, bf16[2,144,128]{2,1,0:T(8,128)(2,1)S(1)}, u32[]{:S(2)}, u32[]{:S(2)}) collective-permute-start(bf16[2,144,128]{2,1,0:T(8,128)(2,1)S(1)} %get-tuple-element.48.refs_5_._), channel_id=1, source_target_pairs={{0,8},{4,28},{8,0},{12,20},{16,24},{20,12},{24,16},{28,4},{1,9},{5... | collective-permute-start | bytes 221192 | tf_op jit(solution)/shard_map/ppermute | solution.py:440
  60.2 1.5 %collective-permute-start.19 = (bf16[4,144,128]{2,1,0:T(8,128)(2,1)S(1)}, bf16[4,144,128]{2,1,0:T(8,128)(2,1)S(1)}, u32[]{:S(2)}, u32[]{:S(2)}) collective-permute-start(bf16[4,144,128]{2,1,0:T(8,128)(2,1)S(1)} %back.1), channel_id=1, source_target_pairs={{0,4},{4,0},{1,5},{5,1},{2,6},{6,2},{3,7},{7,3},{8,12},{12,8},{9,1... | collective-permute-start | bytes 442376 | tf_op jit(solution)/shard_map/ppermute | solution.py:495

commit v5 on v4

--- a/solution.py
+++ b/solution.py
@@ -103,13 +103,14 @@
     )(heads, keys, values, x, shift, scale)
 
 
-def call(kernel, name, limit, shapes, operands, deps=()):
+def call(kernel, name, limit, shapes, operands, deps=(), cost=None):
     return pl.pallas_call(
         kernel,
         out_shape=[jax.ShapeDtypeStruct(s, BF16) for s in shapes],
         in_specs=vmem(len(operands)) + anywhere(len(deps)),
         out_specs=vmem(len(shapes)),
         compiler_params=params(limit),
+        cost_estimate=cost,
         name=name,
     )(*operands, *deps)
 
@@ -192,27 +193,6 @@
         out[j] = r[1]
 
 
-def weight_copies(idx, sources, buffers, sems):
-    copies = []
-    for n, (source, buffer) in enumerate(zip(sources, buffers)):
-        for j in range(4):
-            rows = pl.ds(pl.multiple_of(rank_of(idx, j) * PART, PART), PART)
-            copies.append(
-                pltpu.make_async_copy(source.at[rows, :], buffer.at[j], sems.at[4 * n + j])
-            )
-    for copy in copies:
-        copy.start()
-    return copies
-
-
-def project_copied(xs, buffer, copies):
-    acc = jnp.zeros((ROWS, COLS), F32)
-    for j in range(4):
-        copies[j].wait()
-        acc += jnp.dot(xs[j], buffer[j], preferred_element_type=F32)
-    return acc
-
-
 def project(code, xs, w):
     acc = jnp.zeros((ROWS, COLS), F32)
     for j in range(4):
@@ -225,8 +205,7 @@
     return v * lax.rsqrt(jnp.mean(v * v, axis=-1, keepdims=True) + 1e-06) * gain
 
 
-def query_kernel(idx, x0, x1, x2, x3, m2, wq, qg, own, next_, other, qa, xs, buffer, sems):
-    copies = weight_copies(idx, (wq,), (buffer,), sems)
+def query_kernel(idx, x0, x1, x2, x3, m2, wq, qg, own, next_, other, qa, xs):
     blocks = (x0, x1, x2, x3)
     total = sum(jnp.sum(b[:ROWS].astype(F32), axis=-1, keepdims=True) for b in blocks)
     mean = total / WIDTH
@@ -242,7 +221,7 @@
             normed = (b[rows].astype(F32) - mean[rows]) * rstd[rows]
             out = normed * (1.0 + mods[IMG + i : IMG + i + 1, :]) + mods[i : i + 1, :]
             xs[j, rows, :] = out.astype(BF16)
-    acc = project_copied(xs, buffer, copies)
+    acc = project(idx, xs, wq)
     for h in range(4):
         cut = slice(h * HEAD, (h + 1) * HEAD)
         qa[:, cut] = head_norm(acc[:, cut], qg[:1]).astype(BF16)
@@ -262,10 +241,9 @@
             jax.ShapeDtypeStruct((ROWS, COLS), BF16),
             jax.ShapeDtypeStruct((4, ROWS, PART), BF16),
         ],
-        in_specs=[smem()] + vmem(5) + hbm(1) + vmem(1),
+        in_specs=[smem()] + vmem(7),
         out_specs=vmem(5),
-        scratch_shapes=[pltpu.VMEM((4, PART, COLS), BF16), pltpu.SemaphoreType.DMA((4,))],
-        compiler_params=params(50),
+        compiler_params=params(16),
         cost_estimate=pl.CostEstimate(
             flops=2 * ROWS * WIDTH * COLS, bytes_accessed=5 << 20, transcendentals=0
         ),
@@ -471,7 +449,8 @@
     )
     s0, s1 = join([(s0, swap(s0, "y", 1)), (s1, swap(s1, "x", 0))], (x1, x2))
     x3 = swap(x1, "zh", 1)
-    (m2,) = call(mods_kernel, "mods", 8, [(16, PART)], (x1,))
+    cost = pl.CostEstimate(flops=8 << 30, bytes_accessed=1 << 20, transcendentals=0)
+    (m2,) = call(mods_kernel, "mods", 8, [(16, PART)], (x1,), (), cost)
     m2 = lax.ppermute(m2, "core", FLIP)
     own, next_, other, qa, xs = project_queries(
         code, (x0, x1, x2, x3, m2), w_query, gains
@@ -480,7 +459,10 @@
     t0, t1 = swap(s0, "x", 1), swap(s1, "y", 1)
 
     other = lax.ppermute(other, "core", FLIP)
-    g, n = call(query_pairs_kernel, "query_pairs", 8, [(2, ROWS, HEAD)] * 2, (own, next_, other))
+    cost = pl.CostEstimate(flops=8 << 30, bytes_accessed=1 << 20, transcendentals=0)
+    g, n = call(
+        query_pairs_kernel, "query_pairs", 8, [(2, ROWS, HEAD)] * 2, (own, next_, other), (), cost
+    )
     groups = (swap(n, "y", 0), lax.ppermute(g, "zl", FLIP), diagonal(n))
     streams = (s0, t0, s1, t1)
     py, pz, pd = attend(groups, streams, 2)

time: 62.9 us -> 61.1 us (0.971)
  Pallas kernels: 12.8 us -> 11.1 us
  starting transfers between devices: 36.6 us -> 35.3 us
  waiting for transfers between devices: 8.48 us -> 9.73 us
    ppermute x12, starting transfers between devices: 21.6 us -> 18.2 us  [swap(): return lax.ppermute(value, names, perm)]
    ppermute x1, starting transfers between devices: 0.27 us -> 3.21 us  [on_device(): back = lax.ppermute(back, 'core', FLIP)]
    ppermute x2, starting transfers between devices: 6.04 us -> 3.81 us  [on_device(): other = lax.ppermute(other, 'core', FLIP)]
    ppermute x2, starting transfers between devices: 2.02 us -> 4.22 us  [diagonal(): return lax.ppermute(value, ('zl', 'y', 'core'), perm)]
    ppermute x12, waiting for transfers between devices: 2.69 us -> 4.77 us  [swap(): return lax.ppermute(value, names, perm)]
    pallas_call x1, Pallas kernels: 3.23 us -> 1.5 us  [project_queries(): pl.pallas_call(query_kernel, out_shape=[jax.ShapeDtypeStruct((ROWS, HEAD)...]
    ppermute x1, starting transfers between devices: 3.37 us -> 2.11 us  [on_device(): groups = (swap(n, 'y', 0), lax.ppermute(g, 'zl', FLIP), diagonal(n))]
    ppermute x2, waiting for transfers between devices: 0.9 us -> 0.01 us  [on_device(): other = lax.ppermute(other, 'core', FLIP)]
  transfers between devices with their start and end apart: 20 -> 20, of which waited for: 7 -> 8; matrix products, arithmetic and copies ran while one was open for 0% -> 0% of each run, Pallas kernels for 12% -> 9%
where the time goes in v5:
time: 61.1 us; the launch traced here: 60.9 us
  starting transfers between devices  35.3 us (58%)
  Pallas kernels  11.1 us (18%)
  waiting for transfers between devices  9.73 us (16%)
  local copies, waits for them, and re-layouts  3.96 us (6%)
  between operations  0.77 us (1%)
    ppermute x12, starting transfers between devices, swap(): return lax.ppermute(value, names, perm)  18.2 us
    ppermute x12, waiting for transfers between devices, swap(): return lax.ppermute(value, names, perm)  4.77 us
    ppermute x2, starting transfers between devices, diagonal(): return lax.ppermute(value, ('zl', 'y', 'core'), perm)  4.22 us
    pallas_call x2, Pallas kernels, attend(): pl.pallas_call(functools.partial(attend_kernel, number, first_patch), out...  4.11 us
    unnamed x16, local copies, waits for them, and re-layouts  3.96 us
    ppermute x2, starting transfers between devices, on_device(): other = lax.ppermute(other, 'core', FLIP)  3.81 us
    ppermute x1, starting transfers between devices, on_device(): back = lax.ppermute(back, 'core', FLIP)  3.21 us
    ppermute x2, waiting for transfers between devices, diagonal(): return lax.ppermute(value, ('zl', 'y', 'core'), perm)  3.08 us
  transfers between devices with their start and end apart: 20, of which 8 were waited for; matrix products, arithmetic and copies ran while one was open for 0% of the time, Pallas kernels for 9%

profile of v5, /device:TPU:1, one launch (start us, length us, event | category | flops | bytes accessed | tf_op | source)
XLA Modules:
  0.0 60.9 jit_solution(11486631043194531261)
XLA Ops:
  0.6 2.0 %pack.1 = (bf16[2,2,64,128]{3,2,1,0:T(8,128)(2,1)}, bf16[2,2,64,128]{3,2,1,0:T(8,128)(2,1)}, bf16[2,2,2,64,128]{4,3,2,1,0:T(8,128)(2,1)}, bf16[144,1024]{1,0:T(8,128)(2,1)}) custom-call(s32[1]{0:T(128)} %bitcast.heads.idx, bf16[2,64,512]{2,1,0:T(8,128)(2,1)} %keys.1, bf16[2,64,512]{2,1,0:T(8,128)(2,1)} %values.1, bf16[128,1024]{1,0:T(8,128)(2,1)} %bitcast.9, ...), custom_call_target="tpu_custom_call" | custom-call | tf_op jit(solution)/shard_map/pack/pallas_call | solution.py:90
  2.6 3.3 %collective-permute-start.5 = (bf16[2,2,2,64,128]{4,3,2,1,0:T(8,128)(2,1)}, bf16[2,2,2,64,128]{4,3,2,1,0:T(8,128)(2,1)S(1)}, u32[]{:S(2)}, u32[]{:S(2)}) collective-permute-start(bf16[2,2,2,64,128]{4,3,2,1,0:T(8,128)(2,1)} %get-tuple-element.39), channel_id=1, source_target_pairs={{0,4},{4,0},{1,5},{5,1},{2,6},{6,2},{3,7},{7,3},{8,12},{12,8},{9,1... | collective-permute-start | bytes 393224 | tf_op jit(solution)/shard_map/ppermute | solution.py:441
  6.0 4.3 %collective-permute-start = (bf16[144,1024]{1,0:T(8,128)(2,1)}, bf16[144,1024]{1,0:T(8,128)(2,1)S(1)}, u32[]{:S(2)}, u32[]{:S(2)}) collective-permute-start(bf16[144,1024]{1,0:T(8,128)(2,1)} %get-tuple-element.30.x_in), channel_id=1, source_target_pairs={{0,1},{4,7},{1,0},{5,6},{2,3},{6,5},{3,2},{7,4},{8,9},{12,15},{9,8... | collective-permute-start | bytes 884744 | tf_op jit(solution)/shard_map/ppermute | solution.py:418
  10.3 0.0 collective-permute-done.5.b.other
  10.3 0.0 copy-start.4
  10.3 0.8 %copy-done.4 = bf16[2,2,64,128]{3,2,1,0:T(8,128)(2,1)S(1)} copy-done((bf16[2,2,64,128]{3,2,1,0:T(8,128)(2,1)S(1)}, bf16[2,2,64,128]{3,2,1,0:T(8,128)(2,1)}, u32[]{:S(2)}) %copy-start.4) | copy-done | bytes 65560
  11.1 2.8 %collective-permute-start.6 = (bf16[2,2,2,64,128]{4,3,2,1,0:T(8,128)(2,1)S(1)}, bf16[2,2,2,64,128]{4,3,2,1,0:T(8,128)(2,1)S(1)}, u32[]{:S(2)}, u32[]{:S(2)}) collective-permute-start(bf16[2,2,2,64,128]{4,3,2,1,0:T(8,128)(2,1)S(1)} %pair.1), channel_id=1, source_target_pairs={{0,8},{4,28},{8,0},{12,20},{16,24},{20,12},{24,16},{28,4},{1,9},{5... | collective-permute-start | bytes 393224 | tf_op jit(solution)/shard_map/ppermute | solution.py:418
  13.9 1.2 %collective-permute-start.1 = (bf16[128,1024]{1,0:T(8,128)(2,1)}, bf16[128,1024]{1,0:T(8,128)(2,1)S(1)}, u32[]{:S(2)}, u32[]{:S(2)}) collective-permute-start(bf16[128,1024]{1,0:T(8,128)(2,1)} %bitcast.10), channel_id=1, source_target_pairs={{0,3},{4,5},{1,2},{5,4},{2,1},{6,7},{3,0},{7,6},{8,11},{12,13},{9,... | collective-permute-start | bytes 786440 | tf_op jit(solution)/shard_map/ppermute | solution.py:418
  15.1 0.0 copy-start.3
  15.1 1.0 %copy-done.3 = bf16[144,1024]{1,0:T(8,128)(2,1)S(1)} copy-done((bf16[144,1024]{1,0:T(8,128)(2,1)S(1)}, bf16[144,1024]{1,0:T(8,128)(2,1)}, u32[]{:S(2)}) %copy-start.3) | copy-done | bytes 294936
  16.1 0.0 copy-start.5
  16.1 0.8 %copy-done.5 = bf16[2,2,64,128]{3,2,1,0:T(8,128)(2,1)S(1)} copy-done((bf16[2,2,64,128]{3,2,1,0:T(8,128)(2,1)S(1)}, bf16[2,2,64,128]{3,2,1,0:T(8,128)(2,1)}, u32[]{:S(2)}) %copy-start.5) | copy-done | bytes 65560
  16.9 0.0 copy-start.6
  16.9 0.7 %copy-done.6 = f32[128]{0:T(128)S(1)} copy-done((f32[128]{0:T(128)S(1)}, f32[128]{0:T(128)}, u32[]{:S(2)}) %copy-start.6) | copy-done | bytes 536
  17.6 0.0 copy-start.7
  17.6 0.7 %copy-done.7 = f32[128]{0:T(128)S(1)} copy-done((f32[128]{0:T(128)S(1)}, f32[128]{0:T(128)}, u32[]{:S(2)}) %copy-start.7) | copy-done | bytes 536
  18.2 0.0 collective-permute-done.6.far
  18.3 0.1 collective-permute-start.7
  18.4 2.6 %collective-permute-start.8 = (bf16[4,2,64,128]{3,2,1,0:T(8,128)(2,1)S(1)}, bf16[4,2,64,128]{3,2,1,0:T(8,128)(2,1)S(1)}, u32[]{:S(2)}, u32[]{:S(2)}) collective-permute-start(bf16[4,2,64,128]{3,2,1,0:T(8,128)(2,1)S(1)} %get-tuple-element.42.refs_2_), channel_id=1, source_target_pairs={{0,64},{4,196},{64,0},{68,132},{128,192},{132,68},{192,128},{196,4... | collective-permute-start | bytes 393224 | tf_op jit(solution)/shard_map/ppermute | solution.py:418
  20.9 0.0 collective-permute-done.x.x1.refs_4_
  21.0 2.2 %collective-permute-start.2 = (bf16[144,1024]{1,0:T(8,128)(2,1)S(1)}, bf16[144,1024]{1,0:T(8,128)(2,1)S(1)}, u32[]{:S(2)}, u32[]{:S(2)}) collective-permute-start(bf16[144,1024]{1,0:T(8,128)(2,1)S(1)} %collective-permute-done.x.x1.refs_4_), channel_id=1, source_target_pairs={{0,3},{4,5},{1,2},{5,4},{2,1},{6,7},{3,0},{7,6},{8,11},{12,13},{9,... | collective-permute-start | bytes 884744 | tf_op jit(solution)/shard_map/ppermute | solution.py:418
  23.2 0.0 collective-permute-done.1.x2.refs_5_
  23.2 0.0 collective-permute-done.7.refs_1_
  23.2 0.5 collective-permute-done.8.refs_3_
  23.7 2.7 %collective-permute-start.9 = (bf16[8,2,64,128]{3,2,1,0:T(8,128)(2,1)S(1)}, bf16[8,2,64,128]{3,2,1,0:T(8,128)(2,1)S(1)}, u32[]{:S(2)}, u32[]{:S(2)}) collective-permute-start(bf16[8,2,64,128]{3,2,1,0:T(8,128)(2,1)S(1)} %get-tuple-element.43.refs_0_), channel_id=1, source_target_pairs={{0,64},{4,196},{64,0},{68,132},{128,192},{132,68},{192,128},{196,4... | collective-permute-start | bytes 786440 | tf_op jit(solution)/shard_map/ppermute | solution.py:418
  26.4 0.0 copy-start
  26.4 0.0 collective-permute-start.10
  26.4 2.3 %collective-permute-start.3 = (bf16[16,1024]{1,0:T(8,128)(2,1)S(1)}, bf16[16,1024]{1,0:T(8,128)(2,1)S(1)}, u32[]{:S(2)}, u32[]{:S(2)}) collective-permute-start(bf16[16,1024]{1,0:T(8,128)(2,1)S(1)} %mods.1), channel_id=1, source_target_pairs={{0,4},{4,0},{1,5},{5,1},{2,6},{6,2},{3,7},{7,3},{8,12},{12,8},{9,1... | collective-permute-start | bytes 98312 | tf_op jit(solution)/shard_map/ppermute | solution.py:454
  28.7 0.9 %collective-permute-done.3.m2 = bf16[16,1024]{1,0:T(8,128)(2,1)S(1)} collective-permute-done((bf16[16,1024]{1,0:T(8,128)(2,1)S(1)}, bf16[16,1024]{1,0:T(8,128)(2,1)S(1)}, u32[]{:S(2)}, u32[]{:S(2)}) %collective-permute-start.3) | collective-permute-done | bytes 32800 | tf_op jit(solution)/shard_map/ppermute | solution.py:454
  29.6 1.3 %collective-permute-done.2.x3 = bf16[144,1024]{1,0:T(8,128)(2,1)S(1)} collective-permute-done((bf16[144,1024]{1,0:T(8,128)(2,1)S(1)}, bf16[144,1024]{1,0:T(8,128)(2,1)S(1)}, u32[]{:S(2)}, u32[]{:S(2)}) %collective-permute-start.2) | collective-permute-done | bytes 294944 | tf_op jit(solution)/shard_map/ppermute | solution.py:418
  30.9 0.0 copy-done
  30.9 1.5 %queries.1 = (bf16[128,128]{1,0:T(8,128)(2,1)S(1)}, bf16[128,128]{1,0:T(8,128)(2,1)S(1)}, bf16[2,128,128]{2,1,0:T(8,128)(2,1)S(1)}, bf16[128,512]{1,0:T(8,128)(2,1)S(1)}, bf16[4,128,1024]{2,1,0:T(8,128)(2,1)S(1)}) custom-call(s32[1]{0:T(128)} %bitcast.heads.idx, bf16[144,1024]{1,0:T(8,128)(2,1)S(1)} %get-tuple-element.32.x0, ...), custom_call_target="tpu_custom_call" | custom-call | flops 536870912 | bytes 5242880 | tf_op jit(solution)/shard_map/queries/pallas_call | solution.py:235
  32.4 0.5 collective-permute-start.4
  32.9 0.0 collective-permute-done.9.refs_1_
  32.9 1.0 %collective-permute-done.10.refs_3_ = bf16[8,2,64,128]{3,2,1,0:T(8,128)(2,1)S(1)} collective-permute-done((bf16[8,2,64,128]{3,2,1,0:T(8,128)(2,1)S(1)}, bf16[8,2,64,128]{3,2,1,0:T(8,128)(2,1)S(1)}, u32[]{:S(2)}, u32[]{:S(2)}) %collective-permute-start.10) | collective-permute-done | bytes 262176 | tf_op jit(solution)/shard_map/ppermute | solution.py:418
  33.8 0.1 join.3
  33.9 1.1 %collective-permute-start.11 = (bf16[16,2,64,128]{3,2,1,0:T(8,128)(2,1)S(1)}, bf16[16,2,64,128]{3,2,1,0:T(8,128)(2,1)S(1)}, u32[]{:S(2)}, u32[]{:S(2)}) collective-permute-start(bf16[16,2,64,128]{3,2,1,0:T(8,128)(2,1)S(1)} %get-tuple-element.45.refs_3_.refs_1_), channel_id=1, source_target_pairs={{0,192},{4,68},{64,128},{68,4},{128,64},{132,196},{192,0},{196,132... | collective-permute-start | bytes 1572872 | tf_op jit(solution)/shard_map/ppermute | solution.py:418
  35.0 0.4 collective-permute-start.12
  35.5 0.0 collective-permute-done.4.other
  35.5 2.1 %collective-permute-start.14 = (bf16[2,128,128]{2,1,0:T(8,128)(2,1)S(1)}, bf16[2,128,128]{2,1,0:T(8,128)(2,1)S(1)}, u32[]{:S(2)}, u32[]{:S(2)}) collective-permute-start(bf16[2,128,128]{2,1,0:T(8,128)(2,1)S(1)} %get-tuple-element.37.refs_0_), channel_id=1, source_target_pairs={{0,32},{32,0},{1,33},{33,1},{2,34},{34,2},{3,35},{35,3},{4,36},{36... | collective-permute-start | bytes 196616 | tf_op jit(solution)/shard_map/ppermute | solution.py:466
  37.6 1.9 %collective-permute-start.15 = (bf16[2,128,128]{2,1,0:T(8,128)(2,1)S(1)}, bf16[2,128,128]{2,1,0:T(8,128)(2,1)S(1)}, u32[]{:S(2)}, u32[]{:S(2)}) collective-permute-start(bf16[2,128,128]{2,1,0:T(8,128)(2,1)S(1)} %get-tuple-element.47), channel_id=1, source_target_pairs={{0,40},{4,60},{8,32},{12,52},{16,56},{20,44},{24,48},{28,36},{32,8... | collective-permute-start | bytes 196616 | tf_op jit(solution)/shard_map/ppermute | solution.py:428
  39.5 0.6 collective-permute-start.13
  40.1 0.0 collective-permute-done.14.refs_1_
  40.1 3.1 %collective-permute-done.15.refs_2_ = bf16[2,128,128]{2,1,0:T(8,128)(2,1)S(1)} collective-permute-done((bf16[2,128,128]{2,1,0:T(8,128)(2,1)S(1)}, bf16[2,128,128]{2,1,0:T(8,128)(2,1)S(1)}, u32[]{:S(2)}, u32[]{:S(2)}) %collective-permute-start.15) | collective-permute-done | bytes 65568 | tf_op jit(solution)/shard_map/ppermute | solution.py:428
  43.2 1.7 %collective-permute-done.13.refs_0_ = bf16[2,128,128]{2,1,0:T(8,128)(2,1)S(1)} collective-permute-done((bf16[2,128,128]{2,1,0:T(8,128)(2,1)S(1)}, bf16[2,128,128]{2,1,0:T(8,128)(2,1)S(1)}, u32[]{:S(2)}, u32[]{:S(2)}) %collective-permute-start.13) | collective-permute-done | bytes 65568 | tf_op jit(solution)/shard_map/ppermute | solution.py:418
  44.9 0.0 collective-permute-done.11.refs_4_.refs_2_
  44.9 0.0 collective-permute-done.12.refs_6_.refs_4_
  44.9 0.0 copy-start.2
  44.9 2.5 %attend.2 = (bf16[2,144,128]{2,1,0:T(8,128)(2,1)S(1)}, bf16[2,144,128]{2,1,0:T(8,128)(2,1)S(1)}, bf16[2,144,128]{2,1,0:T(8,128)(2,1)S(1)}) custom-call(bf16[2,128,128]{2,1,0:T(8,128)(2,1)S(1)} %collective-permute-done.13.refs_0_, bf16[2,128,128]{2,1,0:T(8,128)(2,1)S(1)} %collective-permute-done.14.refs_1_, ...), custom_call_target="tpu_custom_call" | custom-call | flops 6442450944 | bytes 8388608 | tf_op jit(solution)/shard_map/attend/pallas_call | solution.py:361
  47.5 0.0 copy-start.1
  47.5 1.4 %collective-permute-start.16 = (bf16[2,144,128]{2,1,0:T(8,128)(2,1)S(1)}, bf16[2,144,128]{2,1,0:T(8,128)(2,1)S(1)}, u32[]{:S(2)}, u32[]{:S(2)}) collective-permute-start(bf16[2,144,128]{2,1,0:T(8,128)(2,1)S(1)} %get-tuple-element.49), channel_id=1, source_target_pairs={{0,32},{32,0},{1,33},{33,1},{2,34},{34,2},{3,35},{35,3},{4,36},{36... | collective-permute-start | bytes 221192 | tf_op jit(solution)/shard_map/ppermute | solution.py:473
  48.9 2.3 %collective-permute-start.18 = (bf16[2,144,128]{2,1,0:T(8,128)(2,1)S(1)}, bf16[2,144,128]{2,1,0:T(8,128)(2,1)S(1)}, u32[]{:S(2)}, u32[]{:S(2)}) collective-permute-start(bf16[2,144,128]{2,1,0:T(8,128)(2,1)S(1)} %get-tuple-element.50), channel_id=1, source_target_pairs={{0,40},{4,60},{8,32},{12,52},{16,56},{20,44},{24,48},{28,36},{32,8... | collective-permute-start | bytes 221192 | tf_op jit(solution)/shard_map/ppermute | solution.py:428
  51.2 0.2 collective-permute-start.17
  51.4 1.6 %attend.3.g = bf16[2,144,128]{2,1,0:T(8,128)(2,1)S(1)} custom-call(bf16[2,128,128]{2,1,0:T(8,128)(2,1)S(1)} %get-tuple-element.37.refs_0_, bf16[16,2,64,128]{3,2,1,0:T(8,128)(2,1)S(1)} %get-tuple-element.45.refs_3_.refs_1_, bf16[16,2,64,128]{3,2,1,0:T(8,128)(2,1)S(1)} %collective-permute-done.11.refs_4_.refs_2_, ...), custom_call_target="tpu_custom_call" | custom-call | flops 2147483648 | bytes 8388608 | tf_op jit(solution)/shard_map/attend/pallas_call | solution.py:361
  53.0 0.0 copy-done.2
  53.0 0.0 copy-done.1
  53.0 2.3 %fresh.1 = (bf16[128,512]{1,0:T(8,128)(2,1)}, bf16[128,512]{1,0:T(8,128)(2,1)}, f32[128,512]{1,0:T(8,128)S(1)}, f32[128,128]{1,0:T(8,128)S(1)}) custom-call(s32[1]{0:T(128)} %bitcast.heads.idx, bf16[4,128,1024]{2,1,0:T(8,128)(2,1)S(1)} %get-tuple-element.51.xs, bf16[128,512]{1,0:T(8,128)(2,1)S(1)} %get-tuple-element.52.qa, bf16[4096,512]{1,0:T(8,128)(2,1)S(1)} %copy-done.1, ...), custom_call_target="tpu_custom_call" | custom-call | flops 1073741824 | bytes 9437184 | tf_op jit(solution)/shard_map/fresh/pallas_call | solution.py:279
  55.3 0.0 collective-permute-done.16.z
  55.3 0.0 collective-permute-done.18.d
  55.3 0.3 collective-permute-done.17.y
  55.7 3.2 %collective-permute-start.19 = (bf16[4,144,128]{2,1,0:T(8,128)(2,1)S(1)}, bf16[4,144,128]{2,1,0:T(8,128)(2,1)S(1)}, u32[]{:S(2)}, u32[]{:S(2)}) collective-permute-start(bf16[4,144,128]{2,1,0:T(8,128)(2,1)S(1)} %back.1), channel_id=1, source_target_pairs={{0,4},{4,0},{1,5},{5,1},{2,6},{6,2},{3,7},{7,3},{8,12},{12,8},{9,1... | collective-permute-start | bytes 442376 | tf_op jit(solution)/shard_map/ppermute | solution.py:477
  58.9 1.0 %collective-permute-done.19.other = bf16[4,144,128]{2,1,0:T(8,128)(2,1)S(1)} collective-permute-done((bf16[4,144,128]{2,1,0:T(8,128)(2,1)S(1)}, bf16[4,144,128]{2,1,0:T(8,128)(2,1)S(1)}, u32[]{:S(2)}, u32[]{:S(2)}) %collective-permute-start.19) | collective-permute-done | bytes 147488 | tf_op jit(solution)/shard_map/ppermute | solution.py:477
  59.9 1.0 %combine.1 = bf16[128,512]{1,0:T(8,128)(2,1)} custom-call(s32[1]{0:T(128)} %bitcast.heads.idx, bf16[2,144,128]{2,1,0:T(8,128)(2,1)S(1)} %attend.3.g, bf16[2,144,128]{2,1,0:T(8,128)(2,1)S(1)} %collective-permute-done.16.z, bf16[2,144,128]{2,1,0:T(8,128)(2,1)S(1)} %collective-permute-done.17.y, bf16[2,144,128]{2,1,0:T(8,128)(2,1)S(1)} %collective-permute-done.18.d, ...), custom_call_target="tpu_custom_call" | custom-call | tf_op jit(solution)/shard_map/combine/pallas_call | solution.py:397
  (7 shorter events, 0.1 us)
Async XLA Ops:
  2.6 7.6 %collective-permute-start.5 = (bf16[2,2,2,64,128]{4,3,2,1,0:T(8,128)(2,1)}, bf16[2,2,2,64,128]{4,3,2,1,0:T(8,128)(2,1)S(1)}, u32[]{:S(2)}, u32[]{:S(2)}) collective-permute-start(bf16[2,2,2,64,128]{4,3,2,1,0:T(8,128)(2,1)} %get-tuple-element.39), channel_id=1, source_target_pairs={{0,4},{4,0},{1,5},{5,1},{2,6},{6,2},{3,7},{7,3},{8,12},{12,8},{9,1... | collective-permute-start | bytes 393224 | tf_op jit(solution)/shard_map/ppermute | solution.py:441
  6.0 15.0 %collective-permute-start = (bf16[144,1024]{1,0:T(8,128)(2,1)}, bf16[144,1024]{1,0:T(8,128)(2,1)S(1)}, u32[]{:S(2)}, u32[]{:S(2)}) collective-permute-start(bf16[144,1024]{1,0:T(8,128)(2,1)} %get-tuple-element.30.x_in), channel_id=1, source_target_pairs={{0,1},{4,7},{1,0},{5,6},{2,3},{6,5},{3,2},{7,4},{8,9},{12,15},{9,8... | collective-permute-start | bytes 884744 | tf_op jit(solution)/shard_map/ppermute | solution.py:418
  10.3 0.8 %copy-start.4 = (bf16[2,2,64,128]{3,2,1,0:T(8,128)(2,1)S(1)}, bf16[2,2,64,128]{3,2,1,0:T(8,128)(2,1)}, u32[]{:S(2)}) copy-start(bf16[2,2,64,128]{3,2,1,0:T(8,128)(2,1)} %get-tuple-element.40.a) | copy-start | bytes 196612
  11.1 7.1 %collective-permute-start.6 = (bf16[2,2,2,64,128]{4,3,2,1,0:T(8,128)(2,1)S(1)}, bf16[2,2,2,64,128]{4,3,2,1,0:T(8,128)(2,1)S(1)}, u32[]{:S(2)}, u32[]{:S(2)}) collective-permute-start(bf16[2,2,2,64,128]{4,3,2,1,0:T(8,128)(2,1)S(1)} %pair.1), channel_id=1, source_target_pairs={{0,8},{4,28},{8,0},{12,20},{16,24},{20,12},{24,16},{28,4},{1,9},{5... | collective-permute-start | bytes 393224 | tf_op jit(solution)/shard_map/ppermute | solution.py:418
  13.9 9.2 %collective-permute-start.1 = (bf16[128,1024]{1,0:T(8,128)(2,1)}, bf16[128,1024]{1,0:T(8,128)(2,1)S(1)}, u32[]{:S(2)}, u32[]{:S(2)}) collective-permute-start(bf16[128,1024]{1,0:T(8,128)(2,1)} %bitcast.10), channel_id=1, source_target_pairs={{0,3},{4,5},{1,2},{5,4},{2,1},{6,7},{3,0},{7,6},{8,11},{12,13},{9,... | collective-permute-start | bytes 786440 | tf_op jit(solution)/shard_map/ppermute | solution.py:418
  15.1 1.0 %copy-start.3 = (bf16[144,1024]{1,0:T(8,128)(2,1)S(1)}, bf16[144,1024]{1,0:T(8,128)(2,1)}, u32[]{:S(2)}) copy-start(bf16[144,1024]{1,0:T(8,128)(2,1)} %get-tuple-element.30.x_in) | copy-start | bytes 884740
  16.1 0.8 %copy-start.5 = (bf16[2,2,64,128]{3,2,1,0:T(8,128)(2,1)S(1)}, bf16[2,2,64,128]{3,2,1,0:T(8,128)(2,1)}, u32[]{:S(2)}) copy-start(bf16[2,2,64,128]{3,2,1,0:T(8,128)(2,1)} %get-tuple-element.31.own_in) | copy-start | bytes 196612
  16.9 0.7 %copy-start.6 = (f32[128]{0:T(128)S(1)}, f32[128]{0:T(128)}, u32[]{:S(2)}) copy-start(f32[128]{0:T(128)} %param.16) | copy-start | bytes 1540
  17.6 0.7 %copy-start.7 = (f32[128]{0:T(128)S(1)}, f32[128]{0:T(128)}, u32[]{:S(2)}) copy-start(f32[128]{0:T(128)} %param.17) | copy-start | bytes 1540
  18.3 4.9 %collective-permute-start.7 = (bf16[4,2,64,128]{3,2,1,0:T(8,128)(2,1)S(1)}, bf16[4,2,64,128]{3,2,1,0:T(8,128)(2,1)S(1)}, u32[]{:S(2)}, u32[]{:S(2)}) collective-permute-start(bf16[4,2,64,128]{3,2,1,0:T(8,128)(2,1)S(1)} %get-tuple-element.41.refs_0_), channel_id=1, source_target_pairs={{0,24},{4,12},{8,16},{12,4},{16,8},{20,28},{24,0},{28,20},{1,25},{... | collective-permute-start | bytes 393224 | tf_op jit(solution)/shard_map/ppermute | solution.py:418
  18.4 5.3 %collective-permute-start.8 = (bf16[4,2,64,128]{3,2,1,0:T(8,128)(2,1)S(1)}, bf16[4,2,64,128]{3,2,1,0:T(8,128)(2,1)S(1)}, u32[]{:S(2)}, u32[]{:S(2)}) collective-permute-start(bf16[4,2,64,128]{3,2,1,0:T(8,128)(2,1)S(1)} %get-tuple-element.42.refs_2_), channel_id=1, source_target_pairs={{0,64},{4,196},{64,0},{68,132},{128,192},{132,68},{192,128},{196,4... | collective-permute-start | bytes 393224 | tf_op jit(solution)/shard_map/ppermute | solution.py:418
  21.0 9.9 %collective-permute-start.2 = (bf16[144,1024]{1,0:T(8,128)(2,1)S(1)}, bf16[144,1024]{1,0:T(8,128)(2,1)S(1)}, u32[]{:S(2)}, u32[]{:S(2)}) collective-permute-start(bf16[144,1024]{1,0:T(8,128)(2,1)S(1)} %collective-permute-done.x.x1.refs_4_), channel_id=1, source_target_pairs={{0,3},{4,5},{1,2},{5,4},{2,1},{6,7},{3,0},{7,6},{8,11},{12,13},{9,... | collective-permute-start | bytes 884744 | tf_op jit(solution)/shard_map/ppermute | solution.py:418
  23.7 9.2 %collective-permute-start.9 = (bf16[8,2,64,128]{3,2,1,0:T(8,128)(2,1)S(1)}, bf16[8,2,64,128]{3,2,1,0:T(8,128)(2,1)S(1)}, u32[]{:S(2)}, u32[]{:S(2)}) collective-permute-start(bf16[8,2,64,128]{3,2,1,0:T(8,128)(2,1)S(1)} %get-tuple-element.43.refs_0_), channel_id=1, source_target_pairs={{0,64},{4,196},{64,0},{68,132},{128,192},{132,68},{192,128},{196,4... | collective-permute-start | bytes 786440 | tf_op jit(solution)/shard_map/ppermute | solution.py:418
  26.4 4.5 %copy-start = (bf16[4096,512]{1,0:T(8,128)(2,1)S(1)}, bf16[4096,512]{1,0:T(8,128)(2,1)}, u32[]{:S(2)}) copy-start(bf16[4096,512]{1,0:T(8,128)(2,1)} %wq.1) | copy-start | bytes 12582916
  26.4 7.4 %collective-permute-start.10 = (bf16[8,2,64,128]{3,2,1,0:T(8,128)(2,1)S(1)}, bf16[8,2,64,128]{3,2,1,0:T(8,128)(2,1)S(1)}, u32[]{:S(2)}, u32[]{:S(2)}) collective-permute-start(bf16[8,2,64,128]{3,2,1,0:T(8,128)(2,1)S(1)} %get-tuple-element.44.refs_2_), channel_id=1, source_target_pairs={{0,192},{4,68},{64,128},{68,4},{128,64},{132,196},{192,0},{196,132... | collective-permute-start | bytes 786440 | tf_op jit(solution)/shard_map/ppermute | solution.py:418
  26.4 3.2 %collective-permute-start.3 = (bf16[16,1024]{1,0:T(8,128)(2,1)S(1)}, bf16[16,1024]{1,0:T(8,128)(2,1)S(1)}, u32[]{:S(2)}, u32[]{:S(2)}) collective-permute-start(bf16[16,1024]{1,0:T(8,128)(2,1)S(1)} %mods.1), channel_id=1, source_target_pairs={{0,4},{4,0},{1,5},{5,1},{2,6},{6,2},{3,7},{7,3},{8,12},{12,8},{9,1... | collective-permute-start | bytes 98312 | tf_op jit(solution)/shard_map/ppermute | solution.py:454
  32.4 3.1 %collective-permute-start.4 = (bf16[2,128,128]{2,1,0:T(8,128)(2,1)S(1)}, bf16[2,128,128]{2,1,0:T(8,128)(2,1)S(1)}, u32[]{:S(2)}, u32[]{:S(2)}) collective-permute-start(bf16[2,128,128]{2,1,0:T(8,128)(2,1)S(1)} %get-tuple-element.36), channel_id=1, source_target_pairs={{0,4},{4,0},{1,5},{5,1},{2,6},{6,2},{3,7},{7,3},{8,12},{12,8},{9,1... | collective-permute-start | bytes 196616 | tf_op jit(solution)/shard_map/ppermute | solution.py:461
  33.9 11.0 %collective-permute-start.11 = (bf16[16,2,64,128]{3,2,1,0:T(8,128)(2,1)S(1)}, bf16[16,2,64,128]{3,2,1,0:T(8,128)(2,1)S(1)}, u32[]{:S(2)}, u32[]{:S(2)}) collective-permute-start(bf16[16,2,64,128]{3,2,1,0:T(8,128)(2,1)S(1)} %get-tuple-element.45.refs_3_.refs_1_), channel_id=1, source_target_pairs={{0,192},{4,68},{64,128},{68,4},{128,64},{132,196},{192,0},{196,132... | collective-permute-start | bytes 1572872 | tf_op jit(solution)/shard_map/ppermute | solution.py:418
  35.0 9.9 %collective-permute-start.12 = (bf16[16,2,64,128]{3,2,1,0:T(8,128)(2,1)S(1)}, bf16[16,2,64,128]{3,2,1,0:T(8,128)(2,1)S(1)}, u32[]{:S(2)}, u32[]{:S(2)}) collective-permute-start(bf16[16,2,64,128]{3,2,1,0:T(8,128)(2,1)S(1)} %get-tuple-element.46.refs_5_.refs_3_), channel_id=1, source_target_pairs={{0,24},{4,12},{8,16},{12,4},{16,8},{20,28},{24,0},{28,20},{1,25},{... | collective-permute-start | bytes 1572872 | tf_op jit(solution)/shard_map/ppermute | solution.py:418
  35.5 4.6 %collective-permute-start.14 = (bf16[2,128,128]{2,1,0:T(8,128)(2,1)S(1)}, bf16[2,128,128]{2,1,0:T(8,128)(2,1)S(1)}, u32[]{:S(2)}, u32[]{:S(2)}) collective-permute-start(bf16[2,128,128]{2,1,0:T(8,128)(2,1)S(1)} %get-tuple-element.37.refs_0_), channel_id=1, source_target_pairs={{0,32},{32,0},{1,33},{33,1},{2,34},{34,2},{3,35},{35,3},{4,36},{36... | collective-permute-start | bytes 196616 | tf_op jit(solution)/shard_map/ppermute | solution.py:466
  37.6 5.6 %collective-permute-start.15 = (bf16[2,128,128]{2,1,0:T(8,128)(2,1)S(1)}, bf16[2,128,128]{2,1,0:T(8,128)(2,1)S(1)}, u32[]{:S(2)}, u32[]{:S(2)}) collective-permute-start(bf16[2,128,128]{2,1,0:T(8,128)(2,1)S(1)} %get-tuple-element.47), channel_id=1, source_target_pairs={{0,40},{4,60},{8,32},{12,52},{16,56},{20,44},{24,48},{28,36},{32,8... | collective-permute-start | bytes 196616 | tf_op jit(solution)/shard_map/ppermute | solution.py:428
  39.5 5.4 %collective-permute-start.13 = (bf16[2,128,128]{2,1,0:T(8,128)(2,1)S(1)}, bf16[2,128,128]{2,1,0:T(8,128)(2,1)S(1)}, u32[]{:S(2)}, u32[]{:S(2)}) collective-permute-start(bf16[2,128,128]{2,1,0:T(8,128)(2,1)S(1)} %get-tuple-element.47), channel_id=1, source_target_pairs={{0,8},{4,28},{8,0},{12,20},{16,24},{20,12},{24,16},{28,4},{1,9},{5... | collective-permute-start | bytes 196616 | tf_op jit(solution)/shard_map/ppermute | solution.py:418
  44.9 8.1 %copy-start.2 = (bf16[4096,512]{1,0:T(8,128)(2,1)S(1)}, bf16[4096,512]{1,0:T(8,128)(2,1)}, u32[]{:S(2)}) copy-start(bf16[4096,512]{1,0:T(8,128)(2,1)} %wv.1) | copy-start | bytes 12582916
  47.5 5.5 %copy-start.1 = (bf16[4096,512]{1,0:T(8,128)(2,1)S(1)}, bf16[4096,512]{1,0:T(8,128)(2,1)}, u32[]{:S(2)}) copy-start(bf16[4096,512]{1,0:T(8,128)(2,1)} %wk.1) | copy-start | bytes 12582916
  47.5 7.9 %collective-permute-start.16 = (bf16[2,144,128]{2,1,0:T(8,128)(2,1)S(1)}, bf16[2,144,128]{2,1,0:T(8,128)(2,1)S(1)}, u32[]{:S(2)}, u32[]{:S(2)}) collective-permute-start(bf16[2,144,128]{2,1,0:T(8,128)(2,1)S(1)} %get-tuple-element.49), channel_id=1, source_target_pairs={{0,32},{32,0},{1,33},{33,1},{2,34},{34,2},{3,35},{35,3},{4,36},{36... | collective-permute-start | bytes 221192 | tf_op jit(solution)/shard_map/ppermute | solution.py:473
  48.9 6.4 %collective-permute-start.18 = (bf16[2,144,128]{2,1,0:T(8,128)(2,1)S(1)}, bf16[2,144,128]{2,1,0:T(8,128)(2,1)S(1)}, u32[]{:S(2)}, u32[]{:S(2)}) collective-permute-start(bf16[2,144,128]{2,1,0:T(8,128)(2,1)S(1)} %get-tuple-element.50), channel_id=1, source_target_pairs={{0,40},{4,60},{8,32},{12,52},{16,56},{20,44},{24,48},{28,36},{32,8... | collective-permute-start | bytes 221192 | tf_op jit(solution)/shard_map/ppermute | solution.py:428
  51.2 4.4 %collective-permute-start.17 = (bf16[2,144,128]{2,1,0:T(8,128)(2,1)S(1)}, bf16[2,144,128]{2,1,0:T(8,128)(2,1)S(1)}, u32[]{:S(2)}, u32[]{:S(2)}) collective-permute-start(bf16[2,144,128]{2,1,0:T(8,128)(2,1)S(1)} %get-tuple-element.48.refs_5_._), channel_id=1, source_target_pairs={{0,8},{4,28},{8,0},{12,20},{16,24},{20,12},{24,16},{28,4},{1,9},{5... | collective-permute-start | bytes 221192 | tf_op jit(solution)/shard_map/ppermute | solution.py:418
  55.7 4.2 %collective-permute-start.19 = (bf16[4,144,128]{2,1,0:T(8,128)(2,1)S(1)}, bf16[4,144,128]{2,1,0:T(8,128)(2,1)S(1)}, u32[]{:S(2)}, u32[]{:S(2)}) collective-permute-start(bf16[4,144,128]{2,1,0:T(8,128)(2,1)S(1)} %back.1), channel_id=1, source_target_pairs={{0,4},{4,0},{1,5},{5,1},{2,6},{6,2},{3,7},{7,3},{8,12},{12,8},{9,1... | collective-permute-start | bytes 442376 | tf_op jit(solution)/shard_map/ppermute | solution.py:477

commit v6 on v5

--- a/solution.py
+++ b/solution.py
@@ -162,6 +162,21 @@
         cost_estimate=pl.CostEstimate(flops=0, bytes_accessed=32 << 20, transcendentals=0),
         name="hold",
     )(x0, own, *gains)
+
+
+def mark(dep):
+    def kernel(_, out):
+        out[...] = jnp.zeros_like(out)
+
+    return pl.pallas_call(
+        kernel,
+        out_shape=jax.ShapeDtypeStruct((8, HEAD), F32),
+        in_specs=anywhere(1),
+        out_specs=pl.BlockSpec(memory_space=pltpu.VMEM),
+        compiler_params=params(4),
+        cost_estimate=pl.CostEstimate(flops=4 << 30, bytes_accessed=4096, transcendentals=0),
+        name="mark",
+    )(dep)
 
 
 def mods_kernel(x, out):
@@ -465,14 +480,12 @@
     )
     groups = (swap(n, "y", 0), lax.ppermute(g, "zl", FLIP), diagonal(n))
     streams = (s0, t0, s1, t1)
-    py, pz, pd = attend(groups, streams, 2)
+    fk, fv, near_out, near_lse = fresh(code, xs, qa, w_key, w_value, gains, g)
+    py, pz, pd = attend(groups, streams, 2, (near_lse,))
     (pg,) = attend((g,), streams, 0, (py,))
-    fk, fv, near_out, near_lse = fresh(
-        code, xs, qa, w_key, w_value, gains, py
-    )
     py, pz, pd = swap(py, "y", 0), lax.ppermute(pz, "zl", FLIP), diagonal(pd)
     (back,) = call(
-        back_kernel, "back", 8, [(4, ROWS + 16, HEAD)], (pg, py, pz, pd), (near_lse,)
+        back_kernel, "back", 8, [(4, ROWS + 16, HEAD)], (pg, py, pz, pd), (mark(pd),)
     )
     back = lax.ppermute(back, "core", FLIP)
     att = combine(code, (pg, pz, py, pd, back), near_out, near_lse)

time: 61.1 us -> 59.5 us (0.974)
  starting transfers between devices: 35.3 us -> 33.8 us
    ppermute x2, starting transfers between devices: 4.22 us -> 7.85 us  [diagonal(): return lax.ppermute(value, ('zl', 'y', 'core'), perm)]
    ppermute x2, waiting for transfers between devices: 3.08 us -> 0.01 us  [diagonal(): return lax.ppermute(value, ('zl', 'y', 'core'), perm)]
    ppermute x1, starting transfers between devices: 2.11 us -> 0.01 us  [on_device(): groups = (swap(n, 'y', 0), lax.ppermute(g, 'zl', FLIP), diagonal(n))]
    ppermute x1, starting transfers between devices: 3.21 us -> 1.52 us  [on_device(): back = lax.ppermute(back, 'core', FLIP)]
    ppermute x1, waiting for transfers between devices: 0.01 us -> 1.54 us  [on_device(): py, pz, pd = (swap(py, 'y', 0), lax.ppermute(pz, 'zl', FLIP), diagonal(pd))]
    ppermute x1, starting transfers between devices: 1.42 us -> 0.01 us  [on_device(): py, pz, pd = (swap(py, 'y', 0), lax.ppermute(pz, 'zl', FLIP), diagonal(pd))]
    ppermute x12, starting transfers between devices: 18.2 us -> 19.5 us  [swap(): return lax.ppermute(value, names, perm)]
    ppermute x1, starting transfers between devices: 2.33 us -> 1.18 us  [on_device(): m2 = lax.ppermute(m2, 'core', FLIP)]
  transfers between devices with their start and end apart: 20 -> 20, of which waited for: 8 -> 9; matrix products, arithmetic and copies ran while one was open for 0% -> 0% of each run, Pallas kernels for 9% -> 9%
where the time goes in v6:
time: 59.5 us; the launch traced here: 59.2 us
  starting transfers between devices  33.8 us (57%)
  Pallas kernels  11.1 us (19%)
  waiting for transfers between devices  9.56 us (16%)
  local copies, waits for them, and re-layouts  3.96 us (7%)
  between operations  0.76 us (1%)
    ppermute x12, starting transfers between devices, swap(): return lax.ppermute(value, names, perm)  19.5 us
    ppermute x2, starting transfers between devices, diagonal(): return lax.ppermute(value, ('zl', 'y', 'core'), perm)  7.85 us
    ppermute x12, waiting for transfers between devices, swap(): return lax.ppermute(value, names, perm)  5.06 us
    pallas_call x2, Pallas kernels, attend(): pl.pallas_call(functools.partial(attend_kernel, number, first_patch), out...  4.08 us
    unnamed x16, local copies, waits for them, and re-layouts  3.96 us
    ppermute x2, starting transfers between devices, on_device(): other = lax.ppermute(other, 'core', FLIP)  3.74 us
    pallas_call x1, Pallas kernels, fresh(): pl.pallas_call(fresh_kernel, out_shape=[jax.ShapeDtypeStruct((ROWS, COLS)...  2.32 us
    pallas_call x1, Pallas kernels, pack(): pl.pallas_call(pack_kernel, out_shape=[jax.ShapeDtypeStruct(shape, BF16),...  1.99 us
  transfers between devices with their start and end apart: 20, of which 9 were waited for; matrix products, arithmetic and copies ran while one was open for 0% of the time, Pallas kernels for 9%

profile of v6, /device:TPU:1, one launch (start us, length us, event | category | flops | bytes accessed | tf_op | source)
XLA Modules:
  0.0 59.2 jit_solution(9308711959100833199)
XLA Ops:
  0.6 2.0 %pack.1 = (bf16[2,2,64,128]{3,2,1,0:T(8,128)(2,1)}, bf16[2,2,64,128]{3,2,1,0:T(8,128)(2,1)}, bf16[2,2,2,64,128]{4,3,2,1,0:T(8,128)(2,1)}, bf16[144,1024]{1,0:T(8,128)(2,1)}) custom-call(s32[1]{0:T(128)} %bitcast.heads.idx, bf16[2,64,512]{2,1,0:T(8,128)(2,1)} %keys.1, bf16[2,64,512]{2,1,0:T(8,128)(2,1)} %values.1, bf16[128,1024]{1,0:T(8,128)(2,1)} %bitcast.9, ...), custom_call_target="tpu_custom_call" | custom-call | tf_op jit(solution)/shard_map/pack/pallas_call | solution.py:90
  2.6 3.3 %collective-permute-start.5 = (bf16[2,2,2,64,128]{4,3,2,1,0:T(8,128)(2,1)}, bf16[2,2,2,64,128]{4,3,2,1,0:T(8,128)(2,1)S(1)}, u32[]{:S(2)}, u32[]{:S(2)}) collective-permute-start(bf16[2,2,2,64,128]{4,3,2,1,0:T(8,128)(2,1)} %get-tuple-element.39), channel_id=1, source_target_pairs={{0,4},{4,0},{1,5},{5,1},{2,6},{6,2},{3,7},{7,3},{8,12},{12,8},{9,1... | collective-permute-start | bytes 393224 | tf_op jit(solution)/shard_map/ppermute | solution.py:456
  6.0 4.3 %collective-permute-start = (bf16[144,1024]{1,0:T(8,128)(2,1)}, bf16[144,1024]{1,0:T(8,128)(2,1)S(1)}, u32[]{:S(2)}, u32[]{:S(2)}) collective-permute-start(bf16[144,1024]{1,0:T(8,128)(2,1)} %get-tuple-element.30.x_in), channel_id=1, source_target_pairs={{0,1},{4,7},{1,0},{5,6},{2,3},{6,5},{3,2},{7,4},{8,9},{12,15},{9,8... | collective-permute-start | bytes 884744 | tf_op jit(solution)/shard_map/ppermute | solution.py:433
  10.3 0.0 collective-permute-done.5.b.other
  10.3 0.0 copy-start.4
  10.3 0.8 %copy-done.4 = bf16[2,2,64,128]{3,2,1,0:T(8,128)(2,1)S(1)} copy-done((bf16[2,2,64,128]{3,2,1,0:T(8,128)(2,1)S(1)}, bf16[2,2,64,128]{3,2,1,0:T(8,128)(2,1)}, u32[]{:S(2)}) %copy-start.4) | copy-done | bytes 65560
  11.1 2.8 %collective-permute-start.6 = (bf16[2,2,2,64,128]{4,3,2,1,0:T(8,128)(2,1)S(1)}, bf16[2,2,2,64,128]{4,3,2,1,0:T(8,128)(2,1)S(1)}, u32[]{:S(2)}, u32[]{:S(2)}) collective-permute-start(bf16[2,2,2,64,128]{4,3,2,1,0:T(8,128)(2,1)S(1)} %pair.1), channel_id=1, source_target_pairs={{0,8},{4,28},{8,0},{12,20},{16,24},{20,12},{24,16},{28,4},{1,9},{5... | collective-permute-start | bytes 393224 | tf_op jit(solution)/shard_map/ppermute | solution.py:433
  13.9 1.2 %collective-permute-start.1 = (bf16[128,1024]{1,0:T(8,128)(2,1)}, bf16[128,1024]{1,0:T(8,128)(2,1)S(1)}, u32[]{:S(2)}, u32[]{:S(2)}) collective-permute-start(bf16[128,1024]{1,0:T(8,128)(2,1)} %bitcast.10), channel_id=1, source_target_pairs={{0,3},{4,5},{1,2},{5,4},{2,1},{6,7},{3,0},{7,6},{8,11},{12,13},{9,... | collective-permute-start | bytes 786440 | tf_op jit(solution)/shard_map/ppermute | solution.py:433
  15.1 0.0 copy-start.3
  15.1 1.0 %copy-done.3 = bf16[144,1024]{1,0:T(8,128)(2,1)S(1)} copy-done((bf16[144,1024]{1,0:T(8,128)(2,1)S(1)}, bf16[144,1024]{1,0:T(8,128)(2,1)}, u32[]{:S(2)}) %copy-start.3) | copy-done | bytes 294936
  16.1 0.0 copy-start.5
  16.1 0.8 %copy-done.5 = bf16[2,2,64,128]{3,2,1,0:T(8,128)(2,1)S(1)} copy-done((bf16[2,2,64,128]{3,2,1,0:T(8,128)(2,1)S(1)}, bf16[2,2,64,128]{3,2,1,0:T(8,128)(2,1)}, u32[]{:S(2)}) %copy-start.5) | copy-done | bytes 65560
  16.9 0.0 copy-start.6
  16.9 0.7 %copy-done.6 = f32[128]{0:T(128)S(1)} copy-done((f32[128]{0:T(128)S(1)}, f32[128]{0:T(128)}, u32[]{:S(2)}) %copy-start.6) | copy-done | bytes 536
  17.6 0.0 copy-start.7
  17.6 0.7 %copy-done.7 = f32[128]{0:T(128)S(1)} copy-done((f32[128]{0:T(128)S(1)}, f32[128]{0:T(128)}, u32[]{:S(2)}) %copy-start.7) | copy-done | bytes 536
  18.2 0.0 collective-permute-done.6.far
  18.3 0.1 collective-permute-start.7
  18.4 2.6 %collective-permute-start.8 = (bf16[4,2,64,128]{3,2,1,0:T(8,128)(2,1)S(1)}, bf16[4,2,64,128]{3,2,1,0:T(8,128)(2,1)S(1)}, u32[]{:S(2)}, u32[]{:S(2)}) collective-permute-start(bf16[4,2,64,128]{3,2,1,0:T(8,128)(2,1)S(1)} %get-tuple-element.42.refs_2_), channel_id=1, source_target_pairs={{0,64},{4,196},{64,0},{68,132},{128,192},{132,68},{192,128},{196,4... | collective-permute-start | bytes 393224 | tf_op jit(solution)/shard_map/ppermute | solution.py:433
  20.9 0.0 collective-permute-done.x.x1.refs_4_
  21.0 2.2 %collective-permute-start.2 = (bf16[144,1024]{1,0:T(8,128)(2,1)S(1)}, bf16[144,1024]{1,0:T(8,128)(2,1)S(1)}, u32[]{:S(2)}, u32[]{:S(2)}) collective-permute-start(bf16[144,1024]{1,0:T(8,128)(2,1)S(1)} %collective-permute-done.x.x1.refs_4_), channel_id=1, source_target_pairs={{0,3},{4,5},{1,2},{5,4},{2,1},{6,7},{3,0},{7,6},{8,11},{12,13},{9,... | collective-permute-start | bytes 884744 | tf_op jit(solution)/shard_map/ppermute | solution.py:433
  23.2 0.0 collective-permute-done.1.x2.refs_5_
  23.2 0.0 collective-permute-done.7.refs_1_
  23.2 0.5 collective-permute-done.8.refs_3_
  23.7 1.4 %collective-permute-start.10 = (bf16[8,2,64,128]{3,2,1,0:T(8,128)(2,1)S(1)}, bf16[8,2,64,128]{3,2,1,0:T(8,128)(2,1)S(1)}, u32[]{:S(2)}, u32[]{:S(2)}) collective-permute-start(bf16[8,2,64,128]{3,2,1,0:T(8,128)(2,1)S(1)} %get-tuple-element.44.refs_2_), channel_id=1, source_target_pairs={{0,192},{4,68},{64,128},{68,4},{128,64},{132,196},{192,0},{196,132... | collective-permute-start | bytes 786440 | tf_op jit(solution)/shard_map/ppermute | solution.py:433
  25.1 0.0 copy-start.2
  25.1 1.8 %collective-permute-start.9 = (bf16[8,2,64,128]{3,2,1,0:T(8,128)(2,1)S(1)}, bf16[8,2,64,128]{3,2,1,0:T(8,128)(2,1)S(1)}, u32[]{:S(2)}, u32[]{:S(2)}) collective-permute-start(bf16[8,2,64,128]{3,2,1,0:T(8,128)(2,1)S(1)} %get-tuple-element.43.refs_0_), channel_id=1, source_target_pairs={{0,64},{4,196},{64,0},{68,132},{128,192},{132,68},{192,128},{196,4... | collective-permute-start | bytes 786440 | tf_op jit(solution)/shard_map/ppermute | solution.py:433
  27.0 1.2 %collective-permute-start.3 = (bf16[16,1024]{1,0:T(8,128)(2,1)S(1)}, bf16[16,1024]{1,0:T(8,128)(2,1)S(1)}, u32[]{:S(2)}, u32[]{:S(2)}) collective-permute-start(bf16[16,1024]{1,0:T(8,128)(2,1)S(1)} %mods.1), channel_id=1, source_target_pairs={{0,4},{4,0},{1,5},{5,1},{2,6},{6,2},{3,7},{7,3},{8,12},{12,8},{9,1... | collective-permute-start | bytes 98312 | tf_op jit(solution)/shard_map/ppermute | solution.py:469
  28.1 0.9 %collective-permute-done.3.m2 = bf16[16,1024]{1,0:T(8,128)(2,1)S(1)} collective-permute-done((bf16[16,1024]{1,0:T(8,128)(2,1)S(1)}, bf16[16,1024]{1,0:T(8,128)(2,1)S(1)}, u32[]{:S(2)}, u32[]{:S(2)}) %collective-permute-start.3) | collective-permute-done | bytes 32800 | tf_op jit(solution)/shard_map/ppermute | solution.py:469
  29.0 1.9 %collective-permute-done.2.x3 = bf16[144,1024]{1,0:T(8,128)(2,1)S(1)} collective-permute-done((bf16[144,1024]{1,0:T(8,128)(2,1)S(1)}, bf16[144,1024]{1,0:T(8,128)(2,1)S(1)}, u32[]{:S(2)}, u32[]{:S(2)}) %collective-permute-start.2) | collective-permute-done | bytes 294944 | tf_op jit(solution)/shard_map/ppermute | solution.py:433
  30.9 0.0 copy-done.2
  30.9 1.5 %queries.1 = (bf16[128,128]{1,0:T(8,128)(2,1)S(1)}, bf16[128,128]{1,0:T(8,128)(2,1)S(1)}, bf16[2,128,128]{2,1,0:T(8,128)(2,1)S(1)}, bf16[128,512]{1,0:T(8,128)(2,1)S(1)}, bf16[4,128,1024]{2,1,0:T(8,128)(2,1)S(1)}) custom-call(s32[1]{0:T(128)} %bitcast.heads.idx, bf16[144,1024]{1,0:T(8,128)(2,1)S(1)} %get-tuple-element.32.x0, ...), custom_call_target="tpu_custom_call" | custom-call | flops 536870912 | bytes 5242880 | tf_op jit(solution)/shard_map/queries/pallas_call | solution.py:250
  32.4 0.4 collective-permute-start.4
  32.9 0.0 collective-permute-done.10.refs_3_
  32.9 1.4 %collective-permute-done.9.refs_1_ = bf16[8,2,64,128]{3,2,1,0:T(8,128)(2,1)S(1)} collective-permute-done((bf16[8,2,64,128]{3,2,1,0:T(8,128)(2,1)S(1)}, bf16[8,2,64,128]{3,2,1,0:T(8,128)(2,1)S(1)}, u32[]{:S(2)}, u32[]{:S(2)}) %collective-permute-start.9) | collective-permute-done | bytes 262176 | tf_op jit(solution)/shard_map/ppermute | solution.py:433
  34.3 0.1 join.3
  34.4 0.7 %collective-permute-start.11 = (bf16[16,2,64,128]{3,2,1,0:T(8,128)(2,1)S(1)}, bf16[16,2,64,128]{3,2,1,0:T(8,128)(2,1)S(1)}, u32[]{:S(2)}, u32[]{:S(2)}) collective-permute-start(bf16[16,2,64,128]{3,2,1,0:T(8,128)(2,1)S(1)} %get-tuple-element.45.refs_3_.refs_1_), channel_id=1, source_target_pairs={{0,192},{4,68},{64,128},{68,4},{128,64},{132,196},{192,0},{196,132... | collective-permute-start | bytes 1572872 | tf_op jit(solution)/shard_map/ppermute | solution.py:433
  35.0 0.6 collective-permute-start.12
  35.6 0.0 collective-permute-done.4.other
  35.6 0.0 copy-start
  35.6 0.0 copy-start.1
  35.6 1.5 %collective-permute-start.13 = (bf16[2,128,128]{2,1,0:T(8,128)(2,1)S(1)}, bf16[2,128,128]{2,1,0:T(8,128)(2,1)S(1)}, u32[]{:S(2)}, u32[]{:S(2)}) collective-permute-start(bf16[2,128,128]{2,1,0:T(8,128)(2,1)S(1)} %get-tuple-element.47), channel_id=1, source_target_pairs={{0,8},{4,28},{8,0},{12,20},{16,24},{20,12},{24,16},{28,4},{1,9},{5... | collective-permute-start | bytes 196616 | tf_op jit(solution)/shard_map/ppermute | solution.py:433
  37.1 2.9 %collective-permute-start.15 = (bf16[2,128,128]{2,1,0:T(8,128)(2,1)S(1)}, bf16[2,128,128]{2,1,0:T(8,128)(2,1)S(1)}, u32[]{:S(2)}, u32[]{:S(2)}) collective-permute-start(bf16[2,128,128]{2,1,0:T(8,128)(2,1)S(1)} %get-tuple-element.47), channel_id=1, source_target_pairs={{0,40},{4,60},{8,32},{12,52},{16,56},{20,44},{24,48},{28,36},{32,8... | collective-permute-start | bytes 196616 | tf_op jit(solution)/shard_map/ppermute | solution.py:443
  40.0 0.0 collective-permute-start.14
  40.0 0.0 copy-done
  40.0 0.0 copy-done.1
  40.0 2.3 %fresh.1 = (bf16[128,512]{1,0:T(8,128)(2,1)}, bf16[128,512]{1,0:T(8,128)(2,1)}, f32[128,512]{1,0:T(8,128)S(1)}, f32[128,128]{1,0:T(8,128)S(1)}) custom-call(s32[1]{0:T(128)} %bitcast.heads.idx, bf16[4,128,1024]{2,1,0:T(8,128)(2,1)S(1)} %get-tuple-element.48.xs, bf16[128,512]{1,0:T(8,128)(2,1)S(1)} %get-tuple-element.49.qa, bf16[4096,512]{1,0:T(8,128)(2,1)S(1)} %copy-done, ...), custom_call_target="tpu_custom_call" | custom-call | flops 1073741824 | bytes 9437184 | tf_op jit(solution)/shard_map/fresh/pallas_call | solution.py:294
  42.3 0.0 collective-permute-done.13.refs_0_
  42.3 1.1 %collective-permute-done.14.refs_1_ = bf16[2,128,128]{2,1,0:T(8,128)(2,1)S(1)} collective-permute-done((bf16[2,128,128]{2,1,0:T(8,128)(2,1)S(1)}, bf16[2,128,128]{2,1,0:T(8,128)(2,1)S(1)}, u32[]{:S(2)}, u32[]{:S(2)}) %collective-permute-start.14) | collective-permute-done | bytes 65568 | tf_op jit(solution)/shard_map/ppermute | solution.py:481
  43.4 0.0 collective-permute-done.15.refs_2_
  43.4 0.0 collective-permute-done.11.refs_4_.refs_2_
  43.4 0.2 collective-permute-done.12.refs_6_.refs_4_
  43.6 2.5 %attend.2 = (bf16[2,144,128]{2,1,0:T(8,128)(2,1)S(1)}, bf16[2,144,128]{2,1,0:T(8,128)(2,1)S(1)}, bf16[2,144,128]{2,1,0:T(8,128)(2,1)S(1)}) custom-call(bf16[2,128,128]{2,1,0:T(8,128)(2,1)S(1)} %collective-permute-done.13.refs_0_, bf16[2,128,128]{2,1,0:T(8,128)(2,1)S(1)} %collective-permute-done.14.refs_1_, ...), custom_call_target="tpu_custom_call" | custom-call | flops 6442450944 | bytes 8388608 | tf_op jit(solution)/shard_map/attend/pallas_call | solution.py:376
  46.1 5.0 %collective-permute-start.18 = (bf16[2,144,128]{2,1,0:T(8,128)(2,1)S(1)}, bf16[2,144,128]{2,1,0:T(8,128)(2,1)S(1)}, u32[]{:S(2)}, u32[]{:S(2)}) collective-permute-start(bf16[2,144,128]{2,1,0:T(8,128)(2,1)S(1)} %get-tuple-element.53), channel_id=1, source_target_pairs={{0,40},{4,60},{8,32},{12,52},{16,56},{20,44},{24,48},{28,36},{32,8... | collective-permute-start | bytes 221192 | tf_op jit(solution)/shard_map/ppermute | solution.py:443
  51.1 0.0 collective-permute-start.16
  51.1 0.4 collective-permute-start.17
  51.5 1.6 %attend.3.g = bf16[2,144,128]{2,1,0:T(8,128)(2,1)S(1)} custom-call(bf16[2,128,128]{2,1,0:T(8,128)(2,1)S(1)} %get-tuple-element.37._.refs_0_, bf16[16,2,64,128]{3,2,1,0:T(8,128)(2,1)S(1)} %get-tuple-element.45.refs_3_.refs_1_, bf16[16,2,64,128]{3,2,1,0:T(8,128)(2,1)S(1)} %collective-permute-done.11.refs_4_.refs_2_, ...), custom_call_target="tpu_custom_call" | custom-call | flops 2147483648 | bytes 8388608 | tf_op jit(solution)/shard_map/attend/pallas_call | solution.py:376
  53.0 0.0 collective-permute-done.18._.d
  53.1 1.5 %collective-permute-done.16.z = bf16[2,144,128]{2,1,0:T(8,128)(2,1)S(1)} collective-permute-done((bf16[2,144,128]{2,1,0:T(8,128)(2,1)S(1)}, bf16[2,144,128]{2,1,0:T(8,128)(2,1)S(1)}, u32[]{:S(2)}, u32[]{:S(2)}) %collective-permute-start.16) | collective-permute-done | bytes 73760 | tf_op jit(solution)/shard_map/ppermute | solution.py:486
  54.6 1.1 %collective-permute-done.17.y = bf16[2,144,128]{2,1,0:T(8,128)(2,1)S(1)} collective-permute-done((bf16[2,144,128]{2,1,0:T(8,128)(2,1)S(1)}, bf16[2,144,128]{2,1,0:T(8,128)(2,1)S(1)}, u32[]{:S(2)}, u32[]{:S(2)}) %collective-permute-start.17) | collective-permute-done | bytes 73760 | tf_op jit(solution)/shard_map/ppermute | solution.py:433
  55.7 1.5 %collective-permute-start.19 = (bf16[4,144,128]{2,1,0:T(8,128)(2,1)S(1)}, bf16[4,144,128]{2,1,0:T(8,128)(2,1)S(1)}, u32[]{:S(2)}, u32[]{:S(2)}) collective-permute-start(bf16[4,144,128]{2,1,0:T(8,128)(2,1)S(1)} %back.1), channel_id=1, source_target_pairs={{0,4},{4,0},{1,5},{5,1},{2,6},{6,2},{3,7},{7,3},{8,12},{12,8},{9,1... | collective-permute-start | bytes 442376 | tf_op jit(solution)/shard_map/ppermute | solution.py:490
  57.2 1.0 %collective-permute-done.19.other = bf16[4,144,128]{2,1,0:T(8,128)(2,1)S(1)} collective-permute-done((bf16[4,144,128]{2,1,0:T(8,128)(2,1)S(1)}, bf16[4,144,128]{2,1,0:T(8,128)(2,1)S(1)}, u32[]{:S(2)}, u32[]{:S(2)}) %collective-permute-start.19) | collective-permute-done | bytes 147488 | tf_op jit(solution)/shard_map/ppermute | solution.py:490
  58.2 1.0 %combine.1 = bf16[128,512]{1,0:T(8,128)(2,1)} custom-call(s32[1]{0:T(128)} %bitcast.heads.idx, bf16[2,144,128]{2,1,0:T(8,128)(2,1)S(1)} %attend.3.g, bf16[2,144,128]{2,1,0:T(8,128)(2,1)S(1)} %collective-permute-done.16.z, bf16[2,144,128]{2,1,0:T(8,128)(2,1)S(1)} %collective-permute-done.17.y, bf16[2,144,128]{2,1,0:T(8,128)(2,1)S(1)} %collective-permute-done.18._.d, ...), custom_call_target="tpu_custom_call" | custom-call | tf_op jit(solution)/shard_map/combine/pallas_call | solution.py:412
  (8 shorter events, 0.1 us)
Async XLA Ops:
  2.6 7.6 %collective-permute-start.5 = (bf16[2,2,2,64,128]{4,3,2,1,0:T(8,128)(2,1)}, bf16[2,2,2,64,128]{4,3,2,1,0:T(8,128)(2,1)S(1)}, u32[]{:S(2)}, u32[]{:S(2)}) collective-permute-start(bf16[2,2,2,64,128]{4,3,2,1,0:T(8,128)(2,1)} %get-tuple-element.39), channel_id=1, source_target_pairs={{0,4},{4,0},{1,5},{5,1},{2,6},{6,2},{3,7},{7,3},{8,12},{12,8},{9,1... | collective-permute-start | bytes 393224 | tf_op jit(solution)/shard_map/ppermute | solution.py:456
  6.0 15.0 %collective-permute-start = (bf16[144,1024]{1,0:T(8,128)(2,1)}, bf16[144,1024]{1,0:T(8,128)(2,1)S(1)}, u32[]{:S(2)}, u32[]{:S(2)}) collective-permute-start(bf16[144,1024]{1,0:T(8,128)(2,1)} %get-tuple-element.30.x_in), channel_id=1, source_target_pairs={{0,1},{4,7},{1,0},{5,6},{2,3},{6,5},{3,2},{7,4},{8,9},{12,15},{9,8... | collective-permute-start | bytes 884744 | tf_op jit(solution)/shard_map/ppermute | solution.py:433
  10.3 0.8 %copy-start.4 = (bf16[2,2,64,128]{3,2,1,0:T(8,128)(2,1)S(1)}, bf16[2,2,64,128]{3,2,1,0:T(8,128)(2,1)}, u32[]{:S(2)}) copy-start(bf16[2,2,64,128]{3,2,1,0:T(8,128)(2,1)} %get-tuple-element.40.a) | copy-start | bytes 196612
  11.1 7.1 %collective-permute-start.6 = (bf16[2,2,2,64,128]{4,3,2,1,0:T(8,128)(2,1)S(1)}, bf16[2,2,2,64,128]{4,3,2,1,0:T(8,128)(2,1)S(1)}, u32[]{:S(2)}, u32[]{:S(2)}) collective-permute-start(bf16[2,2,2,64,128]{4,3,2,1,0:T(8,128)(2,1)S(1)} %pair.1), channel_id=1, source_target_pairs={{0,8},{4,28},{8,0},{12,20},{16,24},{20,12},{24,16},{28,4},{1,9},{5... | collective-permute-start | bytes 393224 | tf_op jit(solution)/shard_map/ppermute | solution.py:433
  13.9 9.2 %collective-permute-start.1 = (bf16[128,1024]{1,0:T(8,128)(2,1)}, bf16[128,1024]{1,0:T(8,128)(2,1)S(1)}, u32[]{:S(2)}, u32[]{:S(2)}) collective-permute-start(bf16[128,1024]{1,0:T(8,128)(2,1)} %bitcast.10), channel_id=1, source_target_pairs={{0,3},{4,5},{1,2},{5,4},{2,1},{6,7},{3,0},{7,6},{8,11},{12,13},{9,... | collective-permute-start | bytes 786440 | tf_op jit(solution)/shard_map/ppermute | solution.py:433
  15.1 1.0 %copy-start.3 = (bf16[144,1024]{1,0:T(8,128)(2,1)S(1)}, bf16[144,1024]{1,0:T(8,128)(2,1)}, u32[]{:S(2)}) copy-start(bf16[144,1024]{1,0:T(8,128)(2,1)} %get-tuple-element.30.x_in) | copy-start | bytes 884740
  16.1 0.8 %copy-start.5 = (bf16[2,2,64,128]{3,2,1,0:T(8,128)(2,1)S(1)}, bf16[2,2,64,128]{3,2,1,0:T(8,128)(2,1)}, u32[]{:S(2)}) copy-start(bf16[2,2,64,128]{3,2,1,0:T(8,128)(2,1)} %get-tuple-element.31.own_in) | copy-start | bytes 196612
  16.9 0.7 %copy-start.6 = (f32[128]{0:T(128)S(1)}, f32[128]{0:T(128)}, u32[]{:S(2)}) copy-start(f32[128]{0:T(128)} %param.16) | copy-start | bytes 1540
  17.6 0.7 %copy-start.7 = (f32[128]{0:T(128)S(1)}, f32[128]{0:T(128)}, u32[]{:S(2)}) copy-start(f32[128]{0:T(128)} %param.17) | copy-start | bytes 1540
  18.3 4.9 %collective-permute-start.7 = (bf16[4,2,64,128]{3,2,1,0:T(8,128)(2,1)S(1)}, bf16[4,2,64,128]{3,2,1,0:T(8,128)(2,1)S(1)}, u32[]{:S(2)}, u32[]{:S(2)}) collective-permute-start(bf16[4,2,64,128]{3,2,1,0:T(8,128)(2,1)S(1)} %get-tuple-element.41.refs_0_), channel_id=1, source_target_pairs={{0,24},{4,12},{8,16},{12,4},{16,8},{20,28},{24,0},{28,20},{1,25},{... | collective-permute-start | bytes 393224 | tf_op jit(solution)/shard_map/ppermute | solution.py:433
  18.4 5.3 %collective-permute-start.8 = (bf16[4,2,64,128]{3,2,1,0:T(8,128)(2,1)S(1)}, bf16[4,2,64,128]{3,2,1,0:T(8,128)(2,1)S(1)}, u32[]{:S(2)}, u32[]{:S(2)}) collective-permute-start(bf16[4,2,64,128]{3,2,1,0:T(8,128)(2,1)S(1)} %get-tuple-element.42.refs_2_), channel_id=1, source_target_pairs={{0,64},{4,196},{64,0},{68,132},{128,192},{132,68},{192,128},{196,4... | collective-permute-start | bytes 393224 | tf_op jit(solution)/shard_map/ppermute | solution.py:433
  21.0 10.0 %collective-permute-start.2 = (bf16[144,1024]{1,0:T(8,128)(2,1)S(1)}, bf16[144,1024]{1,0:T(8,128)(2,1)S(1)}, u32[]{:S(2)}, u32[]{:S(2)}) collective-permute-start(bf16[144,1024]{1,0:T(8,128)(2,1)S(1)} %collective-permute-done.x.x1.refs_4_), channel_id=1, source_target_pairs={{0,3},{4,5},{1,2},{5,4},{2,1},{6,7},{3,0},{7,6},{8,11},{12,13},{9,... | collective-permute-start | bytes 884744 | tf_op jit(solution)/shard_map/ppermute | solution.py:433
  23.7 9.2 %collective-permute-start.10 = (bf16[8,2,64,128]{3,2,1,0:T(8,128)(2,1)S(1)}, bf16[8,2,64,128]{3,2,1,0:T(8,128)(2,1)S(1)}, u32[]{:S(2)}, u32[]{:S(2)}) collective-permute-start(bf16[8,2,64,128]{3,2,1,0:T(8,128)(2,1)S(1)} %get-tuple-element.44.refs_2_), channel_id=1, source_target_pairs={{0,192},{4,68},{64,128},{68,4},{128,64},{132,196},{192,0},{196,132... | collective-permute-start | bytes 786440 | tf_op jit(solution)/shard_map/ppermute | solution.py:433
  25.1 5.8 %copy-start.2 = (bf16[4096,512]{1,0:T(8,128)(2,1)S(1)}, bf16[4096,512]{1,0:T(8,128)(2,1)}, u32[]{:S(2)}) copy-start(bf16[4096,512]{1,0:T(8,128)(2,1)} %wq.1) | copy-start | bytes 12582916
  25.1 9.1 %collective-permute-start.9 = (bf16[8,2,64,128]{3,2,1,0:T(8,128)(2,1)S(1)}, bf16[8,2,64,128]{3,2,1,0:T(8,128)(2,1)S(1)}, u32[]{:S(2)}, u32[]{:S(2)}) collective-permute-start(bf16[8,2,64,128]{3,2,1,0:T(8,128)(2,1)S(1)} %get-tuple-element.43.refs_0_), channel_id=1, source_target_pairs={{0,64},{4,196},{64,0},{68,132},{128,192},{132,68},{192,128},{196,4... | collective-permute-start | bytes 786440 | tf_op jit(solution)/shard_map/ppermute | solution.py:433
  27.0 2.0 %collective-permute-start.3 = (bf16[16,1024]{1,0:T(8,128)(2,1)S(1)}, bf16[16,1024]{1,0:T(8,128)(2,1)S(1)}, u32[]{:S(2)}, u32[]{:S(2)}) collective-permute-start(bf16[16,1024]{1,0:T(8,128)(2,1)S(1)} %mods.1), channel_id=1, source_target_pairs={{0,4},{4,0},{1,5},{5,1},{2,6},{6,2},{3,7},{7,3},{8,12},{12,8},{9,1... | collective-permute-start | bytes 98312 | tf_op jit(solution)/shard_map/ppermute | solution.py:469
  32.4 3.2 %collective-permute-start.4 = (bf16[2,128,128]{2,1,0:T(8,128)(2,1)S(1)}, bf16[2,128,128]{2,1,0:T(8,128)(2,1)S(1)}, u32[]{:S(2)}, u32[]{:S(2)}) collective-permute-start(bf16[2,128,128]{2,1,0:T(8,128)(2,1)S(1)} %get-tuple-element.36), channel_id=1, source_target_pairs={{0,4},{4,0},{1,5},{5,1},{2,6},{6,2},{3,7},{7,3},{8,12},{12,8},{9,1... | collective-permute-start | bytes 196616 | tf_op jit(solution)/shard_map/ppermute | solution.py:476
  34.4 9.1 %collective-permute-start.11 = (bf16[16,2,64,128]{3,2,1,0:T(8,128)(2,1)S(1)}, bf16[16,2,64,128]{3,2,1,0:T(8,128)(2,1)S(1)}, u32[]{:S(2)}, u32[]{:S(2)}) collective-permute-start(bf16[16,2,64,128]{3,2,1,0:T(8,128)(2,1)S(1)} %get-tuple-element.45.refs_3_.refs_1_), channel_id=1, source_target_pairs={{0,192},{4,68},{64,128},{68,4},{128,64},{132,196},{192,0},{196,132... | collective-permute-start | bytes 1572872 | tf_op jit(solution)/shard_map/ppermute | solution.py:433
  35.0 8.5 %collective-permute-start.12 = (bf16[16,2,64,128]{3,2,1,0:T(8,128)(2,1)S(1)}, bf16[16,2,64,128]{3,2,1,0:T(8,128)(2,1)S(1)}, u32[]{:S(2)}, u32[]{:S(2)}) collective-permute-start(bf16[16,2,64,128]{3,2,1,0:T(8,128)(2,1)S(1)} %get-tuple-element.46.refs_5_.refs_3_), channel_id=1, source_target_pairs={{0,24},{4,12},{8,16},{12,4},{16,8},{20,28},{24,0},{28,20},{1,25},{... | collective-permute-start | bytes 1572872 | tf_op jit(solution)/shard_map/ppermute | solution.py:433
  35.6 4.4 %copy-start = (bf16[4096,512]{1,0:T(8,128)(2,1)S(1)}, bf16[4096,512]{1,0:T(8,128)(2,1)}, u32[]{:S(2)}) copy-start(bf16[4096,512]{1,0:T(8,128)(2,1)} %wk.1) | copy-start | bytes 12582916
  35.6 4.4 %copy-start.1 = (bf16[4096,512]{1,0:T(8,128)(2,1)S(1)}, bf16[4096,512]{1,0:T(8,128)(2,1)}, u32[]{:S(2)}) copy-start(bf16[4096,512]{1,0:T(8,128)(2,1)} %wv.1) | copy-start | bytes 12582916
  35.6 6.7 %collective-permute-start.13 = (bf16[2,128,128]{2,1,0:T(8,128)(2,1)S(1)}, bf16[2,128,128]{2,1,0:T(8,128)(2,1)S(1)}, u32[]{:S(2)}, u32[]{:S(2)}) collective-permute-start(bf16[2,128,128]{2,1,0:T(8,128)(2,1)S(1)} %get-tuple-element.47), channel_id=1, source_target_pairs={{0,8},{4,28},{8,0},{12,20},{16,24},{20,12},{24,16},{28,4},{1,9},{5... | collective-permute-start | bytes 196616 | tf_op jit(solution)/shard_map/ppermute | solution.py:433
  37.1 6.3 %collective-permute-start.15 = (bf16[2,128,128]{2,1,0:T(8,128)(2,1)S(1)}, bf16[2,128,128]{2,1,0:T(8,128)(2,1)S(1)}, u32[]{:S(2)}, u32[]{:S(2)}) collective-permute-start(bf16[2,128,128]{2,1,0:T(8,128)(2,1)S(1)} %get-tuple-element.47), channel_id=1, source_target_pairs={{0,40},{4,60},{8,32},{12,52},{16,56},{20,44},{24,48},{28,36},{32,8... | collective-permute-start | bytes 196616 | tf_op jit(solution)/shard_map/ppermute | solution.py:443
  40.0 3.4 %collective-permute-start.14 = (bf16[2,128,128]{2,1,0:T(8,128)(2,1)S(1)}, bf16[2,128,128]{2,1,0:T(8,128)(2,1)S(1)}, u32[]{:S(2)}, u32[]{:S(2)}) collective-permute-start(bf16[2,128,128]{2,1,0:T(8,128)(2,1)S(1)} %get-tuple-element.37._.refs_0_), channel_id=1, source_target_pairs={{0,32},{32,0},{1,33},{33,1},{2,34},{34,2},{3,35},{35,3},{4,36},{36... | collective-permute-start | bytes 196616 | tf_op jit(solution)/shard_map/ppermute | solution.py:481
  46.1 6.9 %collective-permute-start.18 = (bf16[2,144,128]{2,1,0:T(8,128)(2,1)S(1)}, bf16[2,144,128]{2,1,0:T(8,128)(2,1)S(1)}, u32[]{:S(2)}, u32[]{:S(2)}) collective-permute-start(bf16[2,144,128]{2,1,0:T(8,128)(2,1)S(1)} %get-tuple-element.53), channel_id=1, source_target_pairs={{0,40},{4,60},{8,32},{12,52},{16,56},{20,44},{24,48},{28,36},{32,8... | collective-permute-start | bytes 221192 | tf_op jit(solution)/shard_map/ppermute | solution.py:443
  51.1 3.5 %collective-permute-start.16 = (bf16[2,144,128]{2,1,0:T(8,128)(2,1)S(1)}, bf16[2,144,128]{2,1,0:T(8,128)(2,1)S(1)}, u32[]{:S(2)}, u32[]{:S(2)}) collective-permute-start(bf16[2,144,128]{2,1,0:T(8,128)(2,1)S(1)} %get-tuple-element.52), channel_id=1, source_target_pairs={{0,32},{32,0},{1,33},{33,1},{2,34},{34,2},{3,35},{35,3},{4,36},{36... | collective-permute-start | bytes 221192 | tf_op jit(solution)/shard_map/ppermute | solution.py:486
  51.1 4.6 %collective-permute-start.17 = (bf16[2,144,128]{2,1,0:T(8,128)(2,1)S(1)}, bf16[2,144,128]{2,1,0:T(8,128)(2,1)S(1)}, u32[]{:S(2)}, u32[]{:S(2)}) collective-permute-start(bf16[2,144,128]{2,1,0:T(8,128)(2,1)S(1)} %get-tuple-element.51.refs_5_), channel_id=1, source_target_pairs={{0,8},{4,28},{8,0},{12,20},{16,24},{20,12},{24,16},{28,4},{1,9},{5... | collective-permute-start | bytes 221192 | tf_op jit(solution)/shard_map/ppermute | solution.py:433
  55.7 2.5 %collective-permute-start.19 = (bf16[4,144,128]{2,1,0:T(8,128)(2,1)S(1)}, bf16[4,144,128]{2,1,0:T(8,128)(2,1)S(1)}, u32[]{:S(2)}, u32[]{:S(2)}) collective-permute-start(bf16[4,144,128]{2,1,0:T(8,128)(2,1)S(1)} %back.1), channel_id=1, source_target_pairs={{0,4},{4,0},{1,5},{5,1},{2,6},{6,2},{3,7},{7,3},{8,12},{12,8},{9,1... | collective-permute-start | bytes 442376 | tf_op jit(solution)/shard_map/ppermute | solution.py:490

commit v7 on v6

--- a/solution.py
+++ b/solution.py
@@ -203,9 +203,10 @@
     n[1] = other[1]
 
 
-def back_kernel(g, y, z, d, _, out):
+def back_kernel(g, y, z, d, _, out, kept):
     for j, r in enumerate((g, z, y, d)):
         out[j] = r[1]
+        kept[j] = r[0]
 
 
 def project(code, xs, w):
@@ -386,37 +387,55 @@
     )(*groups, *streams, *deps)
 
 
-def combine_kernel(heads, g, z, y, d, other, near_out, near_lse, att):
+def merge(code, head, pair, near_out, near_lse):
     row = lax.broadcasted_iota(jnp.int32, (ROWS, HEAD), 0)
     lane = lax.broadcasted_iota(jnp.int32, (ROWS, HEAD), 1)
-    halves = ((g.at[0], z.at[0]), (y.at[0], d.at[0]), (other.at[0], other.at[1]),
-              (other.at[2], other.at[3]))
-    for h, pair in enumerate(halves):
-        cut = head_slice(heads, h)
-        levels = [
-            jnp.sum(jnp.where(lane == head_of(heads, h), near_lse[...], 0.0), axis=1, keepdims=True)
-        ]
-        parts = [near_out[:, cut]]
-        for r in pair:
-            tail = r[ROWS : ROWS + 16, :].astype(F32)
-            level = tail[0:1] + tail[1:2] + tail[2:3]
-            levels.append(jnp.sum(jnp.where(lane == row, level, 0.0), axis=1, keepdims=True))
-            parts.append(r[:ROWS, :].astype(F32))
-        top = jnp.maximum(jnp.maximum(levels[0], levels[1]), levels[2])
-        weights = [jnp.exp2(level - top) for level in levels]
-        out = sum(w * p for w, p in zip(weights, parts))
-        att[:, cut] = (out / sum(weights)).astype(BF16)
-
-
-def combine(heads, parts, near_out, near_lse):
+    level = jnp.where(lane == head_of(code, head), near_lse[...], 0.0)
+    levels = [jnp.sum(level, axis=1, keepdims=True)]
+    parts = [near_out[:, head_slice(code, head)]]
+    for r in pair:
+        tail = r[ROWS : ROWS + 16, :].astype(F32)
+        level = tail[0:1] + tail[1:2] + tail[2:3]
+        levels.append(jnp.sum(jnp.where(lane == row, level, 0.0), axis=1, keepdims=True))
+        parts.append(r[:ROWS, :].astype(F32))
+    top = jnp.maximum(jnp.maximum(levels[0], levels[1]), levels[2])
+    weights = [jnp.exp2(level - top) for level in levels]
+    out = sum(w * p for w, p in zip(weights, parts))
+    return (out / sum(weights)).astype(BF16)
+
+
+def combine_here_kernel(code, kept, near_out, near_lse, out):
+    for h in range(2):
+        out[h] = merge(code, h, (kept.at[2 * h], kept.at[2 * h + 1]), near_out, near_lse)
+
+
+def combine_here(code, kept, near_out, near_lse):
+    return pl.pallas_call(
+        combine_here_kernel,
+        out_shape=jax.ShapeDtypeStruct((2, ROWS, HEAD), BF16),
+        in_specs=[smem()] + vmem(3),
+        out_specs=pl.BlockSpec(memory_space=pltpu.VMEM),
+        compiler_params=params(8),
+        name="combine_here",
+    )(code, kept, near_out, near_lse)
+
+
+def combine_kernel(code, other, here, near_out, near_lse, att):
+    for h in range(2):
+        att[:, head_slice(code, h)] = here[h]
+        pair = (other.at[2 * h], other.at[2 * h + 1])
+        att[:, head_slice(code, 2 + h)] = merge(code, 2 + h, pair, near_out, near_lse)
+
+
+def combine(code, other, here, near_out, near_lse):
     return pl.pallas_call(
         combine_kernel,
         out_shape=jax.ShapeDtypeStruct((ROWS, COLS), BF16),
-        in_specs=[smem()] + vmem(7),
+        in_specs=[smem()] + vmem(4),
         out_specs=pl.BlockSpec(memory_space=pltpu.VMEM),
         compiler_params=params(8),
         name="combine",
-    )(heads, *parts, near_out, near_lse)
+    )(code, other, here, near_out, near_lse)
 
 
 def swap(value, axis, step):
@@ -484,11 +503,12 @@
     py, pz, pd = attend(groups, streams, 2, (near_lse,))
     (pg,) = attend((g,), streams, 0, (py,))
     py, pz, pd = swap(py, "y", 0), lax.ppermute(pz, "zl", FLIP), diagonal(pd)
-    (back,) = call(
-        back_kernel, "back", 8, [(4, ROWS + 16, HEAD)], (pg, py, pz, pd), (mark(pd),)
+    back, kept = call(
+        back_kernel, "back", 8, [(4, ROWS + 16, HEAD)] * 2, (pg, py, pz, pd), (mark(pd),)
     )
     back = lax.ppermute(back, "core", FLIP)
-    att = combine(code, (pg, pz, py, pd, back), near_out, near_lse)
+    here = combine_here(code, kept, near_out, near_lse)
+    att = combine(code, back, here, near_out, near_lse)
     shape = (IMG, TOK, COLS)
     return att.reshape(shape), fk.reshape(shape), fv.reshape(shape)
 

time: 59.5 us -> 60.2 us (1.012)
  starting transfers between devices: 33.8 us -> 34.7 us
    ppermute x1, waiting for transfers between devices: 1.54 us -> 0.01 us  [on_device(): py, pz, pd = (swap(py, 'y', 0), lax.ppermute(pz, 'zl', FLIP), diagonal(pd))]
    ppermute x12, waiting for transfers between devices: 5.06 us -> 6.6 us  [swap(): return lax.ppermute(value, names, perm)]
    ppermute x1, starting transfers between devices: 1.52 us -> 2.42 us  [on_device(): back = lax.ppermute(back, 'core', FLIP)]
  transfers between devices with their start and end apart: 20 -> 20, of which waited for: 9 -> 8; matrix products, arithmetic and copies ran while one was open for 0% -> 0% of each run, Pallas kernels for 9% -> 10%
where the time goes in v7:
time: 60.2 us; the launch traced here: 60 us
  starting transfers between devices  34.7 us (58%)
  Pallas kernels  11.2 us (19%)
  waiting for transfers between devices  9.33 us (15%)
  local copies, waits for them, and re-layouts  3.96 us (7%)
  between operations  0.77 us (1%)
    ppermute x12, starting transfers between devices, swap(): return lax.ppermute(value, names, perm)  19.2 us
    ppermute x2, starting transfers between devices, diagonal(): return lax.ppermute(value, ('zl', 'y', 'core'), perm)  7.85 us
    ppermute x12, waiting for transfers between devices, swap(): return lax.ppermute(value, names, perm)  6.6 us
    pallas_call x2, Pallas kernels, attend(): pl.pallas_call(functools.partial(attend_kernel, number, first_patch), out...  4.07 us
    unnamed x16, local copies, waits for them, and re-layouts  3.96 us
    ppermute x2, starting transfers between devices, on_device(): other = lax.ppermute(other, 'core', FLIP)  3.75 us
    ppermute x1, starting transfers between devices, on_device(): back = lax.ppermute(back, 'core', FLIP)  2.42 us
    pallas_call x1, Pallas kernels, fresh(): pl.pallas_call(fresh_kernel, out_shape=[jax.ShapeDtypeStruct((ROWS, COLS)...  2.32 us
  transfers between devices with their start and end apart: 20, of which 8 were waited for; matrix products, arithmetic and copies ran while one was open for 0% of the time, Pallas kernels for 10%

profile of v7, /device:TPU:1, one launch (start us, length us, event | category | flops | bytes accessed | tf_op | source)
XLA Modules:
  0.0 60.0 jit_solution(2548319619837661944)
XLA Ops:
  0.6 2.0 %pack.1 = (bf16[2,2,64,128]{3,2,1,0:T(8,128)(2,1)}, bf16[2,2,64,128]{3,2,1,0:T(8,128)(2,1)}, bf16[2,2,2,64,128]{4,3,2,1,0:T(8,128)(2,1)}, bf16[144,1024]{1,0:T(8,128)(2,1)}) custom-call(s32[1]{0:T(128)} %bitcast.heads.idx.code, bf16[2,64,512]{2,1,0:T(8,128)(2,1)} %keys.1, bf16[2,64,512]{2,1,0:T(8,128)(2,1)} %values.1, bf16[128,1024]{1,0:T(8,128)(2,1)} %bitcast.9, ...), custom_call_target="tpu_custom_call" | custom-call | tf_op jit(solution)/shard_map/pack/pallas_call | solution.py:90
  2.6 3.3 %collective-permute-start.5 = (bf16[2,2,2,64,128]{4,3,2,1,0:T(8,128)(2,1)}, bf16[2,2,2,64,128]{4,3,2,1,0:T(8,128)(2,1)S(1)}, u32[]{:S(2)}, u32[]{:S(2)}) collective-permute-start(bf16[2,2,2,64,128]{4,3,2,1,0:T(8,128)(2,1)} %get-tuple-element.41), channel_id=1, source_target_pairs={{0,4},{4,0},{1,5},{5,1},{2,6},{6,2},{3,7},{7,3},{8,12},{12,8},{9,1... | collective-permute-start | bytes 393224 | tf_op jit(solution)/shard_map/ppermute | solution.py:475
  5.9 4.3 %collective-permute-start = (bf16[144,1024]{1,0:T(8,128)(2,1)}, bf16[144,1024]{1,0:T(8,128)(2,1)S(1)}, u32[]{:S(2)}, u32[]{:S(2)}) collective-permute-start(bf16[144,1024]{1,0:T(8,128)(2,1)} %get-tuple-element.32.x_in), channel_id=1, source_target_pairs={{0,1},{4,7},{1,0},{5,6},{2,3},{6,5},{3,2},{7,4},{8,9},{12,15},{9,8... | collective-permute-start | bytes 884744 | tf_op jit(solution)/shard_map/ppermute | solution.py:452
  10.2 0.0 collective-permute-done.5.b.other
  10.2 0.0 copy-start.4
  10.2 0.8 %copy-done.4 = bf16[2,2,64,128]{3,2,1,0:T(8,128)(2,1)S(1)} copy-done((bf16[2,2,64,128]{3,2,1,0:T(8,128)(2,1)S(1)}, bf16[2,2,64,128]{3,2,1,0:T(8,128)(2,1)}, u32[]{:S(2)}) %copy-start.4) | copy-done | bytes 65560
  11.1 2.8 %collective-permute-start.6 = (bf16[2,2,2,64,128]{4,3,2,1,0:T(8,128)(2,1)S(1)}, bf16[2,2,2,64,128]{4,3,2,1,0:T(8,128)(2,1)S(1)}, u32[]{:S(2)}, u32[]{:S(2)}) collective-permute-start(bf16[2,2,2,64,128]{4,3,2,1,0:T(8,128)(2,1)S(1)} %pair.1), channel_id=1, source_target_pairs={{0,8},{4,28},{8,0},{12,20},{16,24},{20,12},{24,16},{28,4},{1,9},{5... | collective-permute-start | bytes 393224 | tf_op jit(solution)/shard_map/ppermute | solution.py:452
  13.9 1.2 %collective-permute-start.1 = (bf16[128,1024]{1,0:T(8,128)(2,1)}, bf16[128,1024]{1,0:T(8,128)(2,1)S(1)}, u32[]{:S(2)}, u32[]{:S(2)}) collective-permute-start(bf16[128,1024]{1,0:T(8,128)(2,1)} %bitcast.10), channel_id=1, source_target_pairs={{0,3},{4,5},{1,2},{5,4},{2,1},{6,7},{3,0},{7,6},{8,11},{12,13},{9,... | collective-permute-start | bytes 786440 | tf_op jit(solution)/shard_map/ppermute | solution.py:452
  15.1 0.0 copy-start.3
  15.1 1.0 %copy-done.3 = bf16[144,1024]{1,0:T(8,128)(2,1)S(1)} copy-done((bf16[144,1024]{1,0:T(8,128)(2,1)S(1)}, bf16[144,1024]{1,0:T(8,128)(2,1)}, u32[]{:S(2)}) %copy-start.3) | copy-done | bytes 294936
  16.0 0.0 copy-start.5
  16.0 0.8 %copy-done.5 = bf16[2,2,64,128]{3,2,1,0:T(8,128)(2,1)S(1)} copy-done((bf16[2,2,64,128]{3,2,1,0:T(8,128)(2,1)S(1)}, bf16[2,2,64,128]{3,2,1,0:T(8,128)(2,1)}, u32[]{:S(2)}) %copy-start.5) | copy-done | bytes 65560
  16.9 0.0 copy-start.6
  16.9 0.7 %copy-done.6 = f32[128]{0:T(128)S(1)} copy-done((f32[128]{0:T(128)S(1)}, f32[128]{0:T(128)}, u32[]{:S(2)}) %copy-start.6) | copy-done | bytes 536
  17.5 0.0 copy-start.7
  17.5 0.7 %copy-done.7 = f32[128]{0:T(128)S(1)} copy-done((f32[128]{0:T(128)S(1)}, f32[128]{0:T(128)}, u32[]{:S(2)}) %copy-start.7) | copy-done | bytes 536
  18.2 0.0 collective-permute-done.6.far
  18.3 0.1 collective-permute-start.7
  18.4 2.6 %collective-permute-start.8 = (bf16[4,2,64,128]{3,2,1,0:T(8,128)(2,1)S(1)}, bf16[4,2,64,128]{3,2,1,0:T(8,128)(2,1)S(1)}, u32[]{:S(2)}, u32[]{:S(2)}) collective-permute-start(bf16[4,2,64,128]{3,2,1,0:T(8,128)(2,1)S(1)} %get-tuple-element.44.refs_2_), channel_id=1, source_target_pairs={{0,64},{4,196},{64,0},{68,132},{128,192},{132,68},{192,128},{196,4... | collective-permute-start | bytes 393224 | tf_op jit(solution)/shard_map/ppermute | solution.py:452
  20.9 0.0 collective-permute-done.x.x1.refs_4_
  20.9 2.2 %collective-permute-start.2 = (bf16[144,1024]{1,0:T(8,128)(2,1)S(1)}, bf16[144,1024]{1,0:T(8,128)(2,1)S(1)}, u32[]{:S(2)}, u32[]{:S(2)}) collective-permute-start(bf16[144,1024]{1,0:T(8,128)(2,1)S(1)} %collective-permute-done.x.x1.refs_4_), channel_id=1, source_target_pairs={{0,3},{4,5},{1,2},{5,4},{2,1},{6,7},{3,0},{7,6},{8,11},{12,13},{9,... | collective-permute-start | bytes 884744 | tf_op jit(solution)/shard_map/ppermute | solution.py:452
  23.1 0.0 collective-permute-done.1.x2.refs_5_
  23.1 0.0 collective-permute-done.7.refs_1_
  23.1 0.5 collective-permute-done.8.refs_3_
  23.7 1.4 %collective-permute-start.10 = (bf16[8,2,64,128]{3,2,1,0:T(8,128)(2,1)S(1)}, bf16[8,2,64,128]{3,2,1,0:T(8,128)(2,1)S(1)}, u32[]{:S(2)}, u32[]{:S(2)}) collective-permute-start(bf16[8,2,64,128]{3,2,1,0:T(8,128)(2,1)S(1)} %get-tuple-element.46.refs_2_), channel_id=1, source_target_pairs={{0,192},{4,68},{64,128},{68,4},{128,64},{132,196},{192,0},{196,132... | collective-permute-start | bytes 786440 | tf_op jit(solution)/shard_map/ppermute | solution.py:452
  25.1 0.0 copy-start.2
  25.1 1.8 %collective-permute-start.9 = (bf16[8,2,64,128]{3,2,1,0:T(8,128)(2,1)S(1)}, bf16[8,2,64,128]{3,2,1,0:T(8,128)(2,1)S(1)}, u32[]{:S(2)}, u32[]{:S(2)}) collective-permute-start(bf16[8,2,64,128]{3,2,1,0:T(8,128)(2,1)S(1)} %get-tuple-element.45.refs_0_), channel_id=1, source_target_pairs={{0,64},{4,196},{64,0},{68,132},{128,192},{132,68},{192,128},{196,4... | collective-permute-start | bytes 786440 | tf_op jit(solution)/shard_map/ppermute | solution.py:452
  26.9 1.2 %collective-permute-start.3 = (bf16[16,1024]{1,0:T(8,128)(2,1)S(1)}, bf16[16,1024]{1,0:T(8,128)(2,1)S(1)}, u32[]{:S(2)}, u32[]{:S(2)}) collective-permute-start(bf16[16,1024]{1,0:T(8,128)(2,1)S(1)} %mods.1), channel_id=1, source_target_pairs={{0,4},{4,0},{1,5},{5,1},{2,6},{6,2},{3,7},{7,3},{8,12},{12,8},{9,1... | collective-permute-start | bytes 98312 | tf_op jit(solution)/shard_map/ppermute | solution.py:488
  28.1 0.9 %collective-permute-done.3.m2 = bf16[16,1024]{1,0:T(8,128)(2,1)S(1)} collective-permute-done((bf16[16,1024]{1,0:T(8,128)(2,1)S(1)}, bf16[16,1024]{1,0:T(8,128)(2,1)S(1)}, u32[]{:S(2)}, u32[]{:S(2)}) %collective-permute-start.3) | collective-permute-done | bytes 32800 | tf_op jit(solution)/shard_map/ppermute | solution.py:488
  29.0 1.9 %collective-permute-done.2.x3 = bf16[144,1024]{1,0:T(8,128)(2,1)S(1)} collective-permute-done((bf16[144,1024]{1,0:T(8,128)(2,1)S(1)}, bf16[144,1024]{1,0:T(8,128)(2,1)S(1)}, u32[]{:S(2)}, u32[]{:S(2)}) %collective-permute-start.2) | collective-permute-done | bytes 294944 | tf_op jit(solution)/shard_map/ppermute | solution.py:452
  30.9 0.0 copy-done.2
  30.9 1.5 %queries.1 = (bf16[128,128]{1,0:T(8,128)(2,1)S(1)}, bf16[128,128]{1,0:T(8,128)(2,1)S(1)}, bf16[2,128,128]{2,1,0:T(8,128)(2,1)S(1)}, bf16[128,512]{1,0:T(8,128)(2,1)S(1)}, bf16[4,128,1024]{2,1,0:T(8,128)(2,1)S(1)}) custom-call(s32[1]{0:T(128)} %bitcast.heads.idx.code, bf16[144,1024]{1,0:T(8,128)(2,1)S(1)} %get-tuple-element.34.x0, ...), custom_call_target="tpu_custom_call" | custom-call | flops 536870912 | bytes 5242880 | tf_op jit(solution)/shard_map/queries/pallas_call | solution.py:251
  32.4 0.4 collective-permute-start.4
  32.8 0.0 collective-permute-done.10.refs_3_
  32.8 1.4 %collective-permute-done.9.refs_1_ = bf16[8,2,64,128]{3,2,1,0:T(8,128)(2,1)S(1)} collective-permute-done((bf16[8,2,64,128]{3,2,1,0:T(8,128)(2,1)S(1)}, bf16[8,2,64,128]{3,2,1,0:T(8,128)(2,1)S(1)}, u32[]{:S(2)}, u32[]{:S(2)}) %collective-permute-start.9) | collective-permute-done | bytes 262176 | tf_op jit(solution)/shard_map/ppermute | solution.py:452
  34.3 0.1 join.3
  34.3 0.7 %collective-permute-start.11 = (bf16[16,2,64,128]{3,2,1,0:T(8,128)(2,1)S(1)}, bf16[16,2,64,128]{3,2,1,0:T(8,128)(2,1)S(1)}, u32[]{:S(2)}, u32[]{:S(2)}) collective-permute-start(bf16[16,2,64,128]{3,2,1,0:T(8,128)(2,1)S(1)} %get-tuple-element.47.refs_3_.refs_1_), channel_id=1, source_target_pairs={{0,192},{4,68},{64,128},{68,4},{128,64},{132,196},{192,0},{196,132... | collective-permute-start | bytes 1572872 | tf_op jit(solution)/shard_map/ppermute | solution.py:452
  35.0 0.6 collective-permute-start.12
  35.6 0.0 collective-permute-done.4.other
  35.6 0.0 copy-start
  35.6 0.0 copy-start.1
  35.6 1.5 %collective-permute-start.13 = (bf16[2,128,128]{2,1,0:T(8,128)(2,1)S(1)}, bf16[2,128,128]{2,1,0:T(8,128)(2,1)S(1)}, u32[]{:S(2)}, u32[]{:S(2)}) collective-permute-start(bf16[2,128,128]{2,1,0:T(8,128)(2,1)S(1)} %get-tuple-element.49), channel_id=1, source_target_pairs={{0,8},{4,28},{8,0},{12,20},{16,24},{20,12},{24,16},{28,4},{1,9},{5... | collective-permute-start | bytes 196616 | tf_op jit(solution)/shard_map/ppermute | solution.py:452
  37.1 2.9 %collective-permute-start.15 = (bf16[2,128,128]{2,1,0:T(8,128)(2,1)S(1)}, bf16[2,128,128]{2,1,0:T(8,128)(2,1)S(1)}, u32[]{:S(2)}, u32[]{:S(2)}) collective-permute-start(bf16[2,128,128]{2,1,0:T(8,128)(2,1)S(1)} %get-tuple-element.49), channel_id=1, source_target_pairs={{0,40},{4,60},{8,32},{12,52},{16,56},{20,44},{24,48},{28,36},{32,8... | collective-permute-start | bytes 196616 | tf_op jit(solution)/shard_map/ppermute | solution.py:462
  40.0 0.0 collective-permute-start.14
  40.0 0.0 copy-done
  40.0 0.0 copy-done.1
  40.0 2.3 %fresh.1 = (bf16[128,512]{1,0:T(8,128)(2,1)}, bf16[128,512]{1,0:T(8,128)(2,1)}, f32[128,512]{1,0:T(8,128)S(1)}, f32[128,128]{1,0:T(8,128)S(1)}) custom-call(s32[1]{0:T(128)} %bitcast.heads.idx.code, bf16[4,128,1024]{2,1,0:T(8,128)(2,1)S(1)} %get-tuple-element.50.xs, bf16[128,512]{1,0:T(8,128)(2,1)S(1)} %get-tuple-element.51.qa, ...), custom_call_target="tpu_custom_call" | custom-call | flops 1073741824 | bytes 9437184 | tf_op jit(solution)/shard_map/fresh/pallas_call | solution.py:295
  42.3 0.0 collective-permute-done.13.refs_0_
  42.3 1.1 %collective-permute-done.14.refs_1_ = bf16[2,128,128]{2,1,0:T(8,128)(2,1)S(1)} collective-permute-done((bf16[2,128,128]{2,1,0:T(8,128)(2,1)S(1)}, bf16[2,128,128]{2,1,0:T(8,128)(2,1)S(1)}, u32[]{:S(2)}, u32[]{:S(2)}) %collective-permute-start.14) | collective-permute-done | bytes 65568 | tf_op jit(solution)/shard_map/ppermute | solution.py:500
  43.4 0.0 collective-permute-done.15.refs_2_
  43.4 0.0 collective-permute-done.11.refs_4_.refs_2_
  43.4 0.2 collective-permute-done.12.refs_6_.refs_4_
  43.6 2.5 %attend.2 = (bf16[2,144,128]{2,1,0:T(8,128)(2,1)S(1)}, bf16[2,144,128]{2,1,0:T(8,128)(2,1)S(1)}, bf16[2,144,128]{2,1,0:T(8,128)(2,1)S(1)}) custom-call(bf16[2,128,128]{2,1,0:T(8,128)(2,1)S(1)} %collective-permute-done.13.refs_0_, bf16[2,128,128]{2,1,0:T(8,128)(2,1)S(1)} %collective-permute-done.14.refs_1_, ...), custom_call_target="tpu_custom_call" | custom-call | flops 6442450944 | bytes 8388608 | tf_op jit(solution)/shard_map/attend/pallas_call | solution.py:377
  46.1 5.0 %collective-permute-start.18 = (bf16[2,144,128]{2,1,0:T(8,128)(2,1)S(1)}, bf16[2,144,128]{2,1,0:T(8,128)(2,1)S(1)}, u32[]{:S(2)}, u32[]{:S(2)}) collective-permute-start(bf16[2,144,128]{2,1,0:T(8,128)(2,1)S(1)} %get-tuple-element.55), channel_id=1, source_target_pairs={{0,40},{4,60},{8,32},{12,52},{16,56},{20,44},{24,48},{28,36},{32,8... | collective-permute-start | bytes 221192 | tf_op jit(solution)/shard_map/ppermute | solution.py:462
  51.1 0.0 collective-permute-start.16
  51.1 0.4 collective-permute-start.17
  51.5 1.6 %attend.3.g = bf16[2,144,128]{2,1,0:T(8,128)(2,1)S(1)} custom-call(bf16[2,128,128]{2,1,0:T(8,128)(2,1)S(1)} %get-tuple-element.39._.refs_0_, bf16[16,2,64,128]{3,2,1,0:T(8,128)(2,1)S(1)} %get-tuple-element.47.refs_3_.refs_1_, bf16[16,2,64,128]{3,2,1,0:T(8,128)(2,1)S(1)} %collective-permute-done.11.refs_4_.refs_2_, ...), custom_call_target="tpu_custom_call" | custom-call | flops 2147483648 | bytes 8388608 | tf_op jit(solution)/shard_map/attend/pallas_call | solution.py:377
  53.0 0.0 collective-permute-done.18._.d
  53.0 2.6 %collective-permute-done.16.y = bf16[2,144,128]{2,1,0:T(8,128)(2,1)S(1)} collective-permute-done((bf16[2,144,128]{2,1,0:T(8,128)(2,1)S(1)}, bf16[2,144,128]{2,1,0:T(8,128)(2,1)S(1)}, u32[]{:S(2)}, u32[]{:S(2)}) %collective-permute-start.16) | collective-permute-done | bytes 73760 | tf_op jit(solution)/shard_map/ppermute | solution.py:452
  55.6 0.0 collective-permute-done.17.z
  55.7 2.4 %collective-permute-start.19 = (bf16[4,144,128]{2,1,0:T(8,128)(2,1)S(1)}, bf16[4,144,128]{2,1,0:T(8,128)(2,1)S(1)}, u32[]{:S(2)}, u32[]{:S(2)}) collective-permute-start(bf16[4,144,128]{2,1,0:T(8,128)(2,1)S(1)} %get-tuple-element.56), channel_id=1, source_target_pairs={{0,4},{4,0},{1,5},{5,1},{2,6},{6,2},{3,7},{7,3},{8,12},{12,8},{9,1... | collective-permute-start | bytes 442376 | tf_op jit(solution)/shard_map/ppermute | solution.py:509
  58.1 0.2 combine_here.1.here
  58.3 0.8 %collective-permute-done.19.other = bf16[4,144,128]{2,1,0:T(8,128)(2,1)S(1)} collective-permute-done((bf16[4,144,128]{2,1,0:T(8,128)(2,1)S(1)}, bf16[4,144,128]{2,1,0:T(8,128)(2,1)S(1)}, u32[]{:S(2)}, u32[]{:S(2)}) %collective-permute-start.19) | collective-permute-done | bytes 147488 | tf_op jit(solution)/shard_map/ppermute | solution.py:509
  59.1 0.9 %combine.1 = bf16[128,512]{1,0:T(8,128)(2,1)} custom-call(s32[1]{0:T(128)} %bitcast.heads.idx.code, bf16[4,144,128]{2,1,0:T(8,128)(2,1)S(1)} %collective-permute-done.19.other, bf16[2,128,128]{2,1,0:T(8,128)(2,1)S(1)} %combine_here.1.here, f32[128,512]{1,0:T(8,128)S(1)} %get-tuple-element.58.near_out, f32[128,128]{1,0:T(8,128)S(1)} %get-tuple-element.52.refs_7_.near_lse), custom_call_target="tpu_custom_call" | custom-call | tf_op jit(solution)/shard_map/combine/pallas_call | solution.py:431
  (8 shorter events, 0.1 us)
Async XLA Ops:
  2.6 7.6 %collective-permute-start.5 = (bf16[2,2,2,64,128]{4,3,2,1,0:T(8,128)(2,1)}, bf16[2,2,2,64,128]{4,3,2,1,0:T(8,128)(2,1)S(1)}, u32[]{:S(2)}, u32[]{:S(2)}) collective-permute-start(bf16[2,2,2,64,128]{4,3,2,1,0:T(8,128)(2,1)} %get-tuple-element.41), channel_id=1, source_target_pairs={{0,4},{4,0},{1,5},{5,1},{2,6},{6,2},{3,7},{7,3},{8,12},{12,8},{9,1... | collective-permute-start | bytes 393224 | tf_op jit(solution)/shard_map/ppermute | solution.py:475
  5.9 15.0 %collective-permute-start = (bf16[144,1024]{1,0:T(8,128)(2,1)}, bf16[144,1024]{1,0:T(8,128)(2,1)S(1)}, u32[]{:S(2)}, u32[]{:S(2)}) collective-permute-start(bf16[144,1024]{1,0:T(8,128)(2,1)} %get-tuple-element.32.x_in), channel_id=1, source_target_pairs={{0,1},{4,7},{1,0},{5,6},{2,3},{6,5},{3,2},{7,4},{8,9},{12,15},{9,8... | collective-permute-start | bytes 884744 | tf_op jit(solution)/shard_map/ppermute | solution.py:452
  10.2 0.8 %copy-start.4 = (bf16[2,2,64,128]{3,2,1,0:T(8,128)(2,1)S(1)}, bf16[2,2,64,128]{3,2,1,0:T(8,128)(2,1)}, u32[]{:S(2)}) copy-start(bf16[2,2,64,128]{3,2,1,0:T(8,128)(2,1)} %get-tuple-element.42.a) | copy-start | bytes 196612
  11.1 7.1 %collective-permute-start.6 = (bf16[2,2,2,64,128]{4,3,2,1,0:T(8,128)(2,1)S(1)}, bf16[2,2,2,64,128]{4,3,2,1,0:T(8,128)(2,1)S(1)}, u32[]{:S(2)}, u32[]{:S(2)}) collective-permute-start(bf16[2,2,2,64,128]{4,3,2,1,0:T(8,128)(2,1)S(1)} %pair.1), channel_id=1, source_target_pairs={{0,8},{4,28},{8,0},{12,20},{16,24},{20,12},{24,16},{28,4},{1,9},{5... | collective-permute-start | bytes 393224 | tf_op jit(solution)/shard_map/ppermute | solution.py:452
  13.9 9.2 %collective-permute-start.1 = (bf16[128,1024]{1,0:T(8,128)(2,1)}, bf16[128,1024]{1,0:T(8,128)(2,1)S(1)}, u32[]{:S(2)}, u32[]{:S(2)}) collective-permute-start(bf16[128,1024]{1,0:T(8,128)(2,1)} %bitcast.10), channel_id=1, source_target_pairs={{0,3},{4,5},{1,2},{5,4},{2,1},{6,7},{3,0},{7,6},{8,11},{12,13},{9,... | collective-permute-start | bytes 786440 | tf_op jit(solution)/shard_map/ppermute | solution.py:452
  15.1 1.0 %copy-start.3 = (bf16[144,1024]{1,0:T(8,128)(2,1)S(1)}, bf16[144,1024]{1,0:T(8,128)(2,1)}, u32[]{:S(2)}) copy-start(bf16[144,1024]{1,0:T(8,128)(2,1)} %get-tuple-element.32.x_in) | copy-start | bytes 884740
  16.0 0.8 %copy-start.5 = (bf16[2,2,64,128]{3,2,1,0:T(8,128)(2,1)S(1)}, bf16[2,2,64,128]{3,2,1,0:T(8,128)(2,1)}, u32[]{:S(2)}) copy-start(bf16[2,2,64,128]{3,2,1,0:T(8,128)(2,1)} %get-tuple-element.33.own_in) | copy-start | bytes 196612
  16.9 0.7 %copy-start.6 = (f32[128]{0:T(128)S(1)}, f32[128]{0:T(128)}, u32[]{:S(2)}) copy-start(f32[128]{0:T(128)} %param.16) | copy-start | bytes 1540
  17.5 0.7 %copy-start.7 = (f32[128]{0:T(128)S(1)}, f32[128]{0:T(128)}, u32[]{:S(2)}) copy-start(f32[128]{0:T(128)} %param.17) | copy-start | bytes 1540
  18.3 4.9 %collective-permute-start.7 = (bf16[4,2,64,128]{3,2,1,0:T(8,128)(2,1)S(1)}, bf16[4,2,64,128]{3,2,1,0:T(8,128)(2,1)S(1)}, u32[]{:S(2)}, u32[]{:S(2)}) collective-permute-start(bf16[4,2,64,128]{3,2,1,0:T(8,128)(2,1)S(1)} %get-tuple-element.43.refs_0_), channel_id=1, source_target_pairs={{0,24},{4,12},{8,16},{12,4},{16,8},{20,28},{24,0},{28,20},{1,25},{... | collective-permute-start | bytes 393224 | tf_op jit(solution)/shard_map/ppermute | solution.py:452
  18.4 5.3 %collective-permute-start.8 = (bf16[4,2,64,128]{3,2,1,0:T(8,128)(2,1)S(1)}, bf16[4,2,64,128]{3,2,1,0:T(8,128)(2,1)S(1)}, u32[]{:S(2)}, u32[]{:S(2)}) collective-permute-start(bf16[4,2,64,128]{3,2,1,0:T(8,128)(2,1)S(1)} %get-tuple-element.44.refs_2_), channel_id=1, source_target_pairs={{0,64},{4,196},{64,0},{68,132},{128,192},{132,68},{192,128},{196,4... | collective-permute-start | bytes 393224 | tf_op jit(solution)/shard_map/ppermute | solution.py:452
  20.9 10.0 %collective-permute-start.2 = (bf16[144,1024]{1,0:T(8,128)(2,1)S(1)}, bf16[144,1024]{1,0:T(8,128)(2,1)S(1)}, u32[]{:S(2)}, u32[]{:S(2)}) collective-permute-start(bf16[144,1024]{1,0:T(8,128)(2,1)S(1)} %collective-permute-done.x.x1.refs_4_), channel_id=1, source_target_pairs={{0,3},{4,5},{1,2},{5,4},{2,1},{6,7},{3,0},{7,6},{8,11},{12,13},{9,... | collective-permute-start | bytes 884744 | tf_op jit(solution)/shard_map/ppermute | solution.py:452
  23.7 9.2 %collective-permute-start.10 = (bf16[8,2,64,128]{3,2,1,0:T(8,128)(2,1)S(1)}, bf16[8,2,64,128]{3,2,1,0:T(8,128)(2,1)S(1)}, u32[]{:S(2)}, u32[]{:S(2)}) collective-permute-start(bf16[8,2,64,128]{3,2,1,0:T(8,128)(2,1)S(1)} %get-tuple-element.46.refs_2_), channel_id=1, source_target_pairs={{0,192},{4,68},{64,128},{68,4},{128,64},{132,196},{192,0},{196,132... | collective-permute-start | bytes 786440 | tf_op jit(solution)/shard_map/ppermute | solution.py:452
  25.1 5.8 %copy-start.2 = (bf16[4096,512]{1,0:T(8,128)(2,1)S(1)}, bf16[4096,512]{1,0:T(8,128)(2,1)}, u32[]{:S(2)}) copy-start(bf16[4096,512]{1,0:T(8,128)(2,1)} %wq.1) | copy-start | bytes 12582916
  25.1 9.1 %collective-permute-start.9 = (bf16[8,2,64,128]{3,2,1,0:T(8,128)(2,1)S(1)}, bf16[8,2,64,128]{3,2,1,0:T(8,128)(2,1)S(1)}, u32[]{:S(2)}, u32[]{:S(2)}) collective-permute-start(bf16[8,2,64,128]{3,2,1,0:T(8,128)(2,1)S(1)} %get-tuple-element.45.refs_0_), channel_id=1, source_target_pairs={{0,64},{4,196},{64,0},{68,132},{128,192},{132,68},{192,128},{196,4... | collective-permute-start | bytes 786440 | tf_op jit(solution)/shard_map/ppermute | solution.py:452
  26.9 2.0 %collective-permute-start.3 = (bf16[16,1024]{1,0:T(8,128)(2,1)S(1)}, bf16[16,1024]{1,0:T(8,128)(2,1)S(1)}, u32[]{:S(2)}, u32[]{:S(2)}) collective-permute-start(bf16[16,1024]{1,0:T(8,128)(2,1)S(1)} %mods.1), channel_id=1, source_target_pairs={{0,4},{4,0},{1,5},{5,1},{2,6},{6,2},{3,7},{7,3},{8,12},{12,8},{9,1... | collective-permute-start | bytes 98312 | tf_op jit(solution)/shard_map/ppermute | solution.py:488
  32.4 3.2 %collective-permute-start.4 = (bf16[2,128,128]{2,1,0:T(8,128)(2,1)S(1)}, bf16[2,128,128]{2,1,0:T(8,128)(2,1)S(1)}, u32[]{:S(2)}, u32[]{:S(2)}) collective-permute-start(bf16[2,128,128]{2,1,0:T(8,128)(2,1)S(1)} %get-tuple-element.38), channel_id=1, source_target_pairs={{0,4},{4,0},{1,5},{5,1},{2,6},{6,2},{3,7},{7,3},{8,12},{12,8},{9,1... | collective-permute-start | bytes 196616 | tf_op jit(solution)/shard_map/ppermute | solution.py:495
  34.3 9.1 %collective-permute-start.11 = (bf16[16,2,64,128]{3,2,1,0:T(8,128)(2,1)S(1)}, bf16[16,2,64,128]{3,2,1,0:T(8,128)(2,1)S(1)}, u32[]{:S(2)}, u32[]{:S(2)}) collective-permute-start(bf16[16,2,64,128]{3,2,1,0:T(8,128)(2,1)S(1)} %get-tuple-element.47.refs_3_.refs_1_), channel_id=1, source_target_pairs={{0,192},{4,68},{64,128},{68,4},{128,64},{132,196},{192,0},{196,132... | collective-permute-start | bytes 1572872 | tf_op jit(solution)/shard_map/ppermute | solution.py:452
  35.0 8.5 %collective-permute-start.12 = (bf16[16,2,64,128]{3,2,1,0:T(8,128)(2,1)S(1)}, bf16[16,2,64,128]{3,2,1,0:T(8,128)(2,1)S(1)}, u32[]{:S(2)}, u32[]{:S(2)}) collective-permute-start(bf16[16,2,64,128]{3,2,1,0:T(8,128)(2,1)S(1)} %get-tuple-element.48.refs_5_.refs_3_), channel_id=1, source_target_pairs={{0,24},{4,12},{8,16},{12,4},{16,8},{20,28},{24,0},{28,20},{1,25},{... | collective-permute-start | bytes 1572872 | tf_op jit(solution)/shard_map/ppermute | solution.py:452
  35.6 4.4 %copy-start = (bf16[4096,512]{1,0:T(8,128)(2,1)S(1)}, bf16[4096,512]{1,0:T(8,128)(2,1)}, u32[]{:S(2)}) copy-start(bf16[4096,512]{1,0:T(8,128)(2,1)} %wk.1) | copy-start | bytes 12582916
  35.6 4.4 %copy-start.1 = (bf16[4096,512]{1,0:T(8,128)(2,1)S(1)}, bf16[4096,512]{1,0:T(8,128)(2,1)}, u32[]{:S(2)}) copy-start(bf16[4096,512]{1,0:T(8,128)(2,1)} %wv.1) | copy-start | bytes 12582916
  35.6 6.7 %collective-permute-start.13 = (bf16[2,128,128]{2,1,0:T(8,128)(2,1)S(1)}, bf16[2,128,128]{2,1,0:T(8,128)(2,1)S(1)}, u32[]{:S(2)}, u32[]{:S(2)}) collective-permute-start(bf16[2,128,128]{2,1,0:T(8,128)(2,1)S(1)} %get-tuple-element.49), channel_id=1, source_target_pairs={{0,8},{4,28},{8,0},{12,20},{16,24},{20,12},{24,16},{28,4},{1,9},{5... | collective-permute-start | bytes 196616 | tf_op jit(solution)/shard_map/ppermute | solution.py:452
  37.1 6.3 %collective-permute-start.15 = (bf16[2,128,128]{2,1,0:T(8,128)(2,1)S(1)}, bf16[2,128,128]{2,1,0:T(8,128)(2,1)S(1)}, u32[]{:S(2)}, u32[]{:S(2)}) collective-permute-start(bf16[2,128,128]{2,1,0:T(8,128)(2,1)S(1)} %get-tuple-element.49), channel_id=1, source_target_pairs={{0,40},{4,60},{8,32},{12,52},{16,56},{20,44},{24,48},{28,36},{32,8... | collective-permute-start | bytes 196616 | tf_op jit(solution)/shard_map/ppermute | solution.py:462
  40.0 3.4 %collective-permute-start.14 = (bf16[2,128,128]{2,1,0:T(8,128)(2,1)S(1)}, bf16[2,128,128]{2,1,0:T(8,128)(2,1)S(1)}, u32[]{:S(2)}, u32[]{:S(2)}) collective-permute-start(bf16[2,128,128]{2,1,0:T(8,128)(2,1)S(1)} %get-tuple-element.39._.refs_0_), channel_id=1, source_target_pairs={{0,32},{32,0},{1,33},{33,1},{2,34},{34,2},{3,35},{35,3},{4,36},{36... | collective-permute-start | bytes 196616 | tf_op jit(solution)/shard_map/ppermute | solution.py:500
  46.1 6.9 %collective-permute-start.18 = (bf16[2,144,128]{2,1,0:T(8,128)(2,1)S(1)}, bf16[2,144,128]{2,1,0:T(8,128)(2,1)S(1)}, u32[]{:S(2)}, u32[]{:S(2)}) collective-permute-start(bf16[2,144,128]{2,1,0:T(8,128)(2,1)S(1)} %get-tuple-element.55), channel_id=1, source_target_pairs={{0,40},{4,60},{8,32},{12,52},{16,56},{20,44},{24,48},{28,36},{32,8... | collective-permute-start | bytes 221192 | tf_op jit(solution)/shard_map/ppermute | solution.py:462
  51.1 4.6 %collective-permute-start.16 = (bf16[2,144,128]{2,1,0:T(8,128)(2,1)S(1)}, bf16[2,144,128]{2,1,0:T(8,128)(2,1)S(1)}, u32[]{:S(2)}, u32[]{:S(2)}) collective-permute-start(bf16[2,144,128]{2,1,0:T(8,128)(2,1)S(1)} %get-tuple-element.53.refs_5_), channel_id=1, source_target_pairs={{0,8},{4,28},{8,0},{12,20},{16,24},{20,12},{24,16},{28,4},{1,9},{5... | collective-permute-start | bytes 221192 | tf_op jit(solution)/shard_map/ppermute | solution.py:452
  51.1 4.6 %collective-permute-start.17 = (bf16[2,144,128]{2,1,0:T(8,128)(2,1)S(1)}, bf16[2,144,128]{2,1,0:T(8,128)(2,1)S(1)}, u32[]{:S(2)}, u32[]{:S(2)}) collective-permute-start(bf16[2,144,128]{2,1,0:T(8,128)(2,1)S(1)} %get-tuple-element.54), channel_id=1, source_target_pairs={{0,32},{32,0},{1,33},{33,1},{2,34},{34,2},{3,35},{35,3},{4,36},{36... | collective-permute-start | bytes 221192 | tf_op jit(solution)/shard_map/ppermute | solution.py:505
  55.7 3.4 %collective-permute-start.19 = (bf16[4,144,128]{2,1,0:T(8,128)(2,1)S(1)}, bf16[4,144,128]{2,1,0:T(8,128)(2,1)S(1)}, u32[]{:S(2)}, u32[]{:S(2)}) collective-permute-start(bf16[4,144,128]{2,1,0:T(8,128)(2,1)S(1)} %get-tuple-element.56), channel_id=1, source_target_pairs={{0,4},{4,0},{1,5},{5,1},{2,6},{6,2},{3,7},{7,3},{8,12},{12,8},{9,1... | collective-permute-start | bytes 442376 | tf_op jit(solution)/shard_map/ppermute | solution.py:509
